TPU v7x, 32 devices: a whole 2x2x4 slice. The times are simulated.
32 devices in a mesh: trade: 8 (over z, y), factor: 4 (over x, core).
Axes of the slice: x: 2, y: 2, z: 4, core: 2. Of those that a mesh axis runs over, the one named last changes fastest.
Arguments:
- sensitivity: bfloat16 [32768, 6400], P('trade', 'factor'), may hold values from -6 to 6
- block_count: int32 [64], P('trade'), may hold values from 0 to 512, as said below
- trade_node: int32 [32768], P('trade'), may hold values from 0 to 4095
- factor_bucket: int32 [6400], replicated, may hold values from 0 to 17, as said below
- risk_weight: float32 [18], replicated, may hold values from 0.005 to 0.12
- bucket_loading: float32 [18], replicated, may hold values from 0.5 to 1
Outputs:
- capital_scaled: float32 [3], replicated
- trade_alloc: float32 [3, 32768], P(None, ('trade', 'factor'))
- node_alloc: float32 [3, 18, 4096], P(None, None, ('trade', 'factor'))
Inputs may be any that keep to these rules, and one draw needn't show every extreme that they name: `block_count`: every index of trade either has all its 8 blocks full (512) or every block of it holds at most 128 trades; at least one index is full. `factor_bucket`: the 5 factors of a name share a bucket; each bucket holds 71 names or one more.
All inputs are finite; a program needn't handle non-finite values.
Results may differ from a plain program's by a relative error of at most 0.007.
Values sent between devices are 32-bit elements; how exact they have to be, the bound alone decides.
No kernel may reach another device: no remote copies, remote signals or barrier semaphores. Data moves between devices by JAX's collectives and lax.ppermute only.
A program may use at most 64 MiB of HBM per device.

v0:
```python
import jax
import jax.numpy as jnp
from jax import lax
from jax.sharding import PartitionSpec as P

TENORS = 5
BUCKETS = 18
SCEN = 3
NODES = 4096
BLOCK = 512


cross_base = 0.5


def level_table():
    base = jnp.array([1.0, 0.65, 0.35, 0.2275], dtype=jnp.float32)
    return jnp.stack(
        [base, jnp.minimum(1.25 * base, 1.0), jnp.maximum(2.0 * base - 1.0, 0.75 * base)]
    )


def correlated(weighted, name_bucket, first_name, count):
    grid = weighted.reshape(-1, TENORS)
    names_onehot = (jnp.arange(BUCKETS, dtype=jnp.int32)[:, None] == name_bucket[None, :]).astype(
        jnp.float32
    )
    tenor_sums = jnp.dot(names_onehot, grid, precision=lax.Precision.HIGHEST)
    name_sums = jnp.sum(grid, 1)
    bucket_total = jnp.sum(tenor_sums, 1)
    own_grid = lax.dynamic_slice_in_dim(grid, first_name, count, 0)
    own_onehot = lax.dynamic_slice_in_dim(names_onehot, first_name, count, 1)
    own_tenor = jnp.dot(own_onehot.T, tenor_sums, precision=lax.Precision.HIGHEST)
    own_total = jnp.dot(own_onehot.T, bucket_total, precision=lax.Precision.HIGHEST)
    own_name = lax.dynamic_slice_in_dim(name_sums, first_name, count, 0)
    levels = level_table()
    same_both = (levels[:, 0] - levels[:, 1] - levels[:, 2] + levels[:, 3])[:, None, None]
    product = levels[:, 3, None, None] * own_total[None, :, None]
    product = product + (levels[:, 2] - levels[:, 3])[:, None, None] * own_tenor[None, :, :]
    product = product + (levels[:, 1] - levels[:, 3])[:, None, None] * own_name[None, :, None]
    product = product + same_both * own_grid[None, :, :]
    return product.reshape(SCEN, count * TENORS)


def capital_terms(bucket_forms, bucket_sums, loading):
    scenario = jnp.array([1.0, 1.25, 0.75], dtype=jnp.float32)[:, None]
    root_forms = jnp.sqrt(bucket_forms + 1e-06)
    radius = jnp.sqrt(root_forms * root_forms + bucket_sums[None, :] * bucket_sums[None, :])
    capped = bucket_sums[None, :] * root_forms / radius
    loaded = jnp.sum(loading[None, :] * capped, 1, keepdims=True)
    squares = jnp.sum((loading[None, :] * capped) ** 2, 1, keepdims=True)
    cross_term = cross_base * scenario * (loaded * loaded - squares)
    total_form = jnp.sum(root_forms * root_forms, 1, keepdims=True) + cross_term
    capital = jnp.sqrt(total_form)
    cross_pull = (
        cross_base
        * scenario
        * (loading[None, :] * loaded - loading[None, :] ** 2 * capped)
        / capital
    )
    grad_root = root_forms / capital + cross_pull * (bucket_sums[None, :] / radius) ** 3
    coef_form = grad_root / root_forms
    coef_sum = cross_pull * (root_forms / radius) ** 3
    return (capital[:, 0], coef_form, coef_sum)


def masked_total(weights, piece_sens):
    return jnp.dot(weights[None, :], piece_sens, preferred_element_type=jnp.float32)[0]


def node_partial(alloc, nodes):
    length = alloc.shape[1]
    piece_rows = BLOCK
    node_index = jnp.arange(NODES, dtype=jnp.int32)
    upper = alloc.astype(jnp.bfloat16)
    lower = (alloc - upper.astype(jnp.float32)).astype(jnp.bfloat16)
    summed = jnp.zeros((alloc.shape[0], NODES), jnp.float32)
    for offset in range(0, length, piece_rows):
        onehot = (nodes[offset : offset + piece_rows, None] == node_index[None, :]).astype(
            jnp.bfloat16
        )
        summed = summed + jnp.dot(
            upper[:, offset : offset + piece_rows], onehot, preferred_element_type=jnp.float32
        )
        summed = summed + jnp.dot(
            lower[:, offset : offset + piece_rows], onehot, preferred_element_type=jnp.float32
        )
    return summed


def local(sensitivity, block_count, trade_node, factor_bucket, risk_weight, bucket_loading):
    trade_rows, own_width = sensitivity.shape
    trades_total = trade_rows * lax.axis_size("trade")
    own_start = lax.axis_index("factor") * own_width
    slot_index = jnp.arange(BLOCK, dtype=jnp.int32)
    live_mask = (slot_index[None, :] < block_count[:, None]).astype(jnp.float32)
    live_flat = live_mask.reshape(-1)
    live_weight = live_flat.astype(jnp.bfloat16)
    partial_value = masked_total(live_weight, sensitivity)
    raw_own = lax.psum(partial_value, "trade")
    raw_all = lax.all_gather(raw_own, "factor", axis=0, tiled=True)
    onehot_all = (jnp.arange(BUCKETS, dtype=jnp.int32)[:, None] == factor_bucket[None, :]).astype(
        jnp.float32
    )
    factor_weight = jnp.sum(onehot_all * risk_weight[:, None], 0)
    weighted = factor_weight * raw_all
    bucket_sums = jnp.dot(onehot_all, weighted, precision=lax.Precision.HIGHEST)
    name_bucket = factor_bucket.reshape(-1, TENORS)[:, 0]
    own_onehot = lax.dynamic_slice_in_dim(onehot_all, own_start, own_width, 1)
    own_weighted = lax.dynamic_slice_in_dim(weighted, own_start, own_width, 0)
    own_factor_weight = lax.dynamic_slice_in_dim(factor_weight, own_start, own_width, 0)
    own_products = correlated(weighted, name_bucket, own_start // TENORS, own_width // TENORS)
    form_part = jnp.dot(
        own_products * own_weighted[None, :], own_onehot.T, precision=lax.Precision.HIGHEST
    )
    bucket_forms = lax.psum(form_part, "factor")
    capital, coef_form, coef_sum = capital_terms(bucket_forms, bucket_sums, bucket_loading)
    gradient = own_factor_weight[None, :] * (
        own_products * jnp.dot(coef_form, own_onehot, precision=lax.Precision.HIGHEST)
        + jnp.dot(coef_sum, own_onehot, precision=lax.Precision.HIGHEST)
    )
    spread = (
        (gradient[:, None, :] * own_onehot[None, :, :])
        .reshape(SCEN * BUCKETS, own_width)
        .astype(jnp.bfloat16)
    )
    contract = (((1,), (1,)), ((), ()))
    alloc = (
        lax.dot_general(spread, sensitivity, contract, preferred_element_type=jnp.float32)
        * live_flat[None, :]
    )
    alloc_sums = lax.psum_scatter(alloc, "factor", scatter_dimension=1, tiled=True)
    share_rows = alloc_sums.shape[1]
    own_nodes = lax.dynamic_slice_in_dim(
        trade_node, lax.axis_index("factor") * share_rows, share_rows, 0
    )
    node_part = node_partial(alloc_sums, own_nodes)
    trade_sums = alloc_sums.reshape(SCEN, BUCKETS, share_rows).sum(1)
    node_sums = lax.psum_scatter(node_part, ("trade", "factor"), scatter_dimension=1, tiled=True)
    trade_alloc = trade_sums * (trades_total / capital)[:, None]
    node_alloc = (
        node_sums.reshape(SCEN, BUCKETS, node_sums.shape[1]) * (NODES / capital)[:, None, None]
    )
    capital_scaled = capital / trades_total**0.5
    return (capital_scaled, trade_alloc, node_alloc)


def solution(mesh):
    return jax.shard_map(
        local,
        mesh=mesh,
        in_specs=(P("trade", "factor"), P("trade"), P("trade"), P(), P(), P()),
        out_specs=(P(), P(None, ("trade", "factor")), P(None, None, ("trade", "factor"))),
        check_vma=False,
    )
```

profile of v0, /device:TPU:0, one launch (start us, length us, event | category | flops | bytes accessed | tf_op | source)
XLA Modules:
  0.0 246.3 jit_solution(2842809727241680529)
XLA Ops:
  7.2 0.0 copy-start.7
  7.2 0.0 copy-start.1
  7.2 0.0 copy-start.2
  7.2 0.0 reduce-scatter.3.cloned.1.call-start
  7.3 0.7 convert_bitcast_fusion
  8.0 0.0 copy-start.5
  8.0 0.0 copy-start.4
  8.1 0.0 copy-start.8
  8.1 0.0 copy-start.9
  8.1 0.0 copy-start.3
  8.1 0.0 copy-start.6
  8.1 8.2 %convolution_reduce_fusion = f32[1600]{0:T(1024)S(1)} fusion(bf16[4096,1]{0,1:T(2,128)(2,1)S(1)} %reshape.203, bf16[4096,1600]{0,1:T(8,128)(2,1)} %param.8), kind=kOutput, calls=%fused_computation.17 | convolution fusion | flops 13107200 | bytes 13121792 | tf_op jit(solution)/shard_map/dot_general | solution.py:68
  16.3 23.4 %psum.14 = f32[1600]{0:T(1024)S(1)} all-reduce(f32[1600]{0:T(1024)S(1)} %convolution_reduce_fusion), channel_id=1, replica_groups=mesh['trade'=8,'factor'=4] {'trade'}, use_global_device_ids=true, to_apply=%region_1.0 | all-reduce | flops 1600 | bytes 12800 | tf_op jit(solution)/shard_map/psum | solution.py:100
  39.8 0.6 dynamic-slice
  41.0 0.3 dynamic-update-slice
  41.3 10.3 %all-reduce = f32[6400]{0:T(1024)S(1)} all-reduce(f32[6400]{0:T(1024)S(1)} %dynamic-update-slice), channel_id=1, replica_groups=mesh['trade'=8,'factor'=4] {'factor'}, use_global_device_ids=true, to_apply=%add | all-reduce | flops 6400 | bytes 51200
  51.6 0.5 reshape.193
  52.1 0.2 select_reduce_fusion
  52.3 0.5 reshape.194
  52.8 0.2 slice_reduce_fusion
  53.1 0.7 fusion.49
  53.8 0.2 reduce_sum.65
  54.0 0.1 iota_compare_fusion.12
  54.1 0.1 dynamic_slice.26
  54.2 0.1 dynamic_slice.28
  54.3 0.2 convolution_reduce_fusion.1
  54.6 0.1 broadcast_multiply_fusion.3
  54.6 0.2 add.90
  54.8 0.3 add.91
  55.1 0.4 fusion.24
  55.5 0.2 mul.237
  55.7 0.1 dynamic_slice.24
  55.8 0.1 broadcast_multiply_fusion.2
  55.9 0.2 add.93
  56.1 0.3 add.94
  56.4 0.2 mul.244
  56.6 0.1 dynamic-slice_convert_fusion
  56.7 0.0 copy-done.8
  56.7 0.0 copy-done.9
  56.7 0.2 fusion.19
  57.0 6.5 %psum.15 = f32[3,18]{1,0:T(4,128)S(1)} all-reduce(f32[3,18]{1,0:T(4,128)S(1)} %fusion.19), channel_id=1, replica_groups=mesh['trade'=8,'factor'=4] {'factor'}, use_global_device_ids=true, to_apply=%region_4.5 | all-reduce | flops 54 | bytes 432 | tf_op jit(solution)/shard_map/psum | solution.py:116
  63.4 0.4 fusion.48
  63.8 0.0 copy-done.3
  63.9 0.2 multiply_reduce_fusion.1
  64.0 0.0 copy-done.6
  64.1 0.3 convolution_multiply_fusion.1
  64.3 0.3 fusion.11
  64.6 0.1 convert_element_type.44
  64.7 8.0 %convolution_multiply_fusion = f32[54,4096]{1,0:T(8,128)} fusion(bf16[54,1600]{1,0:T(8,128)(2,1)S(1)} %convert_element_type.44, bf16[4096,1600]{0,1:T(8,128)(2,1)} %param.8, f32[4096]{0:T(1024)S(1)} %bitcast.20), kind=kOutput, calls=%fused_computation.9 | convolution fusion | flops 708009984 | bytes 14181120 | tf_op jit(solution)/shard_map/dot_general | solution.py:129
  72.7 0.0 reduce-scatter.3.cloned.1.call-update
  72.8 0.2 reduce-scatter.5.cloned.1.call-start
  73.0 0.7 dynamic_slice.30
  73.7 20.0 %reduce-scatter.3.cloned.1.call-done = f32[54,1024]{1,0:T(8,128)} async-done(((f32[54,4096]{1,0:T(8,128)}), f32[54,1024]{1,0:T(8,128)}) %reduce-scatter.3.cloned.1.call-update) | async-done | bytes 221200 | tf_op jit(solution)/shard_map/reduce_scatter | solution.py:132
  93.7 1.1 subtract_convert_fusion
  94.8 1.8 fusion.2
  96.7 1.8 fusion.4
  98.5 1.8 fusion.5
  100.3 2.7 %fusion.6 = f32[54,4096]{1,0:T(8,128)} fusion(f32[54,4096]{1,0:T(8,128)S(1)} %fusion.5, s32[512]{0:T(512)S(1)} %get-tuple-element.10, bf16[54,1024]{1,0:T(8,128)(2,1)S(1)} %get-tuple-element.8), kind=kOutput, calls=%fused_computation.8 | convolution fusion | flops 228810752 | bytes 1861632 | tf_op jit(solution)/shard_map/dot_general | solution.py:85
  103.0 0.0 reduce-scatter.5.cloned.1.call-update
  103.1 0.5 broadcast_divide_fusion.1
  103.7 0.7 broadcast_multiply_fusion.1
  104.3 133.7 %reduce-scatter.5.cloned.1.call-done = f32[54,128]{1,0:T(8,128)} async-done(((f32[54,4096]{1,0:T(8,128)}), f32[54,128]{1,0:T(8,128)}) %reduce-scatter.5.cloned.1.call-update) | async-done | bytes 27664 | tf_op jit(solution)/shard_map/reduce_scatter | solution.py:139
  238.0 0.8 reshape.196
  238.8 0.7 broadcast_multiply_fusion
  (21 shorter events, 0.3 us)
Async XLA Ops:
  7.2 32.6 %copy-start.7 = (u32[32]{0:T(128)S(1)}, u32[32]{0:T(128)}, u32[]{:S(2)}) copy-start(u32[32]{0:T(128)} %constant.82) | copy-start | bytes 388
  7.2 44.4 %copy-start.1 = (s32[6400]{0:T(1024)S(1)}, s32[6400]{0:T(1024)}, u32[]{:S(2)}) copy-start(s32[6400]{0:T(1024)} %param.11) | copy-start | bytes 76804
  7.2 44.9 %copy-start.2 = (f32[18]{0:T(128)S(1)}, f32[18]{0:T(128)}, u32[]{:S(2)}) copy-start(f32[18]{0:T(128)} %param.12) | copy-start | bytes 220
  7.2 86.5 %reduce-scatter.3.cloned.1.call-start = ((), (), s32[]{:S(2)}) async-start(), calls=%async_computation.2 | async-start | bytes 1146880 | tf_op jit(solution)/shard_map/reduce_scatter | solution.py:132
  8.0 46.5 %copy-start.5 = (f32[3]{0:T(128)S(1)}, f32[3]{0:T(128)}, u32[]{:S(2)}) copy-start(f32[3]{0:T(128)} %constant.67) | copy-start | bytes 40
  8.0 47.8 %copy-start.4 = (f32[3]{0:T(128)S(1)}, f32[3]{0:T(128)}, u32[]{:S(2)}) copy-start(f32[3]{0:T(128)} %constant.73) | copy-start | bytes 40
  8.1 48.7 %copy-start.8 = (f32[3]{0:T(128)S(1)}, f32[3]{0:T(128)}, u32[]{:S(2)}) copy-start(f32[3]{0:T(128)} %constant.70) | copy-start | bytes 40
  8.1 48.7 %copy-start.9 = (f32[3]{0:T(128)S(1)}, f32[3]{0:T(128)}, u32[]{:S(2)}) copy-start(f32[3]{0:T(128)} %constant.78) | copy-start | bytes 40
  8.1 55.8 %copy-start.3 = (f32[18]{0:T(128)S(1)}, f32[18]{0:T(128)}, u32[]{:S(2)}) copy-start(f32[18]{0:T(128)} %param.13) | copy-start | bytes 220
  8.1 56.0 %copy-start.6 = (f32[3]{0:T(128)S(1)}, f32[3]{0:T(128)}, u32[]{:S(2)}) copy-start(f32[3]{0:T(128)} %constant.79) | copy-start | bytes 40
  72.8 165.3 %reduce-scatter.5.cloned.1.call-start = ((), (), s32[]{:S(2)}) async-start(), calls=%async_computation.3 | async-start | bytes 946176 | tf_op jit(solution)/shard_map/reduce_scatter | solution.py:139
  93.7 9.9 %copy-start = (f32[54,1024]{1,0:T(8,128)S(1)}, f32[54,1024]{1,0:T(8,128)}, u32[]{:S(2)}) copy-start(f32[54,1024]{1,0:T(8,128)} %reduce-scatter.3.cloned.1.call-done) | copy-start | bytes 663556
Sparse Core Ops, SparseCore 0:
  72.9 20.8 reduce-scatter.2
  103.2 134.7 reduce-scatter.4
where the time goes:
time: 247 us; the launch traced here: 246 us
  waiting for transfers between devices  154 us (62%)
  blocking collectives  40.1 us (16%)
  matrix products  26.9 us (11%)
  between operations  15.1 us (6%)
  local copies, waits for them, and re-layouts  5.43 us (2%)
  other arithmetic  4.82 us (2%)
    reduce_scatter x1, waiting for transfers between devices, local(): lax.psum_scatter(node_part, ('trade', 'factor'), scatter_dimension=1, til...  134 us
    psum x1, blocking collectives, local(): raw_own = lax.psum(partial_value, 'trade')  23.4 us
    reduce_scatter x1, waiting for transfers between devices, local(): lax.psum_scatter(alloc, 'factor', scatter_dimension=1, tiled=True)  20 us
    unnamed x1, blocking collectives  10.3 us
    dot_general x1, matrix products, masked_total(): jnp.dot(weights[None, :], piece_sens, preferred_element_type=jnp.float32)[0]  8.24 us
    dot_general x1, matrix products, local(): lax.dot_general(spread, sensitivity, contract, preferred_element_type=jnp...  8.02 us
    psum x1, blocking collectives, local(): bucket_forms = lax.psum(form_part, 'factor')  6.45 us
  transfers between devices with their start and end apart: 2, of which 2 were waited for; matrix products, arithmetic and copies ran while one was open for 1% of the time, Pallas kernels for 0%

commit v1 on v0

v1 whole, which is shorter than its diff:
```python
import functools

import jax
import jax.numpy as jnp
import numpy as np
from jax import lax
from jax.experimental import pallas as pl
from jax.experimental.pallas import tpu as pltpu
from jax.sharding import PartitionSpec as P

TENORS = 5
BUCKETS = 18
SCEN = 3
NODES = 4096
BLOCK = 512
ROWS = 3 * BUCKETS
LOW = 256
HIGH = NODES // LOW
AXES = ("trade", "factor")
MIB = 1 << 20

BASE = np.array([1.0, 0.65, 0.35, 0.2275], np.float32)
LEVELS = np.stack([BASE, np.minimum(1.25 * BASE, 1.0), np.maximum(2.0 * BASE - 1.0, 0.75 * BASE)])
SCENARIO = (1.0, 1.25, 0.75)
CROSS = 0.5
SAME_BOTH = LEVELS[:, 0] - LEVELS[:, 1] - LEVELS[:, 2] + LEVELS[:, 3]

SMEM = pl.BlockSpec(memory_space=pltpu.SMEM)
VMEM = pl.BlockSpec(memory_space=pltpu.VMEM)
ANY = pl.BlockSpec(memory_space=pl.ANY)
f32 = jnp.float32
bf16 = jnp.bfloat16


def shape(*dims, dtype=f32):
    return jax.ShapeDtypeStruct(dims, dtype)


def call(kernel, out_shape, in_specs, out_specs, name, scratch=(), flops=0, limit=24):
    return pl.pallas_call(
        kernel,
        out_shape=out_shape,
        in_specs=in_specs,
        out_specs=out_specs,
        scratch_shapes=list(scratch),
        name=name,
        compiler_params=pltpu.CompilerParams(vmem_limit_bytes=limit * MIB),
        cost_estimate=pl.CostEstimate(flops=flops, bytes_accessed=1 << 16, transcendentals=0),
    )


def dot_t(a, b):
    return lax.dot_general(a, b, (((1,), (1,)), ((), ())), preferred_element_type=f32)


def totals_kernel(count, sens, held, raw, sems):
    blocks = count.shape[0]
    width = sens.shape[1]
    copies = []
    for i in range(blocks):
        part = pl.ds(i * BLOCK, BLOCK)
        copies.append(pltpu.make_async_copy(sens.at[part], held.at[part], sems.at[i]))
        copies[-1].start()
    row = lax.broadcasted_iota(jnp.int32, (16, width), 0)
    total = jnp.zeros((16, width), f32)
    for i in range(blocks):
        copies[i].wait()
        live = count[i]

        def step(g, total):
            part = held[pl.ds(pl.multiple_of(i * BLOCK + g * 16, 16), 16), :].astype(f32)
            return total + jnp.where(row < live - g * 16, part, 0.0)

        total = lax.fori_loop(0, BLOCK // 16, step, total, unroll=4)
    raw[...] = jnp.sum(total, 0, keepdims=True)


def tables_kernel(
    me,
    weight,
    nodes,
    bucket,
    tenor,
    low_hot,
    high_hot,
    spread_hot,
    tenor_hot,
    factor_weight,
    *,
    spots,
):
    bits = len(spots[0])
    inner = (NODES >> bits).bit_length() - 1
    node = nodes[...]
    owner = node >> inner
    other = owner ^ me[0]
    label = node & ((1 << inner) - 1)
    for i in range(bits):
        spot = jnp.where((owner & 1) == 0, spots[0][i], spots[1][i])
        label = label + ((other >> i) & 1) * spot
    low = label & (LOW - 1)
    high = label >> (LOW.bit_length() - 1)
    trades = node.shape[1]
    for start in range(0, trades, 512):
        part = pl.ds(start, 512)
        here = lax.broadcasted_iota(jnp.int32, (LOW, 512), 0) == low[:, start : start + 512]
        low_hot[:, part] = jnp.where(here, 1.0, 0.0).astype(bf16)
        here = lax.broadcasted_iota(jnp.int32, (HIGH, 512), 0) == high[:, start : start + 512]
        high_hot[:, part] = jnp.where(here, 1.0, 0.0).astype(bf16)
    own = bucket[...]
    width = own.shape[1]
    row = lax.broadcasted_iota(jnp.int32, (56, width), 0)
    hit = (row == own) | (row == own + BUCKETS) | (row == own + 2 * BUCKETS)
    spread_hot[...] = jnp.where(hit, 1.0, 0.0)
    row = lax.broadcasted_iota(jnp.int32, (24, width), 0)
    for m in range(TENORS):
        tenor_hot[24 * m : 24 * m + 24, :] = jnp.where(
            (row == own) & (tenor[...] == m), 1.0, 0.0
        )
    total = jnp.zeros((1, width), f32)
    for b in range(BUCKETS):
        total = jnp.where(own == b, weight[b], total)
    factor_weight[...] = total


def weights_kernel(first, second, factor_weight, tenor, spread_hot, tenor_hot, spread, sums):
    width = first.shape[1]
    weighted = factor_weight[...] * (first[...] + second[...])
    own_tenor = tenor[...]
    name = weighted
    for d in range(1, TENORS):
        zeros = jnp.zeros((1, d), f32)
        after = jnp.concatenate([weighted[:, d:], zeros], 1)
        before = jnp.concatenate([zeros, weighted[:, : width - d]], 1)
        name = name + jnp.where(own_tenor < TENORS - d, after, 0.0)
        name = name + jnp.where(own_tenor >= d, before, 0.0)
    near = float(LEVELS[0, 1] - LEVELS[0, 3]) * name + float(SAME_BOTH[0]) * weighted
    row = lax.broadcasted_iota(jnp.int32, (56, width), 0)
    value = jnp.where(row < BUCKETS, near, jnp.where(row < 2 * BUCKETS, weighted, 1.0))
    full = spread_hot[...] * value
    upper = full.astype(bf16)
    lower = (full[:40] - upper[:40].astype(f32)).astype(bf16)
    spread[...] = jnp.concatenate(
        [upper.astype(f32), tenor_hot[...], lower.astype(f32)], 0
    ).astype(bf16)
    lane = lax.broadcasted_iota(jnp.int32, (24, 128), 1)
    out = jnp.zeros((24, 128), f32)
    square = jnp.zeros((24, 1), f32)
    for m in range(TENORS):
        hot = tenor_hot[24 * m : 24 * m + 24, :]
        part = hot * weighted
        out = jnp.where(lane == m, jnp.sum(part, 1, keepdims=True), out)
        square = square + jnp.sum(part * weighted, 1, keepdims=True)
        if m == 0:
            names = jnp.sum(hot * (name * name), 1, keepdims=True)
    out = jnp.where(lane == TENORS, square, out)
    out = jnp.where(lane == TENORS + 1, names, out)
    sums[...] = out


def spread_kernel(spread, held, near, tenors):
    trades = held.shape[0]
    for start in range(0, trades, BLOCK):
        part = pl.ds(start, BLOCK)
        out = dot_t(spread[...], held[part, :])
        near[:, part] = jnp.concatenate([out[:40] + out[176:216], out[40:56]], 0)
        tenors[:, part] = out[56:176]


def nodes_kernel(
    count, sums, more, near, tenors, low_hot, high_hot, alloc, total, keep, send, rounded
):
    trades = near.shape[1]
    gather = sums[...] + more[...]
    total[...] = gather
    lane = lax.broadcasted_iota(jnp.int32, (24, 128), 1)
    bucket = jnp.sum(jnp.where(lane < TENORS, gather, 0.0), 1, keepdims=True)
    pull = [
        float(LEVELS[0, 2] - LEVELS[0, 3]) * gather[:, m : m + 1] + float(LEVELS[0, 3]) * bucket
        for m in range(TENORS)
    ]
    slot = lax.broadcasted_iota(jnp.int32, (1, BLOCK), 1)
    for i in range(trades // BLOCK):
        part = pl.ds(i * BLOCK, BLOCK)
        live = jnp.where(slot < count[i], 1.0, 0.0)
        far = near[:24, part]
        for m in range(TENORS):
            far = far + pull[m] * tenors[24 * m : 24 * m + 24, part]
        value = jnp.concatenate([far, near[24:, part]], 0) * live
        alloc[:, part] = value
        rounded[:, part] = jnp.concatenate([value, jnp.zeros((8, BLOCK), f32)], 0).astype(bf16)
    step = 4
    for h in range(0, HIGH, step):
        value = rounded[...]
        masked = jnp.concatenate([value * high_hot[h + j : h + j + 1, :] for j in range(step)], 0)
        out = dot_t(masked, low_hot[...])
        for j in range(step):
            keep[h + j] = out[64 * j : 64 * j + ROWS, : LOW // 2]
            send[h + j] = out[64 * j : 64 * j + ROWS, LOW // 2 :]


def capital_kernel(place, terms, total, alloc, keep, send, mix, capital, *, trades_total):
    parts = 2 * keep.shape[0]
    length = keep.shape[2]
    gather = total[...]
    lane = lax.broadcasted_iota(jnp.int32, (24, 128), 1)
    real = lax.broadcasted_iota(jnp.int32, (24, 1), 0) < BUCKETS
    risk = terms[:, 0:1]
    loading = terms[:, 1:2]
    tenor_part = jnp.where(lane < TENORS, gather, 0.0)
    sums = jnp.sum(tenor_part, 1, keepdims=True)
    tenor_square = jnp.sum(tenor_part * tenor_part, 1, keepdims=True)
    own_square = gather[:, TENORS : TENORS + 1]
    name_square = gather[:, TENORS + 1 : TENORS + 2]
    columns = []
    row8 = lax.broadcasted_iota(jnp.int32, (8, 128), 0)
    capitals = jnp.zeros((8, 128), f32)
    for s in range(SCEN):
        level = [float(v) for v in LEVELS[s]]
        form = level[3] * sums * sums + (level[2] - level[3]) * tenor_square
        form = form + (level[1] - level[3]) * name_square + float(SAME_BOTH[s]) * own_square
        root = jnp.sqrt(form + 1e-6)
        radius = jnp.sqrt(root * root + sums * sums)
        capped = sums * root / radius
        pulled = jnp.where(real, loading * capped, 0.0)
        loaded = jnp.sum(pulled, 0, keepdims=True)
        squares = jnp.sum(pulled * pulled, 0, keepdims=True)
        cross = CROSS * SCENARIO[s]
        inside = jnp.sum(jnp.where(real, root * root, 0.0), 0, keepdims=True)
        cap = jnp.sqrt(inside + cross * (loaded * loaded - squares))
        cross_pull = cross * (loading * loaded - loading * loading * capped) / cap
        ratio = sums / radius
        share = root / radius
        coef_form = (root / cap + cross_pull * ratio * ratio * ratio) / root
        coef_sum = cross_pull * share * share * share
        scale = risk / cap
        columns.append(
            [
                (scale * coef_form * SCENARIO[s])[:BUCKETS],
                (scale * coef_form * (1.0 - SCENARIO[s]))[:BUCKETS],
                (scale * coef_sum)[:BUCKETS],
            ]
        )
        capitals = jnp.where(row8 == s, cap, capitals)
    capital[...] = capitals
    column = []
    for s in range(SCEN):
        column.append(jnp.concatenate(columns[s] + [jnp.zeros((2, 1), f32)], 0))
        mix[s] = jnp.broadcast_to(column[s][:ROWS] * float(NODES), (ROWS, 128))
    for p in range(parts):
        block = place[p]
        rows = pl.ds(pl.multiple_of(block * length, 128), length)
        value = alloc[:, rows]
        out = jnp.concatenate(
            [jnp.sum(value * (column[s] * float(trades_total)), 0, keepdims=True) for s in range(SCEN)],
            0,
        )
        if p < parts // 2:
            keep[p] = out
        else:
            send[p - parts // 2] = out


def bit_reverse(value, bits):
    return sum(((value >> i) & 1) << (bits - 1 - i) for i in range(bits))


def local(
    sensitivity,
    block_count,
    trade_node,
    factor_bucket,
    risk_weight,
    bucket_loading,
    *,
    trade_size,
    factor_size,
):
    trade_rows, width = sensitivity.shape
    trades_total = trade_rows * trade_size
    devices = trade_size * factor_size
    trade_bits = trade_size.bit_length() - 1
    factor_bits = factor_size.bit_length() - 1
    bits = trade_bits + factor_bits
    inner = (NODES // devices).bit_length() - 1
    t = lax.axis_index("trade")
    f = lax.axis_index("factor")
    me = t * factor_size + f

    def exchange(x, bit_of):
        pairs = [(o, o ^ (1 << bit_of(o))) for o in range(devices)]
        return lax.ppermute(x, AXES, pairs)

    upper_f = list(range(1, factor_bits))
    all_t = list(range(factor_bits, bits))
    orders = [upper_f + all_t, all_t[:2] + upper_f + all_t[2:]]
    places = [7, 11, 10, 9, 8, 6, 5, 4, 3, 2, 1, 0]
    spots = [[0] * bits, [0] * bits]
    for c in range(2):
        for i, bit in enumerate([0] + orders[c]):
            spots[c][bit] = 1 << places[i]
    block_order = jnp.array(
        [bit_reverse(p, factor_bits) for p in range(factor_size)], jnp.int32
    ) ^ f.astype(jnp.int32)
    bucket = lax.dynamic_slice_in_dim(factor_bucket, f * width, width, 0)[None, :]
    tenor = (jnp.arange(width, dtype=jnp.int32) % TENORS)[None, :]
    terms = jnp.zeros((24, 128), f32)
    terms = terms.at[:BUCKETS, 0].set(risk_weight).at[:BUCKETS, 1].set(bucket_loading)

    held, raw = call(
        totals_kernel,
        (pltpu.VMEM(sensitivity.shape, bf16), shape(1, width)),
        [SMEM, ANY],
        (VMEM, VMEM),
        "totals",
        scratch=[pltpu.SemaphoreType.DMA((block_count.shape[0],))],
        flops=10**7,
    )(block_count, sensitivity)

    low_hot, high_hot, spread_hot, tenor_hot, factor_weight = call(
        functools.partial(tables_kernel, spots=spots),
        (
            pltpu.VMEM((LOW, trade_rows), bf16),
            pltpu.VMEM((HIGH, trade_rows), bf16),
            pltpu.VMEM((56, width), f32),
            pltpu.VMEM((24 * TENORS, width), f32),
            pltpu.VMEM((1, width), f32),
        ),
        [SMEM, SMEM, VMEM, VMEM, VMEM],
        (VMEM,) * 5,
        "tables",
        flops=10**7,
    )(me.astype(jnp.int32)[None], risk_weight, trade_node[None, :], bucket, tenor)

    other = None
    for i in range(trade_bits):
        if other is not None:
            raw = raw + other
        other = exchange(raw, lambda o, i=i: factor_bits + i)

    spread, sums = call(
        weights_kernel,
        (pltpu.VMEM((216, width), bf16), shape(24, 128)),
        [VMEM] * 6,
        (VMEM, VMEM),
        "weights",
        flops=10**6,
    )(raw, other, factor_weight, tenor, spread_hot, tenor_hot)

    near, tenors = call(
        spread_kernel,
        (pltpu.VMEM((56, trade_rows), f32), pltpu.VMEM((24 * TENORS, trade_rows), f32)),
        [VMEM, VMEM],
        (VMEM, VMEM),
        "spread",
        flops=2 * 216 * width * trade_rows,
    )(spread, held)

    more = None
    for i in range(factor_bits):
        if more is not None:
            sums = sums + more
        more = exchange(sums, lambda o, i=i: i)

    alloc, total, keep, send = call(
        nodes_kernel,
        (
            pltpu.VMEM((56, trade_rows), f32),
            shape(24, 128),
            shape(HIGH, ROWS, LOW // 2),
            shape(HIGH, ROWS, LOW // 2),
        ),
        [SMEM, VMEM, VMEM, VMEM, VMEM, VMEM, VMEM],
        (VMEM,) * 4,
        "nodes",
        scratch=[pltpu.VMEM((64, trade_rows), bf16)],
        flops=2 * 1024 * trade_rows * LOW,
        limit=40,
    )(block_count, sums, more, near, tenors, low_hot, high_hot)

    length = trade_rows // factor_size
    trade_keep, trade_send, mix, capital = call(
        functools.partial(capital_kernel, trades_total=trades_total),
        (
            shape(factor_size // 2, SCEN, length),
            shape(factor_size // 2, SCEN, length),
            shape(SCEN, ROWS, 128),
            shape(8, 128),
        ),
        [SMEM, VMEM, VMEM, VMEM],
        (VMEM,) * 4,
        "capital",
        flops=10**7,
    )(block_order, terms, total, alloc)

    keep = keep + exchange(send, lambda o: 0)
    for i in range(bits - 1):
        if keep.shape[0] > 1:
            half = keep.shape[0] // 2
            send, keep = keep[half:], keep[:half]
        else:
            half = keep.shape[2] // 2
            send, keep = keep[..., half:], keep[..., :half]
        keep = keep + exchange(send, lambda o, i=i: orders[o & 1][i])
    keep = keep[0]

    trade_keep = trade_keep + exchange(trade_send, lambda o: 0)
    for i in range(1, factor_bits):
        half = trade_keep.shape[0] // 2
        trade_send, trade_keep = trade_keep[half:], trade_keep[:half]
        trade_keep = trade_keep + exchange(trade_send, lambda o, i=i: i)

    mixed = mix[:, :, : keep.shape[1]] * keep[None]
    node_alloc = mixed.reshape(SCEN, 3, BUCKETS, keep.shape[1]).sum(1)
    capital_scaled = capital[:SCEN, 0] / trades_total**0.5
    return (capital_scaled, trade_keep[0], node_alloc)


def solution(mesh):
    sizes = dict(mesh.shape)
    return jax.shard_map(
        functools.partial(local, trade_size=sizes["trade"], factor_size=sizes["factor"]),
        mesh=mesh,
        in_specs=(P("trade", "factor"), P("trade"), P("trade"), P(), P(), P()),
        out_specs=(P(), P(None, ("trade", "factor")), P(None, None, ("trade", "factor"))),
        check_vma=False,
    )
```

time: 247 us -> 87.4 us (0.35)
  waiting for transfers between devices: 154 us -> 14.5 us
  blocking collectives: 40.1 us -> 0 us
  local copies, waits for them, and re-layouts: 5.43 us -> 35.9 us
  matrix products: 26.9 us -> 0 us
  starting transfers between devices: 0.26 us -> 16.9 us
  Pallas kernels: 0 us -> 16.6 us
  between operations: 15.1 us -> 0.85 us
  other arithmetic: 4.82 us -> 2.04 us
    reduce_scatter x2 -> x0, waiting for transfers between devices: 154 us -> none  [the longest x1 134 us: local(): lax.psum_scatter(node_part, ('trade', 'factor'), scatter_dimension=1, til...]
    unnamed x24 -> x17, local copies, waits for them, and re-layouts: 0.98 us -> 32.6 us
    psum x2 -> x0, blocking collectives: 29.8 us -> none  [the longest x1 23.4 us: local(): raw_own = lax.psum(partial_value, 'trade')]
    dot_general x13 -> x0, matrix products: 26.9 us -> none  [the longest x1 8.24 us: masked_total(): jnp.dot(weights[None, :], piece_sens, preferred_element_type=jnp.float32)[0]]
    ppermute x0 -> x12, starting transfers between devices: none -> 16.9 us  [exchange(): return lax.ppermute(x, AXES, pairs)]
    pallas_call x0 -> x6, Pallas kernels: none -> 16.6 us  [the longest x1 6.16 us: local(): call(totals_kernel, (pltpu.VMEM(sensitivity.shape, bf16), shape(1, width)...]
    ppermute x0 -> x12, waiting for transfers between devices: none -> 14.5 us  [exchange(): return lax.ppermute(x, AXES, pairs)]
    unnamed x1 -> x0, blocking collectives: 10.3 us -> none
  transfers between devices with their start and end apart: 2 -> 12, of which waited for: 2 -> 7; matrix products, arithmetic and copies ran while one was open for 1% -> 5% of each run, Pallas kernels for 0% -> 8%
where the time goes in v1:
time: 87.4 us; the launch traced here: 86.7 us
  local copies, waits for them, and re-layouts  35.9 us (41%)
  starting transfers between devices  16.9 us (19%)
  Pallas kernels  16.6 us (19%)
  waiting for transfers between devices  14.5 us (17%)
  other arithmetic  2.04 us (2%)
    unnamed x17, local copies, waits for them, and re-layouts  32.6 us
    ppermute x12, starting transfers between devices, exchange(): return lax.ppermute(x, AXES, pairs)  16.9 us
    ppermute x12, waiting for transfers between devices, exchange(): return lax.ppermute(x, AXES, pairs)  14.5 us
    pallas_call x1, Pallas kernels, local(): call(totals_kernel, (pltpu.VMEM(sensitivity.shape, bf16), shape(1, width)...  6.16 us
    pallas_call x1, Pallas kernels, local(): call(spread_kernel, (pltpu.VMEM((56, trade_rows), f32), pltpu.VMEM((24 *...  4.35 us
    pallas_call x1, Pallas kernels, local(): call(nodes_kernel, (pltpu.VMEM((56, trade_rows), f32), shape(24, 128), sh...  3.05 us
  transfers between devices with their start and end apart: 12, of which 7 were waited for; matrix products, arithmetic and copies ran while one was open for 5% of the time, Pallas kernels for 8%

profile of v1, /device:TPU:0, one launch (start us, length us, event | category | flops | bytes accessed | tf_op | source)
XLA Modules:
  0.0 86.7 jit_solution(673374051720538842)
XLA Ops:
  0.6 0.0 copy-start.3
  0.6 17.9 %copy.15.sens = bf16[4096,1600]{1,0:T(8,128)(2,1)} copy(bf16[4096,1600]{0,1:T(8,128)(2,1)} %param.11) | data formatting | bytes 26214400 | tf_op args[0]
  18.5 0.0 copy-done.3
  18.5 0.0 copy-start
  18.5 4.9 %copy-done = bf16[4096,1600]{1,0:T(8,128)(2,1)S(1)} copy-done((bf16[4096,1600]{1,0:T(8,128)(2,1)S(1)}, bf16[4096,1600]{1,0:T(8,128)(2,1)}, u32[]{:S(2)}) %copy-start) | copy-done | bytes 13107224
  23.4 0.0 copy-start.4
  23.4 0.0 copy-start.5
  23.4 6.2 %totals.1 = (bf16[4096,1600]{1,0:T(8,128)(2,1)S(1)}, f32[1,1600]{1,0:T(1,128)S(1)}) custom-call(s32[8]{0:T(128)S(1)} %copy-done.3, bf16[4096,1600]{1,0:T(8,128)(2,1)S(1)} %copy-done), custom_call_target="tpu_custom_call" | custom-call | flops 10000000 | bytes 65536 | tf_op jit(solution)/shard_map/totals/pallas_call | solution.py:310
  29.6 0.0 copy-start.1
  29.6 4.9 %copy-done.1 = bf16[4096,1600]{1,0:T(8,128)(2,1)} copy-done((bf16[4096,1600]{1,0:T(8,128)(2,1)}, bf16[4096,1600]{1,0:T(8,128)(2,1)S(1)}, u32[]{:S(2)}) %copy-start.1) | copy-done | bytes 13107224
  34.5 0.0 copy-start.6
  34.5 0.0 copy-start.7
  34.5 3.0 %collective-permute-start = (f32[1,1600]{1,0:T(1,128)S(1)}, f32[1,1600]{1,0:T(1,128)S(1)}, u32[]{:S(2)}, u32[]{:S(2)}) collective-permute-start(f32[1,1600]{1,0:T(1,128)S(1)} %get-tuple-element.46), channel_id=1, source_target_pairs={{0,4},{1,5},{2,6},{3,7},{4,0},{5,1},{6,2},{7,3},{8,12},{9,13},{10,... | collective-permute-start | bytes 19208 | tf_op jit(solution)/shard_map/ppermute | solution.py:292
  37.5 1.6 %collective-permute-done = f32[1,1600]{1,0:T(1,128)S(1)} collective-permute-done((f32[1,1600]{1,0:T(1,128)S(1)}, f32[1,1600]{1,0:T(1,128)S(1)}, u32[]{:S(2)}, u32[]{:S(2)}) %collective-permute-start) | collective-permute-done | bytes 6432 | tf_op jit(solution)/shard_map/ppermute | solution.py:292
  39.1 2.1 %collective-permute-start.1 = (f32[1,1600]{1,0:T(1,128)S(1)}, f32[1,1600]{1,0:T(1,128)S(1)}, u32[]{:S(2)}, u32[]{:S(2)}) collective-permute-start(f32[1,1600]{1,0:T(1,128)S(1)} %add.57), channel_id=1, source_target_pairs={{0,8},{1,9},{2,10},{3,11},{4,12},{5,13},{6,14},{7,15},{8,0},{9,1},... | collective-permute-start | bytes 19208 | tf_op jit(solution)/shard_map/ppermute | solution.py:292
  41.2 1.6 %collective-permute-done.1 = f32[1,1600]{1,0:T(1,128)S(1)} collective-permute-done((f32[1,1600]{1,0:T(1,128)S(1)}, f32[1,1600]{1,0:T(1,128)S(1)}, u32[]{:S(2)}, u32[]{:S(2)}) %collective-permute-start.1) | collective-permute-done | bytes 6432 | tf_op jit(solution)/shard_map/ppermute | solution.py:292
  42.9 3.1 %collective-permute-start.2 = (f32[1,1600]{1,0:T(1,128)S(1)}, f32[1,1600]{1,0:T(1,128)S(1)}, u32[]{:S(2)}, u32[]{:S(2)}) collective-permute-start(f32[1,1600]{1,0:T(1,128)S(1)} %add.58.first), channel_id=1, source_target_pairs={{0,16},{1,17},{2,18},{3,19},{4,20},{5,21},{6,22},{7,23},{8,24},{9,... | collective-permute-start | bytes 19208 | tf_op jit(solution)/shard_map/ppermute | solution.py:292
  46.0 0.8 dynamic_slice.3
  46.8 0.0 copy-done.4
  46.8 0.0 copy-done.5
  46.8 1.2 %tables.1 = (bf16[256,4096]{1,0:T(8,128)(2,1)S(1)}, bf16[16,4096]{1,0:T(8,128)(2,1)S(1)}, f32[56,1600]{1,0:T(8,128)S(1)}, f32[120,1600]{1,0:T(8,128)S(1)}, f32[1,1600]{1,0:T(1,128)S(1)}) custom-call(s32[1]{0:T(128)} %bitcast.4.me, f32[18]{0:T(128)S(1)} %copy-done.4, s32[1,4096]{1,0:T(1,128)S(1)} %bitcast.11, s32[1,1600]{1,0:T(1,128)S(1)} %broadcast_in_dim.13.bucket, ...), custom_call_target="tpu_custom_call" | custom-call | flops 10000000 | bytes 65536 | tf_op jit(solution)/shard_map/tables/pallas_call | solution.py:320
  48.0 0.0 collective-permute-done.2.second
  48.0 0.4 weights.1
  48.4 0.0 collective-permute-start.3
  48.4 1.2 %collective-permute-done.3 = f32[24,128]{1,0:T(8,128)S(1)} collective-permute-done((f32[24,128]{1,0:T(8,128)S(1)}, f32[24,128]{1,0:T(8,128)S(1)}, u32[]{:S(2)}, u32[]{:S(2)}) %collective-permute-start.3) | collective-permute-done | bytes 12320 | tf_op jit(solution)/shard_map/ppermute | solution.py:292
  49.6 1.5 %collective-permute-start.4 = (f32[24,128]{1,0:T(8,128)S(1)}, f32[24,128]{1,0:T(8,128)S(1)}, u32[]{:S(2)}, u32[]{:S(2)}) collective-permute-start(f32[24,128]{1,0:T(8,128)S(1)} %add.62.sums), channel_id=1, source_target_pairs={{0,2},{1,3},{2,0},{3,1},{4,6},{5,7},{6,4},{7,5},{8,10},{9,11},{10,... | collective-permute-start | bytes 36872 | tf_op jit(solution)/shard_map/ppermute | solution.py:292
  51.1 0.0 copy-start.2
  51.1 4.9 %copy-done.2 = bf16[4096,1600]{1,0:T(8,128)(2,1)S(1)} copy-done((bf16[4096,1600]{1,0:T(8,128)(2,1)S(1)}, bf16[4096,1600]{1,0:T(8,128)(2,1)}, u32[]{:S(2)}) %copy-start.2) | copy-done | bytes 13107224
  56.0 4.4 %spread.1 = (f32[56,4096]{1,0:T(8,128)S(1)}, f32[120,4096]{1,0:T(8,128)S(1)}) custom-call(bf16[216,1600]{1,0:T(8,128)(2,1)S(1)} %get-tuple-element.51.spread, bf16[4096,1600]{1,0:T(8,128)(2,1)S(1)} %copy-done.2), custom_call_target="tpu_custom_call" | custom-call | flops 2831155200 | bytes 65536 | tf_op jit(solution)/shard_map/spread/pallas_call | solution.py:350
  60.3 0.0 collective-permute-done.4.more
  60.3 3.0 %nodes.1 = (f32[56,4096]{1,0:T(8,128)S(1)}, f32[24,128]{1,0:T(8,128)S(1)}, f32[16,54,128]{2,1,0:T(8,128)S(1)}, f32[16,54,128]{2,1,0:T(8,128)S(1)}) custom-call(s32[8]{0:T(128)S(1)} %copy-done.3, f32[24,128]{1,0:T(8,128)S(1)} %add.62.sums, f32[24,128]{1,0:T(8,128)S(1)} %collective-permute-done.4.more, f32[56,4096]{1,0:T(8,128)S(1)} %get-tuple-element.53.near, ...), custom_call_target="tpu_custom_call" | custom-call | flops 2147483648 | bytes 65536 | tf_op jit(solution)/shard_map/nodes/pallas_call | solution.py:365
  63.4 0.1 collective-permute-start.7
  63.5 0.1 copy.13
  63.6 0.0 copy-done.6
  63.6 0.1 copy.14
  63.7 1.6 %collective-permute-done.7 = f32[16,54,128]{2,1,0:T(8,128)S(1)} collective-permute-done((f32[16,54,128]{2,1,0:T(8,128)S(1)}, f32[16,54,128]{2,1,0:T(8,128)S(1)}, u32[]{:S(2)}, u32[]{:S(2)}) %collective-permute-start.7) | collective-permute-done | bytes 442400 | tf_op jit(solution)/shard_map/ppermute | solution.py:292
  65.4 0.6 collective-permute-start.8
  66.0 0.0 copy-done.7
  66.0 5.5 %collective-permute-done.8 = f32[8,54,128]{2,1,0:T(8,128)S(1)} collective-permute-done((f32[8,54,128]{2,1,0:T(8,128)S(1)}, f32[8,54,128]{2,1,0:T(8,128)S(1)}, u32[]{:S(2)}, u32[]{:S(2)}) %collective-permute-start.8) | collective-permute-done | bytes 221216 | tf_op jit(solution)/shard_map/ppermute | solution.py:292
  71.5 1.6 %collective-permute-start.9 = (f32[4,54,128]{2,1,0:T(8,128)S(1)}, f32[4,54,128]{2,1,0:T(8,128)S(1)}, u32[]{:S(2)}, u32[]{:S(2)}) collective-permute-start(f32[4,54,128]{2,1,0:T(8,128)S(1)} %slice.88), channel_id=1, source_target_pairs={{0,4},{1,9},{2,6},{3,11},{4,0},{5,13},{6,2},{7,15},{8,12},{9,1},{1... | collective-permute-start | bytes 331784 | tf_op jit(solution)/shard_map/ppermute | solution.py:292
  73.1 0.6 fusion.2
  73.7 1.7 %scatter.9.terms = f32[24,128]{1,0:T(8,128)S(1)} dynamic-update-slice(f32[24,128]{1,0:T(8,128)S(1)} %scatter.6, f32[18,1]{1,0:T(8,128)S(1)} %copy.14, s32[]{:T(128)} %bitcast.2, s32[]{:T(128)} %bitcast.3) | dynamic-update-slice | bytes 148 | tf_op jit(solution)/shard_map/scatter | solution.py:308
  75.4 1.5 %capital.1 = (f32[2,3,1024]{2,1,0:T(4,128)S(1)}, f32[2,3,1024]{2,1,0:T(4,128)S(1)}, f32[3,54,128]{2,1,0:T(8,128)S(1)}, f32[8,128]{1,0:T(8,128)S(1)}) custom-call(s32[4]{0:T(128)S(1)} %broadcast_xor_fusion.place, f32[24,128]{1,0:T(8,128)S(1)} %scatter.9.terms, f32[24,128]{1,0:T(8,128)S(1)} %get-tuple-element.57.total, f32[56,4096]{1,0:T(8,128)S(1)} %get-tuple-element.58.alloc), custom_call_target="tpu_custom_call" | custom-call | flops 10000000 | bytes 65536 | tf_op jit(solution)/shard_map/capital/pallas_call | solution.py:382
  76.8 0.1 collective-permute-start.5
  76.9 0.0 collective-permute-done.9
  77.0 1.6 %collective-permute-start.10 = (f32[2,54,128]{2,1,0:T(8,128)S(1)}, f32[2,54,128]{2,1,0:T(8,128)S(1)}, u32[]{:S(2)}, u32[]{:S(2)}) collective-permute-start(f32[2,54,128]{2,1,0:T(8,128)S(1)} %slice.90), channel_id=1, source_target_pairs={{0,8},{1,3},{2,10},{3,1},{4,12},{5,7},{6,14},{7,5},{8,0},{9,11},{1... | collective-permute-start | bytes 165896 | tf_op jit(solution)/shard_map/ppermute | solution.py:292
  78.6 0.6 multiply_reduce_fusion
  79.2 0.0 collective-permute-done.5
  79.3 0.6 collective-permute-start.6
  79.9 1.3 %collective-permute-done.10 = f32[2,54,128]{2,1,0:T(8,128)S(1)} collective-permute-done((f32[2,54,128]{2,1,0:T(8,128)S(1)}, f32[2,54,128]{2,1,0:T(8,128)S(1)}, u32[]{:S(2)}, u32[]{:S(2)}) %collective-permute-start.10) | collective-permute-done | bytes 55328 | tf_op jit(solution)/shard_map/ppermute | solution.py:292
  81.2 2.6 %collective-permute-start.11 = (f32[1,54,128]{2,1,0:T(8,128)S(1)}, f32[1,54,128]{2,1,0:T(8,128)S(1)}, u32[]{:S(2)}, u32[]{:S(2)}) collective-permute-start(f32[1,54,128]{2,1,0:T(8,128)S(1)} %slice.92), channel_id=1, source_target_pairs={{0,16},{1,17},{2,18},{3,19},{4,20},{5,21},{6,22},{7,23},{8,24},{9,... | collective-permute-start | bytes 82952 | tf_op jit(solution)/shard_map/ppermute | solution.py:292
  83.8 0.0 collective-permute-done.6
  83.8 0.6 fusion.1
  84.4 1.6 %collective-permute-done.11 = f32[1,54,128]{2,1,0:T(8,128)S(1)} collective-permute-done((f32[1,54,128]{2,1,0:T(8,128)S(1)}, f32[1,54,128]{2,1,0:T(8,128)S(1)}, u32[]{:S(2)}, u32[]{:S(2)}) %collective-permute-start.11) | collective-permute-done | bytes 27680 | tf_op jit(solution)/shard_map/ppermute | solution.py:292
  86.1 0.6 reduce_sum.9
  (21 shorter events, 0.2 us)
Async XLA Ops:
  0.6 17.9 %copy-start.3 = (s32[8]{0:T(128)S(1)}, s32[8]{0:T(128)}, u32[]{:S(2)}) copy-start(s32[8]{0:T(128)} %count.3) | copy-start | bytes 100
  18.5 4.9 %copy-start = (bf16[4096,1600]{1,0:T(8,128)(2,1)S(1)}, bf16[4096,1600]{1,0:T(8,128)(2,1)}, u32[]{:S(2)}) copy-start(bf16[4096,1600]{1,0:T(8,128)(2,1)} %copy.15.sens) | copy-start | bytes 39321604
  23.4 23.4 %copy-start.4 = (f32[18]{0:T(128)S(1)}, f32[18]{0:T(128)}, u32[]{:S(2)}) copy-start(f32[18]{0:T(128)} %weight.1) | copy-start | bytes 220
  23.4 23.4 %copy-start.5 = (s32[4096]{0:T(1024)S(1)}, s32[4096]{0:T(1024)}, u32[]{:S(2)}) copy-start(s32[4096]{0:T(1024)} %param.13) | copy-start | bytes 49156
  29.6 4.9 %copy-start.1 = (bf16[4096,1600]{1,0:T(8,128)(2,1)}, bf16[4096,1600]{1,0:T(8,128)(2,1)S(1)}, u32[]{:S(2)}) copy-start(bf16[4096,1600]{1,0:T(8,128)(2,1)S(1)} %get-tuple-element.52.held) | copy-start | bytes 39321604
  34.5 29.1 %copy-start.6 = (f32[18]{0:T(128)S(1)}, f32[18]{0:T(128)}, u32[]{:S(2)}) copy-start(f32[18]{0:T(128)} %param.16) | copy-start | bytes 220
  34.5 31.5 %copy-start.7 = (s32[4]{0:T(128)S(1)}, s32[4]{0:T(128)}, u32[]{:S(2)}) copy-start(s32[4]{0:T(128)} %constant.83.clone) | copy-start | bytes 52
  34.5 4.6 %collective-permute-start = (f32[1,1600]{1,0:T(1,128)S(1)}, f32[1,1600]{1,0:T(1,128)S(1)}, u32[]{:S(2)}, u32[]{:S(2)}) collective-permute-start(f32[1,1600]{1,0:T(1,128)S(1)} %get-tuple-element.46), channel_id=1, source_target_pairs={{0,4},{1,5},{2,6},{3,7},{4,0},{5,1},{6,2},{7,3},{8,12},{9,13},{10,... | collective-permute-start | bytes 19208 | tf_op jit(solution)/shard_map/ppermute | solution.py:292
  39.1 3.8 %collective-permute-start.1 = (f32[1,1600]{1,0:T(1,128)S(1)}, f32[1,1600]{1,0:T(1,128)S(1)}, u32[]{:S(2)}, u32[]{:S(2)}) collective-permute-start(f32[1,1600]{1,0:T(1,128)S(1)} %add.57), channel_id=1, source_target_pairs={{0,8},{1,9},{2,10},{3,11},{4,12},{5,13},{6,14},{7,15},{8,0},{9,1},... | collective-permute-start | bytes 19208 | tf_op jit(solution)/shard_map/ppermute | solution.py:292
  42.9 5.1 %collective-permute-start.2 = (f32[1,1600]{1,0:T(1,128)S(1)}, f32[1,1600]{1,0:T(1,128)S(1)}, u32[]{:S(2)}, u32[]{:S(2)}) collective-permute-start(f32[1,1600]{1,0:T(1,128)S(1)} %add.58.first), channel_id=1, source_target_pairs={{0,16},{1,17},{2,18},{3,19},{4,20},{5,21},{6,22},{7,23},{8,24},{9,... | collective-permute-start | bytes 19208 | tf_op jit(solution)/shard_map/ppermute | solution.py:292
  48.4 1.2 %collective-permute-start.3 = (f32[24,128]{1,0:T(8,128)S(1)}, f32[24,128]{1,0:T(8,128)S(1)}, u32[]{:S(2)}, u32[]{:S(2)}) collective-permute-start(f32[24,128]{1,0:T(8,128)S(1)} %get-tuple-element.50), channel_id=1, source_target_pairs={{0,1},{1,0},{2,3},{3,2},{4,5},{5,4},{6,7},{7,6},{8,9},{9,8},{10,11... | collective-permute-start | bytes 36872 | tf_op jit(solution)/shard_map/ppermute | solution.py:292
  49.6 10.7 %collective-permute-start.4 = (f32[24,128]{1,0:T(8,128)S(1)}, f32[24,128]{1,0:T(8,128)S(1)}, u32[]{:S(2)}, u32[]{:S(2)}) collective-permute-start(f32[24,128]{1,0:T(8,128)S(1)} %add.62.sums), channel_id=1, source_target_pairs={{0,2},{1,3},{2,0},{3,1},{4,6},{5,7},{6,4},{7,5},{8,10},{9,11},{10,... | collective-permute-start | bytes 36872 | tf_op jit(solution)/shard_map/ppermute | solution.py:292
  51.1 4.9 %copy-start.2 = (bf16[4096,1600]{1,0:T(8,128)(2,1)S(1)}, bf16[4096,1600]{1,0:T(8,128)(2,1)}, u32[]{:S(2)}) copy-start(bf16[4096,1600]{1,0:T(8,128)(2,1)} %copy-done.1) | copy-start | bytes 39321604
  63.4 1.9 %collective-permute-start.7 = (f32[16,54,128]{2,1,0:T(8,128)S(1)}, f32[16,54,128]{2,1,0:T(8,128)S(1)}, u32[]{:S(2)}, u32[]{:S(2)}) collective-permute-start(f32[16,54,128]{2,1,0:T(8,128)S(1)} %get-tuple-element.64), channel_id=1, source_target_pairs={{0,1},{1,0},{2,3},{3,2},{4,5},{5,4},{6,7},{7,6},{8,9},{9,8},{10,11... | collective-permute-start | bytes 1327112 | tf_op jit(solution)/shard_map/ppermute | solution.py:292
  65.4 6.1 %collective-permute-start.8 = (f32[8,54,128]{2,1,0:T(8,128)S(1)}, f32[8,54,128]{2,1,0:T(8,128)S(1)}, u32[]{:S(2)}, u32[]{:S(2)}) collective-permute-start(f32[8,54,128]{2,1,0:T(8,128)S(1)} %slice.86), channel_id=1, source_target_pairs={{0,2},{1,5},{2,0},{3,7},{4,6},{5,1},{6,4},{7,3},{8,10},{9,13},{10,... | collective-permute-start | bytes 663560 | tf_op jit(solution)/shard_map/ppermute | solution.py:292
  71.5 5.4 %collective-permute-start.9 = (f32[4,54,128]{2,1,0:T(8,128)S(1)}, f32[4,54,128]{2,1,0:T(8,128)S(1)}, u32[]{:S(2)}, u32[]{:S(2)}) collective-permute-start(f32[4,54,128]{2,1,0:T(8,128)S(1)} %slice.88), channel_id=1, source_target_pairs={{0,4},{1,9},{2,6},{3,11},{4,0},{5,13},{6,2},{7,15},{8,12},{9,1},{1... | collective-permute-start | bytes 331784 | tf_op jit(solution)/shard_map/ppermute | solution.py:292
  76.8 2.4 %collective-permute-start.5 = (f32[2,3,1024]{2,1,0:T(4,128)S(1)}, f32[2,3,1024]{2,1,0:T(4,128)S(1)}, u32[]{:S(2)}, u32[]{:S(2)}) collective-permute-start(f32[2,3,1024]{2,1,0:T(4,128)S(1)} %get-tuple-element.61), channel_id=1, source_target_pairs={{0,1},{1,0},{2,3},{3,2},{4,5},{5,4},{6,7},{7,6},{8,9},{9,8},{10,11... | collective-permute-start | bytes 73736 | tf_op jit(solution)/shard_map/ppermute | solution.py:292
  77.0 4.2 %collective-permute-start.10 = (f32[2,54,128]{2,1,0:T(8,128)S(1)}, f32[2,54,128]{2,1,0:T(8,128)S(1)}, u32[]{:S(2)}, u32[]{:S(2)}) collective-permute-start(f32[2,54,128]{2,1,0:T(8,128)S(1)} %slice.90), channel_id=1, source_target_pairs={{0,8},{1,3},{2,10},{3,1},{4,12},{5,7},{6,14},{7,5},{8,0},{9,11},{1... | collective-permute-start | bytes 165896 | tf_op jit(solution)/shard_map/ppermute | solution.py:292
  79.3 4.5 %collective-permute-start.6 = (f32[1,3,1024]{2,1,0:T(4,128)S(1)}, f32[1,3,1024]{2,1,0:T(4,128)S(1)}, u32[]{:S(2)}, u32[]{:S(2)}) collective-permute-start(f32[1,3,1024]{2,1,0:T(4,128)S(1)} %slice.84), channel_id=1, source_target_pairs={{0,2},{1,3},{2,0},{3,1},{4,6},{5,7},{6,4},{7,5},{8,10},{9,11},{10,... | collective-permute-start | bytes 36872 | tf_op jit(solution)/shard_map/ppermute | solution.py:292
  81.2 4.8 %collective-permute-start.11 = (f32[1,54,128]{2,1,0:T(8,128)S(1)}, f32[1,54,128]{2,1,0:T(8,128)S(1)}, u32[]{:S(2)}, u32[]{:S(2)}) collective-permute-start(f32[1,54,128]{2,1,0:T(8,128)S(1)} %slice.92), channel_id=1, source_target_pairs={{0,16},{1,17},{2,18},{3,19},{4,20},{5,21},{6,22},{7,23},{8,24},{9,... | collective-permute-start | bytes 82952 | tf_op jit(solution)/shard_map/ppermute | solution.py:292

commit v2 on v1

--- a/solution.py
+++ b/solution.py
@@ -14,6 +14,7 @@
 NODES = 4096
 BLOCK = 512
 ROWS = 3 * BUCKETS
+PIECE = 160
 LOW = 256
 HIGH = NODES // LOW
 AXES = ("trade", "factor")
@@ -36,7 +37,7 @@
     return jax.ShapeDtypeStruct(dims, dtype)
 
 
-def call(kernel, out_shape, in_specs, out_specs, name, scratch=(), flops=0, limit=24):
+def call(kernel, out_shape, in_specs, out_specs, name, scratch=(), flops=0, limit=12):
     return pl.pallas_call(
         kernel,
         out_shape=out_shape,
@@ -49,30 +50,57 @@
     )
 
 
+def dot(a, b):
+    return lax.dot_general(a, b, (((1,), (0,)), ((), ())), preferred_element_type=f32)
+
+
 def dot_t(a, b):
     return lax.dot_general(a, b, (((1,), (1,)), ((), ())), preferred_element_type=f32)
 
 
-def totals_kernel(count, sens, held, raw, sems):
-    blocks = count.shape[0]
-    width = sens.shape[1]
-    copies = []
-    for i in range(blocks):
-        part = pl.ds(i * BLOCK, BLOCK)
-        copies.append(pltpu.make_async_copy(sens.at[part], held.at[part], sems.at[i]))
-        copies[-1].start()
-    row = lax.broadcasted_iota(jnp.int32, (16, width), 0)
-    total = jnp.zeros((16, width), f32)
-    for i in range(blocks):
-        copies[i].wait()
-        live = count[i]
-
-        def step(g, total):
-            part = held[pl.ds(pl.multiple_of(i * BLOCK + g * 16, 16), 16), :].astype(f32)
-            return total + jnp.where(row < live - g * 16, part, 0.0)
-
-        total = lax.fori_loop(0, BLOCK // 16, step, total, unroll=4)
-    raw[...] = jnp.sum(total, 0, keepdims=True)
+def totals_kernel(count, sens, held, raw, partial, sems):
+    width, trades = sens.shape
+    pieces = width // PIECE
+    lanes = 128
+
+    def copy(i):
+        part = pl.ds(pl.multiple_of(i * PIECE, PIECE), PIECE)
+        return pltpu.make_async_copy(sens.at[part], held.at[part], sems.at[i])
+
+    for i in range(pieces):
+        copy(i).start()
+
+    def run(tiles):
+        def piece(i, carry):
+            copy(i).wait()
+            rows = pl.ds(pl.multiple_of(i * PIECE, PIECE), PIECE)
+            total = jnp.zeros((PIECE, lanes), f32)
+            for start, live in tiles:
+                part = held[rows, start : start + lanes].astype(f32)
+                total = total + (part if live is None else jnp.where(live, part, 0.0))
+            partial[rows, :] = total
+            return carry
+
+        lax.fori_loop(0, pieces, piece, 0)
+
+    full = count[0] == BLOCK
+
+    @pl.when(full)
+    def _():
+        run([(start, None) for start in range(0, trades, lanes)])
+
+    @pl.when(jnp.logical_not(full))
+    def _():
+        slot = lax.broadcasted_iota(jnp.int32, (PIECE, lanes), 1)
+        run([(i * BLOCK, slot < count[i]) for i in range(trades // BLOCK)])
+
+    value = partial[...]
+    upper = value.astype(bf16)
+    value = value - upper.astype(f32)
+    middle = value.astype(bf16)
+    lower = (value - middle.astype(f32)).astype(bf16)
+    ones = jnp.ones((16, 3 * lanes), bf16)
+    raw[...] = dot_t(ones, jnp.concatenate([upper, middle, lower], 1))[:1]
 
 
 def tables_kernel(
@@ -139,10 +167,9 @@
     value = jnp.where(row < BUCKETS, near, jnp.where(row < 2 * BUCKETS, weighted, 1.0))
     full = spread_hot[...] * value
     upper = full.astype(bf16)
-    lower = (full[:40] - upper[:40].astype(f32)).astype(bf16)
-    spread[...] = jnp.concatenate(
-        [upper.astype(f32), tenor_hot[...], lower.astype(f32)], 0
-    ).astype(bf16)
+    lower = full[:40] - upper[:40].astype(f32)
+    fill = jnp.zeros((32, width), f32)
+    spread[...] = jnp.concatenate([upper.astype(f32), lower, fill], 0).astype(bf16)
     lane = lax.broadcasted_iota(jnp.int32, (24, 128), 1)
     out = jnp.zeros((24, 128), f32)
     square = jnp.zeros((24, 1), f32)
@@ -158,13 +185,20 @@
     sums[...] = out
 
 
-def spread_kernel(spread, held, near, tenors):
-    trades = held.shape[0]
+def ones_kernel(tenor_hot, held, tenors):
+    trades = held.shape[1]
+    hot = jnp.concatenate([tenor_hot[...], jnp.zeros((8, held.shape[0]), f32)], 0).astype(bf16)
     for start in range(0, trades, BLOCK):
         part = pl.ds(start, BLOCK)
-        out = dot_t(spread[...], held[part, :])
-        near[:, part] = jnp.concatenate([out[:40] + out[176:216], out[40:56]], 0)
-        tenors[:, part] = out[56:176]
+        tenors[:, part] = dot(hot, held[:, part])[: 24 * TENORS]
+
+
+def spread_kernel(spread, held, near):
+    trades = held.shape[1]
+    for start in range(0, trades, BLOCK):
+        part = pl.ds(start, BLOCK)
+        out = dot(spread[...], held[:, part])
+        near[:, part] = jnp.concatenate([out[:40] + out[56:96], out[40:56]], 0)
 
 
 def nodes_kernel(
@@ -199,14 +233,18 @@
             send[h + j] = out[64 * j : 64 * j + ROWS, LOW // 2 :]
 
 
-def capital_kernel(place, terms, total, alloc, keep, send, mix, capital, *, trades_total):
+def capital_kernel(place, weight, load, total, alloc, keep, send, mix, capital, *, trades_total):
     parts = 2 * keep.shape[0]
     length = keep.shape[2]
     gather = total[...]
     lane = lax.broadcasted_iota(jnp.int32, (24, 128), 1)
-    real = lax.broadcasted_iota(jnp.int32, (24, 1), 0) < BUCKETS
-    risk = terms[:, 0:1]
-    loading = terms[:, 1:2]
+    row = lax.broadcasted_iota(jnp.int32, (24, 1), 0)
+    risk = jnp.zeros((24, 1), f32)
+    loading = jnp.zeros((24, 1), f32)
+    for b in range(BUCKETS):
+        risk = jnp.where(row == b, weight[b], risk)
+        loading = jnp.where(row == b, load[b], loading)
+    real = row < BUCKETS
     tenor_part = jnp.where(lane < TENORS, gather, 0.0)
     sums = jnp.sum(tenor_part, 1, keepdims=True)
     tenor_square = jnp.sum(tenor_part * tenor_part, 1, keepdims=True)
@@ -304,18 +342,17 @@
     ) ^ f.astype(jnp.int32)
     bucket = lax.dynamic_slice_in_dim(factor_bucket, f * width, width, 0)[None, :]
     tenor = (jnp.arange(width, dtype=jnp.int32) % TENORS)[None, :]
-    terms = jnp.zeros((24, 128), f32)
-    terms = terms.at[:BUCKETS, 0].set(risk_weight).at[:BUCKETS, 1].set(bucket_loading)
-
+
+    by_factor = pltpu.with_memory_space_constraint(sensitivity.T, pltpu.HBM)
     held, raw = call(
         totals_kernel,
-        (pltpu.VMEM(sensitivity.shape, bf16), shape(1, width)),
+        (pltpu.VMEM((width, trade_rows), bf16), shape(1, width)),
         [SMEM, ANY],
         (VMEM, VMEM),
         "totals",
-        scratch=[pltpu.SemaphoreType.DMA((block_count.shape[0],))],
+        scratch=[pltpu.VMEM((width, 128), f32), pltpu.SemaphoreType.DMA((width // PIECE,))],
         flops=10**7,
-    )(block_count, sensitivity)
+    )(block_count, by_factor)
 
     low_hot, high_hot, spread_hot, tenor_hot, factor_weight = call(
         functools.partial(tables_kernel, spots=spots),
@@ -340,20 +377,29 @@
 
     spread, sums = call(
         weights_kernel,
-        (pltpu.VMEM((216, width), bf16), shape(24, 128)),
+        (pltpu.VMEM((128, width), bf16), shape(24, 128)),
         [VMEM] * 6,
         (VMEM, VMEM),
         "weights",
         flops=10**6,
     )(raw, other, factor_weight, tenor, spread_hot, tenor_hot)
 
-    near, tenors = call(
+    tenors = call(
+        ones_kernel,
+        pltpu.VMEM((24 * TENORS, trade_rows), f32),
+        [VMEM, VMEM],
+        VMEM,
+        "ones",
+        flops=2 * 128 * width * trade_rows,
+    )(tenor_hot, held)
+
+    near = call(
         spread_kernel,
-        (pltpu.VMEM((56, trade_rows), f32), pltpu.VMEM((24 * TENORS, trade_rows), f32)),
+        pltpu.VMEM((56, trade_rows), f32),
         [VMEM, VMEM],
-        (VMEM, VMEM),
+        VMEM,
         "spread",
-        flops=2 * 216 * width * trade_rows,
+        flops=2 * 128 * width * trade_rows,
     )(spread, held)
 
     more = None
@@ -375,7 +421,6 @@
         "nodes",
         scratch=[pltpu.VMEM((64, trade_rows), bf16)],
         flops=2 * 1024 * trade_rows * LOW,
-        limit=40,
     )(block_count, sums, more, near, tenors, low_hot, high_hot)
 
     length = trade_rows // factor_size
@@ -387,11 +432,11 @@
             shape(SCEN, ROWS, 128),
             shape(8, 128),
         ),
-        [SMEM, VMEM, VMEM, VMEM],
+        [SMEM, SMEM, SMEM, VMEM, VMEM],
         (VMEM,) * 4,
         "capital",
         flops=10**7,
-    )(block_order, terms, total, alloc)
+    )(block_order, risk_weight, bucket_loading, total, alloc)
 
     keep = keep + exchange(send, lambda o: 0)
     for i in range(bits - 1):

time: 87.4 us -> 62.6 us (0.72)
  local copies, waits for them, and re-layouts: 35.9 us -> 11 us
  starting transfers between devices: 16.9 us -> 19.2 us
  waiting for transfers between devices: 14.5 us -> 13.6 us
    unnamed x17 -> x16, local copies, waits for them, and re-layouts: 32.6 us -> 10.1 us
    ppermute x12, starting transfers between devices: 16.9 us -> 19.2 us  [exchange(): return lax.ppermute(x, AXES, pairs)]
    scatter x2 -> x0, local copies, waits for them, and re-layouts: 1.7 us -> none  [local(): terms.at[:BUCKETS, 0].set(risk_weight).at[:BUCKETS, 1].set(bucket_loading)]
    pallas_call x3 -> x4, Pallas kernels: 10.9 us -> 10.5 us  [the longest x1 5.9 us: local(): call(totals_kernel, (pltpu.VMEM((width, trade_rows), bf16), shape(1, widt...]
  transfers between devices with their start and end apart: 12 -> 12, of which waited for: 7 -> 8; matrix products, arithmetic and copies ran while one was open for 5% -> 3% of each run, Pallas kernels for 8% -> 10%
where the time goes in v2:
time: 62.6 us; the launch traced here: 62.4 us
  starting transfers between devices  19.2 us (31%)
  Pallas kernels  15.8 us (25%)
  waiting for transfers between devices  13.6 us (22%)
  local copies, waits for them, and re-layouts  11 us (18%)
  other arithmetic  2.06 us (3%)
  between operations  0.87 us (1%)
    ppermute x12, starting transfers between devices, exchange(): return lax.ppermute(x, AXES, pairs)  19.2 us
    ppermute x12, waiting for transfers between devices, exchange(): return lax.ppermute(x, AXES, pairs)  13.6 us
    unnamed x16, local copies, waits for them, and re-layouts  10.1 us
    pallas_call x1, Pallas kernels, local(): call(totals_kernel, (pltpu.VMEM((width, trade_rows), bf16), shape(1, widt...  5.9 us
    pallas_call x1, Pallas kernels, local(): call(nodes_kernel, (pltpu.VMEM((56, trade_rows), f32), shape(24, 128), sh...  3.04 us
    pallas_call x1, Pallas kernels, local(): call(ones_kernel, pltpu.VMEM((24 * TENORS, trade_rows), f32), [VMEM, VMEM...  2.09 us
    pallas_call x1, Pallas kernels, local(): call(spread_kernel, pltpu.VMEM((56, trade_rows), f32), [VMEM, VMEM], VMEM...  2.08 us
  transfers between devices with their start and end apart: 12, of which 8 were waited for; matrix products, arithmetic and copies ran while one was open for 3% of the time, Pallas kernels for 10%

profile of v2, /device:TPU:0, one launch (start us, length us, event | category | flops | bytes accessed | tf_op | source)
XLA Modules:
  0.0 62.4 jit_solution(1530068168130145384)
XLA Ops:
  0.6 0.0 copy-start.4
  0.6 0.0 copy-start.2
  0.7 0.7 %copy-done.2 = s32[8]{0:T(128)S(1)} copy-done((s32[8]{0:T(128)S(1)}, s32[8]{0:T(128)}, u32[]{:S(2)}) %copy-start.2) | copy-done | bytes 56
  1.3 0.0 copy-start.6
  1.3 5.9 %totals.1 = (bf16[1600,4096]{1,0:T(8,128)(2,1)S(1)}, f32[1,1600]{1,0:T(1,128)S(1)}) custom-call(s32[8]{0:T(128)S(1)} %copy-done.2, bf16[1600,4096]{1,0:T(8,128)(2,1)} %bitcast.8), custom_call_target="tpu_custom_call" | custom-call | flops 10000000 | bytes 65536 | tf_op jit(solution)/shard_map/totals/pallas_call | solution.py:347
  7.2 0.0 copy-start
  7.2 4.7 %copy-done = bf16[1600,4096]{1,0:T(8,128)(2,1)} copy-done((bf16[1600,4096]{1,0:T(8,128)(2,1)}, bf16[1600,4096]{1,0:T(8,128)(2,1)S(1)}, u32[]{:S(2)}) %copy-start) | copy-done | bytes 13107224
  11.9 3.0 %collective-permute-start = (f32[1,1600]{1,0:T(1,128)S(1)}, f32[1,1600]{1,0:T(1,128)S(1)}, u32[]{:S(2)}, u32[]{:S(2)}) collective-permute-start(f32[1,1600]{1,0:T(1,128)S(1)} %get-tuple-element.20), channel_id=1, source_target_pairs={{0,4},{1,5},{2,6},{3,7},{4,0},{5,1},{6,2},{7,3},{8,12},{9,13},{10,... | collective-permute-start | bytes 19208 | tf_op jit(solution)/shard_map/ppermute | solution.py:330
  14.9 1.6 %collective-permute-done = f32[1,1600]{1,0:T(1,128)S(1)} collective-permute-done((f32[1,1600]{1,0:T(1,128)S(1)}, f32[1,1600]{1,0:T(1,128)S(1)}, u32[]{:S(2)}, u32[]{:S(2)}) %collective-permute-start) | collective-permute-done | bytes 6432 | tf_op jit(solution)/shard_map/ppermute | solution.py:330
  16.5 2.1 %collective-permute-start.1 = (f32[1,1600]{1,0:T(1,128)S(1)}, f32[1,1600]{1,0:T(1,128)S(1)}, u32[]{:S(2)}, u32[]{:S(2)}) collective-permute-start(f32[1,1600]{1,0:T(1,128)S(1)} %add.51), channel_id=1, source_target_pairs={{0,8},{1,9},{2,10},{3,11},{4,12},{5,13},{6,14},{7,15},{8,0},{9,1},... | collective-permute-start | bytes 19208 | tf_op jit(solution)/shard_map/ppermute | solution.py:330
  18.7 1.6 %collective-permute-done.1 = f32[1,1600]{1,0:T(1,128)S(1)} collective-permute-done((f32[1,1600]{1,0:T(1,128)S(1)}, f32[1,1600]{1,0:T(1,128)S(1)}, u32[]{:S(2)}, u32[]{:S(2)}) %collective-permute-start.1) | collective-permute-done | bytes 6432 | tf_op jit(solution)/shard_map/ppermute | solution.py:330
  20.3 3.2 %collective-permute-start.2 = (f32[1,1600]{1,0:T(1,128)S(1)}, f32[1,1600]{1,0:T(1,128)S(1)}, u32[]{:S(2)}, u32[]{:S(2)}) collective-permute-start(f32[1,1600]{1,0:T(1,128)S(1)} %add.52.first), channel_id=1, source_target_pairs={{0,16},{1,17},{2,18},{3,19},{4,20},{5,21},{6,22},{7,23},{8,24},{9,... | collective-permute-start | bytes 19208 | tf_op jit(solution)/shard_map/ppermute | solution.py:330
  23.6 0.8 %dynamic_slice.3 = s32[1600]{0:T(1024)S(1)} dynamic-slice(s32[6400]{0:T(1024)} %param.10, s32[]{:T(128)S(6)} %select_n.19), dynamic_slice_sizes={1600} | dynamic-slice | bytes 12804 | tf_op jit(solution)/shard_map/dynamic_slice | solution.py:343
  24.4 0.0 copy-done.4
  24.4 0.0 copy-done.6
  24.4 1.2 %tables.1 = (bf16[256,4096]{1,0:T(8,128)(2,1)S(1)}, bf16[16,4096]{1,0:T(8,128)(2,1)S(1)}, f32[56,1600]{1,0:T(8,128)S(1)}, f32[120,1600]{1,0:T(8,128)S(1)}, f32[1,1600]{1,0:T(1,128)S(1)}) custom-call(s32[1]{0:T(128)} %bitcast.1.me, f32[18]{0:T(128)S(1)} %copy-done.4, s32[1,4096]{1,0:T(1,128)S(1)} %bitcast.7, s32[1,1600]{1,0:T(1,128)S(1)} %broadcast_in_dim.12.bucket, ...), custom_call_target="tpu_custom_call" | custom-call | flops 10000000 | bytes 65536 | tf_op jit(solution)/shard_map/tables/pallas_call | solution.py:357
  25.6 0.0 collective-permute-done.2.second
  25.6 0.4 weights.1
  26.0 0.0 collective-permute-start.3
  26.0 0.0 copy-start.1
  26.0 4.7 %copy-done.1 = bf16[1600,4096]{1,0:T(8,128)(2,1)S(1)} copy-done((bf16[1600,4096]{1,0:T(8,128)(2,1)S(1)}, bf16[1600,4096]{1,0:T(8,128)(2,1)}, u32[]{:S(2)}) %copy-start.1) | copy-done | bytes 13107224
  30.7 0.0 copy-start.3
  30.7 2.1 %ones.1.tenors = f32[120,4096]{1,0:T(8,128)S(1)} custom-call(f32[120,1600]{1,0:T(8,128)S(1)} %get-tuple-element.23.tenor_hot, bf16[1600,4096]{1,0:T(8,128)(2,1)S(1)} %copy-done.1), custom_call_target="tpu_custom_call" | custom-call | flops 1677721600 | bytes 65536 | tf_op jit(solution)/shard_map/ones/pallas_call | solution.py:387
  32.8 0.0 copy-start.7
  32.8 0.0 copy-start.5
  32.9 0.0 collective-permute-done.3
  32.9 1.5 %collective-permute-start.4 = (f32[24,128]{1,0:T(8,128)S(1)}, f32[24,128]{1,0:T(8,128)S(1)}, u32[]{:S(2)}, u32[]{:S(2)}) collective-permute-start(f32[24,128]{1,0:T(8,128)S(1)} %add.56.sums), channel_id=1, source_target_pairs={{0,2},{1,3},{2,0},{3,1},{4,6},{5,7},{6,4},{7,5},{8,10},{9,11},{10,... | collective-permute-start | bytes 36872 | tf_op jit(solution)/shard_map/ppermute | solution.py:330
  34.4 2.1 %spread.1.near = f32[56,4096]{1,0:T(8,128)S(1)} custom-call(bf16[128,1600]{1,0:T(8,128)(2,1)S(1)} %get-tuple-element.25.spread, bf16[1600,4096]{1,0:T(8,128)(2,1)S(1)} %copy-done.1), custom_call_target="tpu_custom_call" | custom-call | flops 1677721600 | bytes 65536 | tf_op jit(solution)/shard_map/spread/pallas_call | solution.py:396
  36.5 0.1 collective-permute-done.4.more
  36.6 0.0 copy-done.3
  36.6 3.0 %nodes.1 = (f32[56,4096]{1,0:T(8,128)S(1)}, f32[24,128]{1,0:T(8,128)S(1)}, f32[16,54,128]{2,1,0:T(8,128)S(1)}, f32[16,54,128]{2,1,0:T(8,128)S(1)}) custom-call(s32[8]{0:T(128)S(1)} %copy-done.3, f32[24,128]{1,0:T(8,128)S(1)} %add.56.sums, f32[24,128]{1,0:T(8,128)S(1)} %collective-permute-done.4.more, f32[56,4096]{1,0:T(8,128)S(1)} %spread.1.near, ...), custom_call_target="tpu_custom_call" | custom-call | flops 2147483648 | bytes 65536 | tf_op jit(solution)/shard_map/nodes/pallas_call | solution.py:411
  39.7 0.2 collective-permute-start.7
  39.9 1.7 %collective-permute-done.7 = f32[16,54,128]{2,1,0:T(8,128)S(1)} collective-permute-done((f32[16,54,128]{2,1,0:T(8,128)S(1)}, f32[16,54,128]{2,1,0:T(8,128)S(1)}, u32[]{:S(2)}, u32[]{:S(2)}) %collective-permute-start.7) | collective-permute-done | bytes 442400 | tf_op jit(solution)/shard_map/ppermute | solution.py:330
  41.6 0.1 add.59
  41.7 1.5 %collective-permute-start.8 = (f32[8,54,128]{2,1,0:T(8,128)S(1)}, f32[8,54,128]{2,1,0:T(8,128)S(1)}, u32[]{:S(2)}, u32[]{:S(2)}) collective-permute-start(f32[8,54,128]{2,1,0:T(8,128)S(1)} %slice.47), channel_id=1, source_target_pairs={{0,2},{1,5},{2,0},{3,7},{4,6},{5,1},{6,4},{7,3},{8,10},{9,13},{10,... | collective-permute-start | bytes 663560 | tf_op jit(solution)/shard_map/ppermute | solution.py:330
  43.2 4.5 %collective-permute-done.8 = f32[8,54,128]{2,1,0:T(8,128)S(1)} collective-permute-done((f32[8,54,128]{2,1,0:T(8,128)S(1)}, f32[8,54,128]{2,1,0:T(8,128)S(1)}, u32[]{:S(2)}, u32[]{:S(2)}) %collective-permute-start.8) | collective-permute-done | bytes 221216 | tf_op jit(solution)/shard_map/ppermute | solution.py:330
  47.8 1.5 %collective-permute-start.9 = (f32[4,54,128]{2,1,0:T(8,128)S(1)}, f32[4,54,128]{2,1,0:T(8,128)S(1)}, u32[]{:S(2)}, u32[]{:S(2)}) collective-permute-start(f32[4,54,128]{2,1,0:T(8,128)S(1)} %slice.49), channel_id=1, source_target_pairs={{0,4},{1,9},{2,6},{3,11},{4,0},{5,13},{6,2},{7,15},{8,12},{9,1},{1... | collective-permute-start | bytes 331784 | tf_op jit(solution)/shard_map/ppermute | solution.py:330
  49.2 0.0 copy-done.7
  49.3 0.0 copy-done.5
  49.3 1.1 %capital.1 = (f32[2,3,1024]{2,1,0:T(4,128)S(1)}, f32[2,3,1024]{2,1,0:T(4,128)S(1)}, f32[3,54,128]{2,1,0:T(8,128)S(1)}, f32[8,128]{1,0:T(8,128)S(1)}) custom-call(s32[4]{0:T(128)S(1)} %broadcast_xor_fusion.place, f32[18]{0:T(128)S(1)} %copy-done.4, f32[18]{0:T(128)S(1)} %copy-done.5, f32[24,128]{1,0:T(8,128)S(1)} %get-tuple-element.29.total, ...), custom_call_target="tpu_custom_call" | custom-call | flops 10000000 | bytes 65536 | tf_op jit(solution)/shard_map/capital/pallas_call | solution.py:427
  50.4 0.1 collective-permute-start.5
  50.5 2.2 %collective-permute-done.9 = f32[4,54,128]{2,1,0:T(8,128)S(1)} collective-permute-done((f32[4,54,128]{2,1,0:T(8,128)S(1)}, f32[4,54,128]{2,1,0:T(8,128)S(1)}, u32[]{:S(2)}, u32[]{:S(2)}) %collective-permute-start.9) | collective-permute-done | bytes 110624 | tf_op jit(solution)/shard_map/ppermute | solution.py:330
  52.7 1.5 %collective-permute-start.10 = (f32[2,54,128]{2,1,0:T(8,128)S(1)}, f32[2,54,128]{2,1,0:T(8,128)S(1)}, u32[]{:S(2)}, u32[]{:S(2)}) collective-permute-start(f32[2,54,128]{2,1,0:T(8,128)S(1)} %slice.51), channel_id=1, source_target_pairs={{0,8},{1,3},{2,10},{3,1},{4,12},{5,7},{6,14},{7,5},{8,0},{9,11},{1... | collective-permute-start | bytes 165896 | tf_op jit(solution)/shard_map/ppermute | solution.py:330
  54.2 0.6 %multiply_reduce_fusion = f32[3]{0:T(128)} fusion(f32[8,128]{1,0:T(8,128)S(1)} %get-tuple-element.31), kind=kLoop, calls=%fused_computation.9 | loop fusion | flops 3 | bytes 24 | tf_op jit(solution)/shard_map/div | solution.py:460
  54.8 0.0 collective-permute-done.5
  54.9 1.6 %collective-permute-start.6 = (f32[1,3,1024]{2,1,0:T(4,128)S(1)}, f32[1,3,1024]{2,1,0:T(4,128)S(1)}, u32[]{:S(2)}, u32[]{:S(2)}) collective-permute-start(f32[1,3,1024]{2,1,0:T(4,128)S(1)} %slice.45), channel_id=1, source_target_pairs={{0,2},{1,3},{2,0},{3,1},{4,6},{5,7},{6,4},{7,5},{8,10},{9,11},{10,... | collective-permute-start | bytes 36872 | tf_op jit(solution)/shard_map/ppermute | solution.py:330
  56.4 0.5 collective-permute-done.10
  57.0 2.9 %collective-permute-start.11 = (f32[1,54,128]{2,1,0:T(8,128)S(1)}, f32[1,54,128]{2,1,0:T(8,128)S(1)}, u32[]{:S(2)}, u32[]{:S(2)}) collective-permute-start(f32[1,54,128]{2,1,0:T(8,128)S(1)} %slice.53), channel_id=1, source_target_pairs={{0,16},{1,17},{2,18},{3,19},{4,20},{5,21},{6,22},{7,23},{8,24},{9,... | collective-permute-start | bytes 82952 | tf_op jit(solution)/shard_map/ppermute | solution.py:330
  59.9 0.0 collective-permute-done.6
  59.9 0.6 fusion.1
  60.5 1.3 %collective-permute-done.11 = f32[1,54,128]{2,1,0:T(8,128)S(1)} collective-permute-done((f32[1,54,128]{2,1,0:T(8,128)S(1)}, f32[1,54,128]{2,1,0:T(8,128)S(1)}, u32[]{:S(2)}, u32[]{:S(2)}) %collective-permute-start.11) | collective-permute-done | bytes 27680 | tf_op jit(solution)/shard_map/ppermute | solution.py:330
  61.8 0.6 %reduce_sum.9 = f32[3,18,128]{2,1,0:T(8,128)} reduce(f32[3,3,18,128]{3,2,1,0:T(8,128)S(1)} %reshape.33, f32[]{:T(128)} %constant.34.clone.1), dimensions={1}, to_apply=%region_0.1 | reduce | flops 13824 | bytes 110596 | tf_op jit(solution)/shard_map/reduce_sum | solution.py:459
  (18 shorter events, 0.2 us)
Async XLA Ops:
  0.6 23.7 %copy-start.4 = (f32[18]{0:T(128)S(1)}, f32[18]{0:T(128)}, u32[]{:S(2)}) copy-start(f32[18]{0:T(128)} %weight.3) | copy-start | bytes 220
  0.6 0.7 %copy-start.2 = (s32[8]{0:T(128)S(1)}, s32[8]{0:T(128)}, u32[]{:S(2)}) copy-start(s32[8]{0:T(128)} %count.3) | copy-start | bytes 100
  1.3 23.1 %copy-start.6 = (s32[4096]{0:T(1024)S(1)}, s32[4096]{0:T(1024)}, u32[]{:S(2)}) copy-start(s32[4096]{0:T(1024)} %param.9) | copy-start | bytes 49156
  7.2 4.7 %copy-start = (bf16[1600,4096]{1,0:T(8,128)(2,1)}, bf16[1600,4096]{1,0:T(8,128)(2,1)S(1)}, u32[]{:S(2)}) copy-start(bf16[1600,4096]{1,0:T(8,128)(2,1)S(1)} %get-tuple-element.26.held) | copy-start | bytes 39321604
  11.9 4.6 %collective-permute-start = (f32[1,1600]{1,0:T(1,128)S(1)}, f32[1,1600]{1,0:T(1,128)S(1)}, u32[]{:S(2)}, u32[]{:S(2)}) collective-permute-start(f32[1,1600]{1,0:T(1,128)S(1)} %get-tuple-element.20), channel_id=1, source_target_pairs={{0,4},{1,5},{2,6},{3,7},{4,0},{5,1},{6,2},{7,3},{8,12},{9,13},{10,... | collective-permute-start | bytes 19208 | tf_op jit(solution)/shard_map/ppermute | solution.py:330
  16.5 3.8 %collective-permute-start.1 = (f32[1,1600]{1,0:T(1,128)S(1)}, f32[1,1600]{1,0:T(1,128)S(1)}, u32[]{:S(2)}, u32[]{:S(2)}) collective-permute-start(f32[1,1600]{1,0:T(1,128)S(1)} %add.51), channel_id=1, source_target_pairs={{0,8},{1,9},{2,10},{3,11},{4,12},{5,13},{6,14},{7,15},{8,0},{9,1},... | collective-permute-start | bytes 19208 | tf_op jit(solution)/shard_map/ppermute | solution.py:330
  20.3 5.3 %collective-permute-start.2 = (f32[1,1600]{1,0:T(1,128)S(1)}, f32[1,1600]{1,0:T(1,128)S(1)}, u32[]{:S(2)}, u32[]{:S(2)}) collective-permute-start(f32[1,1600]{1,0:T(1,128)S(1)} %add.52.first), channel_id=1, source_target_pairs={{0,16},{1,17},{2,18},{3,19},{4,20},{5,21},{6,22},{7,23},{8,24},{9,... | collective-permute-start | bytes 19208 | tf_op jit(solution)/shard_map/ppermute | solution.py:330
  26.0 6.9 %collective-permute-start.3 = (f32[24,128]{1,0:T(8,128)S(1)}, f32[24,128]{1,0:T(8,128)S(1)}, u32[]{:S(2)}, u32[]{:S(2)}) collective-permute-start(f32[24,128]{1,0:T(8,128)S(1)} %get-tuple-element.24), channel_id=1, source_target_pairs={{0,1},{1,0},{2,3},{3,2},{4,5},{5,4},{6,7},{7,6},{8,9},{9,8},{10,11... | collective-permute-start | bytes 36872 | tf_op jit(solution)/shard_map/ppermute | solution.py:330
  26.0 4.7 %copy-start.1 = (bf16[1600,4096]{1,0:T(8,128)(2,1)S(1)}, bf16[1600,4096]{1,0:T(8,128)(2,1)}, u32[]{:S(2)}) copy-start(bf16[1600,4096]{1,0:T(8,128)(2,1)} %copy-done) | copy-start | bytes 39321604
  30.7 5.9 %copy-start.3 = (s32[8]{0:T(128)S(1)}, s32[8]{0:T(128)}, u32[]{:S(2)}) copy-start(s32[8]{0:T(128)} %count.3) | copy-start | bytes 100
  32.8 16.4 %copy-start.7 = (s32[4]{0:T(128)S(1)}, s32[4]{0:T(128)}, u32[]{:S(2)}) copy-start(s32[4]{0:T(128)} %constant.35.clone) | copy-start | bytes 52
  32.8 16.4 %copy-start.5 = (f32[18]{0:T(128)S(1)}, f32[18]{0:T(128)}, u32[]{:S(2)}) copy-start(f32[18]{0:T(128)} %load.1) | copy-start | bytes 220
  32.9 3.8 %collective-permute-start.4 = (f32[24,128]{1,0:T(8,128)S(1)}, f32[24,128]{1,0:T(8,128)S(1)}, u32[]{:S(2)}, u32[]{:S(2)}) collective-permute-start(f32[24,128]{1,0:T(8,128)S(1)} %add.56.sums), channel_id=1, source_target_pairs={{0,2},{1,3},{2,0},{3,1},{4,6},{5,7},{6,4},{7,5},{8,10},{9,11},{10,... | collective-permute-start | bytes 36872 | tf_op jit(solution)/shard_map/ppermute | solution.py:330
  39.7 1.9 %collective-permute-start.7 = (f32[16,54,128]{2,1,0:T(8,128)S(1)}, f32[16,54,128]{2,1,0:T(8,128)S(1)}, u32[]{:S(2)}, u32[]{:S(2)}) collective-permute-start(f32[16,54,128]{2,1,0:T(8,128)S(1)} %get-tuple-element.36), channel_id=1, source_target_pairs={{0,1},{1,0},{2,3},{3,2},{4,5},{5,4},{6,7},{7,6},{8,9},{9,8},{10,11... | collective-permute-start | bytes 1327112 | tf_op jit(solution)/shard_map/ppermute | solution.py:330
  41.7 6.1 %collective-permute-start.8 = (f32[8,54,128]{2,1,0:T(8,128)S(1)}, f32[8,54,128]{2,1,0:T(8,128)S(1)}, u32[]{:S(2)}, u32[]{:S(2)}) collective-permute-start(f32[8,54,128]{2,1,0:T(8,128)S(1)} %slice.47), channel_id=1, source_target_pairs={{0,2},{1,5},{2,0},{3,7},{4,6},{5,1},{6,4},{7,3},{8,10},{9,13},{10,... | collective-permute-start | bytes 663560 | tf_op jit(solution)/shard_map/ppermute | solution.py:330
  47.8 4.9 %collective-permute-start.9 = (f32[4,54,128]{2,1,0:T(8,128)S(1)}, f32[4,54,128]{2,1,0:T(8,128)S(1)}, u32[]{:S(2)}, u32[]{:S(2)}) collective-permute-start(f32[4,54,128]{2,1,0:T(8,128)S(1)} %slice.49), channel_id=1, source_target_pairs={{0,4},{1,9},{2,6},{3,11},{4,0},{5,13},{6,2},{7,15},{8,12},{9,1},{1... | collective-permute-start | bytes 331784 | tf_op jit(solution)/shard_map/ppermute | solution.py:330
  50.4 4.5 %collective-permute-start.5 = (f32[2,3,1024]{2,1,0:T(4,128)S(1)}, f32[2,3,1024]{2,1,0:T(4,128)S(1)}, u32[]{:S(2)}, u32[]{:S(2)}) collective-permute-start(f32[2,3,1024]{2,1,0:T(4,128)S(1)} %get-tuple-element.33), channel_id=1, source_target_pairs={{0,1},{1,0},{2,3},{3,2},{4,5},{5,4},{6,7},{7,6},{8,9},{9,8},{10,11... | collective-permute-start | bytes 73736 | tf_op jit(solution)/shard_map/ppermute | solution.py:330
  52.7 4.2 %collective-permute-start.10 = (f32[2,54,128]{2,1,0:T(8,128)S(1)}, f32[2,54,128]{2,1,0:T(8,128)S(1)}, u32[]{:S(2)}, u32[]{:S(2)}) collective-permute-start(f32[2,54,128]{2,1,0:T(8,128)S(1)} %slice.51), channel_id=1, source_target_pairs={{0,8},{1,3},{2,10},{3,1},{4,12},{5,7},{6,14},{7,5},{8,0},{9,11},{1... | collective-permute-start | bytes 165896 | tf_op jit(solution)/shard_map/ppermute | solution.py:330
  54.9 5.0 %collective-permute-start.6 = (f32[1,3,1024]{2,1,0:T(4,128)S(1)}, f32[1,3,1024]{2,1,0:T(4,128)S(1)}, u32[]{:S(2)}, u32[]{:S(2)}) collective-permute-start(f32[1,3,1024]{2,1,0:T(4,128)S(1)} %slice.45), channel_id=1, source_target_pairs={{0,2},{1,3},{2,0},{3,1},{4,6},{5,7},{6,4},{7,5},{8,10},{9,11},{10,... | collective-permute-start | bytes 36872 | tf_op jit(solution)/shard_map/ppermute | solution.py:330
  57.0 4.8 %collective-permute-start.11 = (f32[1,54,128]{2,1,0:T(8,128)S(1)}, f32[1,54,128]{2,1,0:T(8,128)S(1)}, u32[]{:S(2)}, u32[]{:S(2)}) collective-permute-start(f32[1,54,128]{2,1,0:T(8,128)S(1)} %slice.53), channel_id=1, source_target_pairs={{0,16},{1,17},{2,18},{3,19},{4,20},{5,21},{6,22},{7,23},{8,24},{9,... | collective-permute-start | bytes 82952 | tf_op jit(solution)/shard_map/ppermute | solution.py:330

commit v3 on v2

v3 whole, which is shorter than its diff:
```python
import functools

import jax
import jax.numpy as jnp
import numpy as np
from jax import lax
from jax.experimental import pallas as pl
from jax.experimental.pallas import tpu as pltpu
from jax.sharding import PartitionSpec as P

TENORS = 5
BUCKETS = 18
GROUP = 24
SCEN = 3
NODES = 4096
BLOCK = 512
LANES = 128
PIECE = 256
LOW = 256
HIGH = NODES // LOW
AXES = ("trade", "factor")
MIB = 1 << 20

BASE = np.array([1.0, 0.65, 0.35, 0.2275], np.float32)
LEVELS = np.stack([BASE, np.minimum(1.25 * BASE, 1.0), np.maximum(2.0 * BASE - 1.0, 0.75 * BASE)])
SCENARIO = (1.0, 1.25, 0.75)
CROSS = 0.5
SAME_BOTH = LEVELS[:, 0] - LEVELS[:, 1] - LEVELS[:, 2] + LEVELS[:, 3]

SMEM = pl.BlockSpec(memory_space=pltpu.SMEM)
VMEM = pl.BlockSpec(memory_space=pltpu.VMEM)
ANY = pl.BlockSpec(memory_space=pl.ANY)
f32 = jnp.float32
bf16 = jnp.bfloat16


def shape(*dims, dtype=f32):
    return jax.ShapeDtypeStruct(dims, dtype)


def call(kernel, out_shape, in_specs, out_specs, name, scratch=(), flops=0, alias=None, limit=8):
    return pl.pallas_call(
        kernel,
        out_shape=out_shape,
        in_specs=in_specs,
        out_specs=out_specs,
        scratch_shapes=list(scratch),
        name=name,
        input_output_aliases=alias or {},
        compiler_params=pltpu.CompilerParams(vmem_limit_bytes=limit * MIB),
        cost_estimate=pl.CostEstimate(flops=flops, bytes_accessed=1 << 16, transcendentals=0),
    )


def dot(a, b):
    return lax.dot_general(a, b, (((1,), (0,)), ((), ())), preferred_element_type=f32)


def dot_t(a, b):
    return lax.dot_general(a, b, (((1,), (1,)), ((), ())), preferred_element_type=f32)


def totals_kernel(count_hbm, sens, held, raw, count, sems, count_sem):
    width, trades = sens.shape
    pieces = [(start, min(PIECE, width - start)) for start in range(0, width, PIECE)]
    counting = pltpu.make_async_copy(count_hbm, count, count_sem)
    counting.start()
    copies = []
    for i, (start, rows) in enumerate(pieces):
        part = pl.ds(start, rows)
        copies.append(pltpu.make_async_copy(sens.at[part], held.at[part], sems.at[i]))
        copies[-1].start()
    counting.wait()
    ones = jnp.ones((16, 3 * LANES), bf16)

    def run(tiles):
        for copy, (start, rows) in zip(copies, pieces):
            copy.wait()
            chains = 1 if rows > 128 else 4
            totals = [None] * chains
            for i, (lane, live) in enumerate(tiles(rows)):
                part = held[start : start + rows, lane : lane + LANES].astype(f32)
                if live is not None:
                    part = jnp.where(live, part, 0.0)
                j = i % chains
                totals[j] = part if totals[j] is None else totals[j] + part
            value = sum(totals[1:], totals[0])
            upper = value.astype(bf16)
            value = value - upper.astype(f32)
            middle = value.astype(bf16)
            lower = (value - middle.astype(f32)).astype(bf16)
            parts = jnp.concatenate([upper, middle, lower], 1)
            raw[:, start : start + rows] = dot_t(ones, parts)[:1]

    full = count[0] == BLOCK

    @pl.when(full)
    def _():
        run(lambda rows: [(lane, None) for lane in range(0, trades, LANES)])

    @pl.when(jnp.logical_not(full))
    def _():
        def tiles(rows):
            slot = lax.broadcasted_iota(jnp.int32, (rows, LANES), 1)
            return [(i * BLOCK, slot < count[i]) for i in range(trades // BLOCK)]

        run(tiles)


def tables_kernel(
    count,
    weight,
    own,
    nodes,
    buckets,
    low_hot,
    pair_hot,
    tenor_hot,
    factor_weight,
    tenor,
    passed,
    mine,
    *,
    spots,
    factor_size,
):
    passed[...] = own[...]
    f = lax.axis_index("factor")
    me = lax.axis_index("trade") * factor_size + f
    bits = len(spots)
    inner = (NODES >> bits).bit_length() - 1
    node = nodes[...]
    other = (node >> inner) ^ me
    label = node & ((1 << inner) - 1)
    for i in range(bits):
        label = label + ((other >> i) & 1) * spots[i]
    low = label & (LOW - 1)
    high = label >> (LOW.bit_length() - 1)
    trades = node.shape[1]
    for start in range(0, trades, 512):
        part = pl.ds(start, 512)
        here = lax.broadcasted_iota(jnp.int32, (LOW, 512), 0) == low[:, start : start + 512]
        low_hot[:, part] = jnp.where(here, 1.0, 0.0).astype(bf16)
        row = lax.broadcasted_iota(jnp.int32, (2 * GROUP, 512), 0)
        away = high[:, start : start + 512] - jnp.where(row < GROUP, 0, 1)
        slot = lax.broadcasted_iota(jnp.int32, (2 * GROUP, 512), 1)
        away = jnp.where(slot < count[start // BLOCK], away, -1)
        for p in range(HIGH // 2):
            pair_hot[p, :, part] = jnp.where(away == 2 * p, 1.0, 0.0).astype(bf16)
    width = own.shape[1]
    for i in range(factor_size):

        @pl.when(f == i)
        def _(i=i):
            mine[...] = buckets[:, i * width : (i + 1) * width]

    bucket = mine[...]
    place = lax.broadcasted_iota(jnp.int32, (1, width), 1)
    column = lax.rem(place, TENORS)
    tenor[...] = column
    row = lax.broadcasted_iota(jnp.int32, (GROUP, width), 0)
    for m in range(TENORS):
        hot = (row == bucket) & (column == m)
        tenor_hot[GROUP * m : GROUP * (m + 1), :] = jnp.where(hot, 1.0, 0.0)
    total = jnp.zeros((1, width), f32)
    for b in range(BUCKETS):
        total = jnp.where(bucket == b, weight[b], total)
    factor_weight[...] = total


def multiply(weights, held, product):
    for start in range(0, held.shape[1], BLOCK):
        part = pl.ds(start, BLOCK)
        product[:, part] = dot(weights, held[:, part])


def twice(value):
    return jnp.concatenate([value, value], 0).astype(bf16)


def ones_kernel(own, tenor_hot, held, product, rounded, passed):
    passed[...] = own[...]
    hot = tenor_hot[...]
    every = sum(hot[GROUP * m : GROUP * (m + 1)] for m in range(TENORS))
    fill = jnp.zeros((8, held.shape[0]), f32)
    hot = jnp.concatenate([hot[: GROUP * (TENORS - 1)], every, fill], 0).astype(bf16)
    multiply(hot, held, product)
    rounded[...] = twice(product[GROUP * (TENORS - 1) : GROUP * TENORS])


def sums_by_node(rounded, low_hot, pair_hot, first, keep, send):
    value = rounded[...]
    masked = jnp.concatenate([value * pair_hot[p] for p in range(HIGH // 2)], 0)
    out = dot_t(masked, low_hot[...])
    for h in range(HIGH):
        rows = out[GROUP * h : GROUP * h + BUCKETS]
        keep[h, first : first + BUCKETS] = rows[:, : LOW // 2]
        send[h, first : first + BUCKETS] = rows[:, LOW // 2 :]


def ones_nodes_kernel(own, rounded, low_hot, pair_hot, keep, send, passed):
    passed[...] = own[...]
    sums_by_node(rounded, low_hot, pair_hot, BUCKETS, keep, send)


def weights_kernel(*refs):
    *raws, factor_weight, tenor, tenor_hot, spread, sums = refs
    width = tenor.shape[1]
    weighted = factor_weight[...] * sum(r[...] for r in raws)
    own_tenor = tenor[...]
    name = weighted
    for d in range(1, TENORS):
        zeros = jnp.zeros((1, d), f32)
        after = jnp.concatenate([weighted[:, d:], zeros], 1)
        before = jnp.concatenate([zeros, weighted[:, : width - d]], 1)
        name = name + jnp.where(own_tenor < TENORS - d, after, 0.0)
        name = name + jnp.where(own_tenor >= d, before, 0.0)
    near = float(LEVELS[0, 1] - LEVELS[0, 3]) * name + float(SAME_BOTH[0]) * weighted
    hot = tenor_hot[:GROUP, :]
    for m in range(1, TENORS):
        hot = hot + tenor_hot[GROUP * m : GROUP * (m + 1), :]
    full = jnp.concatenate([hot * weighted, hot * near], 0)
    upper = full.astype(bf16).astype(f32)
    fill = jnp.zeros((32, width), f32)
    spread[...] = jnp.concatenate([upper, full - upper, fill], 0).astype(bf16)
    lane = lax.broadcasted_iota(jnp.int32, (GROUP, LANES), 1)
    out = jnp.zeros((GROUP, LANES), f32)
    square = jnp.zeros((GROUP, 1), f32)
    for m in range(TENORS):
        hot = tenor_hot[GROUP * m : GROUP * (m + 1), :]
        part = hot * weighted
        out = jnp.where(lane == m, jnp.sum(part, 1, keepdims=True), out)
        square = square + jnp.sum(part * weighted, 1, keepdims=True)
        if m == 0:
            names = jnp.sum(hot * (name * name), 1, keepdims=True)
    out = jnp.where(lane == TENORS, square, out)
    out = jnp.where(lane == TENORS + 1, names, out)
    sums[...] = out


def spread_kernel(spread, held, product, rounded):
    multiply(spread[...], held, product)
    rounded[...] = twice(product[:GROUP] + product[2 * GROUP : 3 * GROUP])


def weighted_nodes_kernel(rounded, low_hot, pair_hot, _, __, keep, send):
    sums_by_node(rounded, low_hot, pair_hot, 0, keep, send)


def product_nodes_kernel(*refs):
    *sums, near, tenors, low_hot, pair_hot, _, _, alloc, total, keep, send, rounded = refs
    gather = sum(r[...] for r in sums)
    total[...] = gather
    lane = lax.broadcasted_iota(jnp.int32, (GROUP, LANES), 1)
    bucket = jnp.sum(jnp.where(lane < TENORS, gather, 0.0), 1, keepdims=True)
    same = float(LEVELS[0, 2] - LEVELS[0, 3])
    last = gather[:, TENORS - 1 : TENORS]
    pull = [same * (gather[:, m : m + 1] - last) for m in range(TENORS - 1)]
    pull.append(same * last + float(LEVELS[0, 3]) * bucket)
    for start in range(0, near.shape[1], BLOCK):
        part = pl.ds(start, BLOCK)
        value = near[GROUP : 2 * GROUP, part] + near[3 * GROUP : 4 * GROUP, part]
        for m in range(TENORS):
            value = value + pull[m] * tenors[GROUP * m : GROUP * (m + 1), part]
        alloc[:, part] = value
        rounded[:, part] = twice(value)
    sums_by_node(rounded, low_hot, pair_hot, 2 * BUCKETS, keep, send)


def join_kernel(own, keep, more, passed, *chunks):
    passed[...] = own[...]
    size = chunks[0].shape[0]
    for c, chunk in enumerate(chunks):
        part = pl.ds(c * size, size)
        chunk[...] = keep[part] + more[part]


def capital_kernel(
    count, weight, load, total, product, near, tenors, keep, send, mix, capital, *, trades_total, parts
):
    half = keep.shape[0]
    length = product.shape[1] // parts
    gather = total[...]
    lane = lax.broadcasted_iota(jnp.int32, (GROUP, LANES), 1)
    row = lax.broadcasted_iota(jnp.int32, (GROUP, 1), 0)
    real = row < BUCKETS
    risk = jnp.zeros((GROUP, 1), f32)
    loading = jnp.zeros((GROUP, 1), f32)
    for b in range(BUCKETS):
        risk = jnp.where(row == b, weight[b], risk)
        loading = jnp.where(row == b, load[b], loading)
    tenor_part = jnp.where(lane < TENORS, gather, 0.0)
    sums = jnp.sum(tenor_part, 1, keepdims=True)
    tenor_square = jnp.sum(tenor_part * tenor_part, 1, keepdims=True)
    own_square = gather[:, TENORS : TENORS + 1]
    name_square = gather[:, TENORS + 1 : TENORS + 2]
    columns = []
    row8 = lax.broadcasted_iota(jnp.int32, (8, LANES), 0)
    capitals = jnp.zeros((8, LANES), f32)
    for s in range(SCEN):
        level = [float(v) for v in LEVELS[s]]
        form = level[3] * sums * sums + (level[2] - level[3]) * tenor_square
        form = form + (level[1] - level[3]) * name_square + float(SAME_BOTH[s]) * own_square
        root = jnp.sqrt(form + 1e-6)
        radius = jnp.sqrt(root * root + sums * sums)
        capped = sums * root / radius
        pulled = jnp.where(real, loading * capped, 0.0)
        loaded = jnp.sum(pulled, 0, keepdims=True)
        squares = jnp.sum(pulled * pulled, 0, keepdims=True)
        cross = CROSS * SCENARIO[s]
        inside = jnp.sum(jnp.where(real, root * root, 0.0), 0, keepdims=True)
        cap = jnp.sqrt(inside + cross * (loaded * loaded - squares))
        cross_pull = cross * (loading * loaded - loading * loading * capped) / cap
        ratio = sums / radius
        share = root / radius
        coef_form = (root / cap + cross_pull * ratio * ratio * ratio) / root
        coef_sum = cross_pull * share * share * share
        scale = jnp.where(real, risk / cap, 0.0)
        columns.append(
            [
                scale * coef_form * (1.0 - SCENARIO[s]),
                scale * coef_sum,
                scale * coef_form * SCENARIO[s],
            ]
        )
        capitals = jnp.where(row8 == s, cap, capitals)
    capital[...] = capitals
    for s in range(SCEN):
        column = jnp.concatenate([c[:BUCKETS] for c in columns[s]], 0)
        mix[s] = jnp.broadcast_to(column * float(NODES), (3 * BUCKETS, LANES))
    f = lax.axis_index("factor")
    bits = parts.bit_length() - 1
    for p in range(parts):
        block = f ^ sum(((p >> i) & 1) << (bits - 1 - i) for i in range(bits))
        rows = pl.ds(pl.multiple_of(block * length, LANES), length)
        values = [
            near[:GROUP, rows] + near[2 * GROUP : 3 * GROUP, rows],
            tenors[GROUP * (TENORS - 1) : GROUP * TENORS, rows],
            product[:, rows],
        ]
        slot = lax.broadcasted_iota(jnp.int32, (1, BLOCK), 1)
        live = [
            jnp.where(slot < count[block * (length // BLOCK) + i], 1.0, 0.0)
            for i in range(length // BLOCK)
        ]
        live = jnp.concatenate(live, 1)
        for s in range(SCEN):
            out = sum(v * (c * float(trades_total)) for v, c in zip(values, columns[s]))
            out = jnp.sum(out, 0, keepdims=True) * live
            for j in range(length // LANES):
                place = s * (length // LANES) + j
                piece = out[:, j * LANES : (j + 1) * LANES]
                if p < half:
                    keep[p, place : place + 1] = piece
                else:
                    send[p - half, place : place + 1] = piece


def finish_kernel(mix, capital, trade_keep, trade_more, *refs, scale):
    *pieces, scaled, trades, nodes = refs
    total = sum(p[...] for p in pieces)
    for s in range(SCEN):
        mixed = mix[s][:, : total.shape[1]] * total
        nodes[s] = sum(mixed[BUCKETS * j : BUCKETS * (j + 1)] for j in range(3))
    value = trade_keep[...] + trade_more[...]
    count = value.shape[0] // SCEN
    for s in range(SCEN):
        for j in range(count):
            place = s * count + j
            trades[s : s + 1, j * LANES : (j + 1) * LANES] = value[place : place + 1]
    for s in range(SCEN):
        scaled[s] = jnp.max(capital[s : s + 1, :]) * scale


def local(
    sensitivity,
    block_count,
    trade_node,
    factor_bucket,
    risk_weight,
    bucket_loading,
    *,
    trade_size,
    factor_size,
):
    trade_rows, width = sensitivity.shape
    trades_total = trade_rows * trade_size
    devices = trade_size * factor_size
    trade_bits = trade_size.bit_length() - 1
    factor_bits = factor_size.bit_length() - 1
    bits = trade_bits + factor_bits

    def exchange(x, mask):
        return lax.ppermute(x, AXES, [(o, o ^ mask) for o in range(devices)])

    over_factor = list(range(1, factor_bits))
    over_trade = list(range(factor_bits, bits))
    groups = [over_trade[:2], over_factor[:1] + over_trade[2:3]]
    groups += [[b] for b in over_factor[1:] + over_trade[3:]]
    order = [0] + sum(groups, [])
    places = [7, 11, 10, 9, 8, 6, 5, 4, 3, 2, 1, 0]
    spots = [0] * bits
    for i, bit in enumerate(order):
        spots[bit] = 1 << places[i]

    by_factor = pltpu.with_memory_space_constraint(sensitivity.T, pltpu.HBM)
    held, raw = call(
        totals_kernel,
        (pltpu.VMEM((width, trade_rows), bf16), shape(1, width)),
        [ANY, ANY],
        (VMEM, VMEM),
        "totals",
        scratch=[
            pltpu.SMEM(block_count.shape, jnp.int32),
            pltpu.SemaphoreType.DMA((-(-width // PIECE),)),
            pltpu.SemaphoreType.DMA,
        ],
        flops=10**7,
    )(pltpu.with_memory_space_constraint(block_count, pltpu.HBM), by_factor)

    rows = pltpu.VMEM((GROUP, trade_rows), f32)
    multiplied = pltpu.VMEM((128, trade_rows), f32)
    rounded = pltpu.VMEM((2 * GROUP, trade_rows), bf16)
    trade_mask = [1 << b for b in over_trade]
    other = exchange(raw, trade_mask[0])
    low_hot, pair_hot, tenor_hot, factor_weight, tenor, raw = call(
        functools.partial(tables_kernel, spots=spots, factor_size=factor_size),
        (
            pltpu.VMEM((LOW, trade_rows), bf16),
            pltpu.VMEM((HIGH // 2, 2 * GROUP, trade_rows), bf16),
            pltpu.VMEM((GROUP * TENORS, width), f32),
            pltpu.VMEM((1, width), f32),
            pltpu.VMEM((1, width), jnp.int32),
            shape(1, width),
        ),
        [SMEM, SMEM, VMEM, VMEM, VMEM],
        (VMEM,) * 6,
        "tables",
        scratch=[pltpu.VMEM((1, width), jnp.int32)],
        flops=10**7,
    )(block_count, risk_weight, raw, trade_node[None, :], factor_bucket[None, :])

    for mask in trade_mask[3:]:
        raw = raw + other
        other = exchange(raw, mask)
    raw = raw + other
    others = [exchange(raw, mask) for mask in (trade_mask[1] + trade_mask[2], trade_mask[2], trade_mask[1])]
    tenors, ones_rounded, raw = call(
        ones_kernel,
        (multiplied, rounded, shape(1, width)),
        [VMEM] * 3,
        (VMEM,) * 3,
        "ones",
        flops=2 * 128 * width * trade_rows,
    )(raw, tenor_hot, held)

    all_nodes = (HIGH, 3 * BUCKETS, LOW // 2)
    nodes_flops = 2 * 512 * trade_rows * LOW
    keep, send, raw = call(
        ones_nodes_kernel,
        (pltpu.VMEM(all_nodes, f32), pltpu.VMEM(all_nodes, f32), shape(1, width)),
        [VMEM] * 4,
        (VMEM,) * 3,
        "ones_nodes",
        flops=nodes_flops,
    )(raw, ones_rounded, low_hot, pair_hot)

    spread, sums = call(
        weights_kernel,
        (pltpu.VMEM((128, width), bf16), shape(GROUP, LANES)),
        [VMEM] * (4 + len(others)),
        (VMEM, VMEM),
        "weights",
        flops=10**6,
    )(raw, *others, factor_weight, tenor, tenor_hot)

    others = [exchange(sums, mask) for mask in range(1, factor_size)]
    near, weighted_rounded = call(
        spread_kernel,
        (multiplied, rounded),
        [VMEM] * 2,
        (VMEM,) * 2,
        "spread",
        flops=2 * 128 * width * trade_rows,
    )(spread, held)
    keep, send = call(
        weighted_nodes_kernel,
        (pltpu.VMEM(all_nodes, f32),) * 2,
        [VMEM] * 5,
        (VMEM,) * 2,
        "weighted_nodes",
        alias={3: 0, 4: 1},
        flops=nodes_flops,
    )(weighted_rounded, low_hot, pair_hot, keep, send)

    product, total, keep, send = call(
        product_nodes_kernel,
        (rows, shape(GROUP, LANES), pltpu.VMEM(all_nodes, f32), pltpu.VMEM(all_nodes, f32)),
        [VMEM] * (7 + len(others)),
        (VMEM,) * 4,
        "product_nodes",
        alias={5 + len(others): 2, 6 + len(others): 3},
        scratch=[rounded],
        flops=nodes_flops,
    )(sums, *others, near, tenors, low_hot, pair_hot, keep, send)
    from_core = exchange(send, 1)

    trade_shape = shape(factor_size // 2, SCEN * trade_rows // factor_size // LANES, LANES)
    trade_keep, trade_send, mix, capital = call(
        functools.partial(capital_kernel, trades_total=trades_total, parts=factor_size),
        (trade_shape, trade_shape, shape(SCEN, 3 * BUCKETS, LANES), shape(8, LANES)),
        [SMEM, SMEM, SMEM] + [VMEM] * 4,
        (VMEM,) * 4,
        "capital",
        flops=10**7,
    )(block_count, risk_weight, bucket_loading, total, product, near, tenors)

    count = 1 << len(groups[0])
    trade_send, *chunks = call(
        join_kernel,
        (trade_shape,) + (shape(HIGH // count, 3 * BUCKETS, LOW // 2),) * count,
        [VMEM] * 3,
        (VMEM,) * (1 + count),
        "join",
        flops=10**6,
    )(trade_send, keep, from_core)
    trade_more = exchange(trade_send, 1)
    for i, group in enumerate(groups):
        count = 1 << len(group)
        if i > 0:
            axis = 0 if keep.shape[0] > 1 else 2
            chunks = jnp.split(keep, count, axis)
        pieces = [chunks[0]]
        for c in range(count - 1, 0, -1):
            part = [b for j, b in enumerate(group) if (c >> (len(group) - 1 - j)) & 1]
            mask = sum(1 << b for b in part)
            message = chunks[c]
            if len(part) == 1 and part[0] in over_factor:
                trade_send, trade_keep = jnp.split(trade_keep + trade_more, 2, 0)[::-1]
                if message.shape[2] == LANES:
                    cut = trade_send.shape[0] * trade_send.shape[1]
                    message = jnp.concatenate(
                        [trade_send.reshape(cut, LANES), message.reshape(-1, LANES)], 0
                    )
                    message = exchange(message, mask)
                    trade_more = message[:cut].reshape(trade_send.shape)
                    message = message[cut:].reshape(chunks[c].shape)
                else:
                    trade_more = exchange(trade_send, mask)
                    message = exchange(message, mask)
            else:
                message = exchange(message, mask)
            pieces.append(message)
        if i + 1 < len(groups):
            keep = sum(pieces[1:], pieces[0])
    return call(
        functools.partial(finish_kernel, scale=1.0 / trades_total**0.5),
        (
            shape(SCEN),
            shape(SCEN, trade_rows // factor_size),
            shape(SCEN, BUCKETS, NODES // devices),
        ),
        [VMEM] * (4 + len(pieces)),
        (SMEM, VMEM, VMEM),
        "finish",
        flops=10**6,
    )(mix, capital, trade_keep[0], trade_more[0], *[p[0] for p in pieces])


def solution(mesh):
    sizes = dict(mesh.shape)
    return jax.shard_map(
        functools.partial(local, trade_size=sizes["trade"], factor_size=sizes["factor"]),
        mesh=mesh,
        in_specs=(P("trade", "factor"), P("trade"), P("trade"), P(), P(), P()),
        out_specs=(P(), P(None, ("trade", "factor")), P(None, None, ("trade", "factor"))),
        check_vma=False,
    )
```

time: 62.6 us -> 47.3 us (0.76)
  local copies, waits for them, and re-layouts: 11 us -> 0.06 us
  waiting for transfers between devices: 13.6 us -> 11.3 us
  other arithmetic: 2.06 us -> 0.05 us
  starting transfers between devices: 19.2 us -> 18.3 us
  Pallas kernels: 15.8 us -> 16.6 us
    unnamed x16 -> x10, local copies, waits for them, and re-layouts: 10.1 us -> 0.02 us
    ppermute x12 -> x15, waiting for transfers between devices: 13.6 us -> 11.3 us  [exchange(): return lax.ppermute(x, AXES, [(o, o ^ mask) for o in range(devices)])]
    pallas_call x6 -> x10, Pallas kernels: 9.89 us -> 11.4 us  [the longest x1 2.18 us: local(): call(spread_kernel, (multiplied, rounded), [VMEM] * 2, (VMEM,) * 2, 'spre...]
    ppermute x12 -> x15, starting transfers between devices: 19.2 us -> 18.3 us  [exchange(): return lax.ppermute(x, AXES, [(o, o ^ mask) for o in range(devices)])]
    dynamic_slice x1 -> x0, local copies, waits for them, and re-layouts: 0.79 us -> none  [local(): lax.dynamic_slice_in_dim(factor_bucket, f * width, width, 0)[None, :]]
    pallas_call x1, Pallas kernels: 5.9 us -> 5.19 us  [local(): call(totals_kernel, (pltpu.VMEM((width, trade_rows), bf16), shape(1, widt...]
  transfers between devices with their start and end apart: 12 -> 15, of which waited for: 8 -> 8; matrix products, arithmetic and copies ran while one was open for 3% -> 0% of each run, Pallas kernels for 10% -> 19%
where the time goes in v3:
time: 47.3 us; the launch traced here: 47.2 us
  starting transfers between devices  18.3 us (39%)
  Pallas kernels  16.6 us (35%)
  waiting for transfers between devices  11.3 us (24%)
  between operations  1.02 us (2%)
    ppermute x15, starting transfers between devices, exchange(): return lax.ppermute(x, AXES, [(o, o ^ mask) for o in range(devices)])  18.3 us
    ppermute x15, waiting for transfers between devices, exchange(): return lax.ppermute(x, AXES, [(o, o ^ mask) for o in range(devices)])  11.3 us
    pallas_call x1, Pallas kernels, local(): call(totals_kernel, (pltpu.VMEM((width, trade_rows), bf16), shape(1, widt...  5.19 us
    pallas_call x1, Pallas kernels, local(): call(spread_kernel, (multiplied, rounded), [VMEM] * 2, (VMEM,) * 2, 'spre...  2.18 us
    pallas_call x1, Pallas kernels, local(): call(ones_kernel, (multiplied, rounded, shape(1, width)), [VMEM] * 3, (VM...  2.09 us
    pallas_call x1, Pallas kernels, local(): call(functools.partial(tables_kernel, spots=spots, factor_size=factor_siz...  1.47 us
    pallas_call x1, Pallas kernels, local(): call(product_nodes_kernel, (rows, shape(GROUP, LANES), pltpu.VMEM(all_nod...  1.29 us
    pallas_call x1, Pallas kernels, local(): call(functools.partial(capital_kernel, trades_total=trades_total, parts=f...  1.2 us
  transfers between devices with their start and end apart: 15, of which 8 were waited for; matrix products, arithmetic and copies ran while one was open for 0% of the time, Pallas kernels for 19%

profile of v3, /device:TPU:0, one launch (start us, length us, event | category | flops | bytes accessed | tf_op | source)
XLA Modules:
  0.0 47.2 jit_solution(6246963775594839781)
XLA Ops:
  0.6 0.0 copy-start.4
  0.6 0.0 copy-start
  0.7 0.0 copy-start.1
  0.7 0.0 copy-start.2
  0.7 5.2 %totals.1 = (bf16[1600,4096]{1,0:T(8,128)(2,1)S(1)}, f32[1,1600]{1,0:T(1,128)S(1)}) custom-call(s32[8]{0:T(128)} %count.3, bf16[1600,4096]{1,0:T(8,128)(2,1)} %bitcast.15), custom_call_target="tpu_custom_call" | custom-call | flops 10000000 | bytes 65536 | tf_op jit(solution)/shard_map/totals/pallas_call | solution.py:407
  5.9 3.0 %collective-permute-start = (f32[1,1600]{1,0:T(1,128)S(1)}, f32[1,1600]{1,0:T(1,128)S(1)}, u32[]{:S(2)}, u32[]{:S(2)}) collective-permute-start(f32[1,1600]{1,0:T(1,128)S(1)} %get-tuple-element.36.own), channel_id=1, source_target_pairs={{0,4},{1,5},{2,6},{3,7},{4,0},{5,1},{6,2},{7,3},{8,12},{9,13},{10,... | collective-permute-start | bytes 19208 | tf_op jit(solution)/shard_map/ppermute | solution.py:394
  8.9 0.0 copy-done.4
  8.9 0.0 copy-done
  8.9 0.0 copy-done.1
  8.9 0.0 copy-done.2
  9.0 1.5 %tables.1 = (bf16[256,4096]{1,0:T(8,128)(2,1)S(1)}, bf16[8,48,4096]{2,1,0:T(8,128)(2,1)S(1)}, f32[120,1600]{1,0:T(8,128)S(1)}, f32[1,1600]{1,0:T(1,128)S(1)}, s3...) custom-call(s32[8]{0:T(128)S(1)} %copy-done.1, f32[18]{0:T(128)S(1)} %copy-done.2, f32[1,1600]{1,0:T(1,128)S(1)} %get-tuple-element.36.own, ...), custom_call_target="tpu_custom_call" | custom-call | flops 10000000 | bytes 65536 | tf_op jit(solution)/shard_map/tables/pallas_call | solution.py:426
  10.4 0.1 collective-permute-done
  10.5 2.1 %collective-permute-start.3 = (f32[1,1600]{1,0:T(1,128)S(1)}, f32[1,1600]{1,0:T(1,128)S(1)}, u32[]{:S(2)}, u32[]{:S(2)}) collective-permute-start(f32[1,1600]{1,0:T(1,128)S(1)} %add.15.own), channel_id=1, source_target_pairs={{0,8},{1,9},{2,10},{3,11},{4,12},{5,13},{6,14},{7,15},{8,0},{9,1},... | collective-permute-start | bytes 19208 | tf_op jit(solution)/shard_map/ppermute | solution.py:394
  12.7 2.6 %collective-permute-start.2 = (f32[1,1600]{1,0:T(1,128)S(1)}, f32[1,1600]{1,0:T(1,128)S(1)}, u32[]{:S(2)}, u32[]{:S(2)}) collective-permute-start(f32[1,1600]{1,0:T(1,128)S(1)} %add.15.own), channel_id=1, source_target_pairs={{0,16},{1,17},{2,18},{3,19},{4,20},{5,21},{6,22},{7,23},{8,24},{9,... | collective-permute-start | bytes 19208 | tf_op jit(solution)/shard_map/ppermute | solution.py:394
  15.3 0.1 collective-permute-start.1
  15.4 2.1 %ones.1 = (f32[128,4096]{1,0:T(8,128)S(1)}, bf16[48,4096]{1,0:T(8,128)(2,1)S(1)}, f32[1,1600]{1,0:T(1,128)S(1)}) custom-call(f32[1,1600]{1,0:T(1,128)S(1)} %add.15.own, f32[120,1600]{1,0:T(8,128)S(1)} %get-tuple-element.38.tenor_hot.refs_6_, bf16[1600,4096]{1,0:T(8,128)(2,1)S(1)} %get-tuple-element.39.held), custom_call_target="tpu_custom_call" | custom-call | flops 1677721600 | bytes 65536 | tf_op jit(solution)/shard_map/ones/pallas_call | solution.py:448
  17.5 1.0 %ones_nodes.1 = (f32[16,54,128]{2,1,0:T(8,128)S(1)}, f32[16,54,128]{2,1,0:T(8,128)S(1)}, f32[1,1600]{1,0:T(1,128)S(1)}) custom-call(f32[1,1600]{1,0:T(1,128)S(1)} %get-tuple-element.40.own, bf16[48,4096]{1,0:T(8,128)(2,1)S(1)} %get-tuple-element.41.rounded, bf16[256,4096]{1,0:T(8,128)(2,1)S(1)} %get-tuple-element.42.low_hot.refs_6_, ...), custom_call_target="tpu_custom_call" | custom-call | flops 1073741824 | bytes 65536 | tf_op jit(solution)/shard_map/ones_nodes/pallas_call | solution.py:459
  18.5 0.0 collective-permute-done.3.refs_3_
  18.5 0.0 collective-permute-done.2.refs_2_
  18.5 2.2 %collective-permute-done.1.refs_1_ = f32[1,1600]{1,0:T(1,128)S(1)} collective-permute-done((f32[1,1600]{1,0:T(1,128)S(1)}, f32[1,1600]{1,0:T(1,128)S(1)}, u32[]{:S(2)}, u32[]{:S(2)}) %collective-permute-start.1) | collective-permute-done | bytes 6432 | tf_op jit(solution)/shard_map/ppermute | solution.py:394
  20.7 0.4 weights.1
  21.1 0.0 collective-permute-start.6
  21.1 1.6 %collective-permute-start.5 = (f32[24,128]{1,0:T(8,128)S(1)}, f32[24,128]{1,0:T(8,128)S(1)}, u32[]{:S(2)}, u32[]{:S(2)}) collective-permute-start(f32[24,128]{1,0:T(8,128)S(1)} %get-tuple-element.47.refs_0_), channel_id=1, source_target_pairs={{0,2},{1,3},{2,0},{3,1},{4,6},{5,7},{6,4},{7,5},{8,10},{9,11},{10,... | collective-permute-start | bytes 36872 | tf_op jit(solution)/shard_map/ppermute | solution.py:394
  22.7 0.3 collective-permute-start.4
  23.0 2.2 %spread.1 = (f32[128,4096]{1,0:T(8,128)S(1)}, bf16[48,4096]{1,0:T(8,128)(2,1)S(1)}) custom-call(bf16[128,1600]{1,0:T(8,128)(2,1)S(1)} %get-tuple-element.48.spread, bf16[1600,4096]{1,0:T(8,128)(2,1)S(1)} %get-tuple-element.39.held), custom_call_target="tpu_custom_call" | custom-call | flops 1677721600 | bytes 65536 | tf_op jit(solution)/shard_map/spread/pallas_call | solution.py:478
  25.2 1.0 %weighted_nodes.1 = (f32[16,54,128]{2,1,0:T(8,128)S(1)}, f32[16,54,128]{2,1,0:T(8,128)S(1)}) custom-call(bf16[48,4096]{1,0:T(8,128)(2,1)S(1)} %get-tuple-element.51.rounded, bf16[256,4096]{1,0:T(8,128)(2,1)S(1)} %get-tuple-element.42.low_hot.refs_6_, ...), custom_call_target="tpu_custom_call", output_to_operand_aliasing={{0}: (3, {}), {1}: (4, {})} | custom-call | flops 1073741824 | bytes 65536 | tf_op jit(solution)/shard_map/weighted_nodes/pallas_call | solution.py:486
  26.2 0.0 collective-permute-done.6.refs_3_
  26.2 0.0 collective-permute-done.5.refs_2_
  26.2 0.0 collective-permute-done.4.refs_1_
  26.2 0.0 copy-start.3
  26.2 1.3 %product_nodes.1 = (f32[24,4096]{1,0:T(8,128)S(1)}, f32[24,128]{1,0:T(8,128)S(1)}, f32[16,54,128]{2,1,0:T(8,128)S(1)}, f32[16,54,128]{2,1,0:T(8,128)S(1)}) custom-call(f32[24,128]{1,0:T(8,128)S(1)} %get-tuple-element.47.refs_0_, f32[24,128]{1,0:T(8,128)S(1)} %collective-permute-done.4.refs_1_, ...), custom_call_target="tpu_custom_call", output_to_operand_aliasing={{2}: (8, {}), {3}: (9, {})} | custom-call | flops 1073741824 | bytes 65536 | tf_op jit(solution)/shard_map/product_nodes/pallas_call | solution.py:496
  27.5 0.3 collective-permute-start.7
  27.8 0.0 copy-done.3
  27.8 1.2 %capital.1 = (f32[2,24,128]{2,1,0:T(8,128)S(1)}, f32[2,24,128]{2,1,0:T(8,128)S(1)}, f32[3,54,128]{2,1,0:T(8,128)S(1)}, f32[8,128]{1,0:T(8,128)S(1)}) custom-call(s32[8]{0:T(128)S(1)} %copy-done.1, f32[18]{0:T(128)S(1)} %copy-done.2, f32[18]{0:T(128)S(1)} %copy-done.3, f32[24,128]{1,0:T(8,128)S(1)} %get-tuple-element.56.total, ...), custom_call_target="tpu_custom_call" | custom-call | flops 10000000 | bytes 65536 | tf_op jit(solution)/shard_map/capital/pallas_call | solution.py:509
  29.0 0.4 collective-permute-done.7.more
  29.4 0.1 join.1
  29.5 0.3 collective-permute-start.8
  29.8 0.0 collective-permute-start.9
  29.8 1.7 %collective-permute-start.10 = (f32[4,54,128]{2,1,0:T(8,128)S(1)}, f32[4,54,128]{2,1,0:T(8,128)S(1)}, u32[]{:S(2)}, u32[]{:S(2)}) collective-permute-start(f32[4,54,128]{2,1,0:T(8,128)S(1)} %get-tuple-element.67), channel_id=1, source_target_pairs={{0,4},{1,5},{2,6},{3,7},{4,0},{5,1},{6,2},{7,3},{8,12},{9,13},{10,... | collective-permute-start | bytes 331784 | tf_op jit(solution)/shard_map/ppermute | solution.py:394
  31.5 1.8 %collective-permute-start.11 = (f32[4,54,128]{2,1,0:T(8,128)S(1)}, f32[4,54,128]{2,1,0:T(8,128)S(1)}, u32[]{:S(2)}, u32[]{:S(2)}) collective-permute-start(f32[4,54,128]{2,1,0:T(8,128)S(1)} %get-tuple-element.68), channel_id=1, source_target_pairs={{0,8},{1,9},{2,10},{3,11},{4,12},{5,13},{6,14},{7,15},{8,0},{9,1},... | collective-permute-start | bytes 331784 | tf_op jit(solution)/shard_map/ppermute | solution.py:394
  33.3 0.0 collective-permute-done.8
  33.3 3.4 %collective-permute-done.9 = f32[4,54,128]{2,1,0:T(8,128)S(1)} collective-permute-done((f32[4,54,128]{2,1,0:T(8,128)S(1)}, f32[4,54,128]{2,1,0:T(8,128)S(1)}, u32[]{:S(2)}, u32[]{:S(2)}) %collective-permute-start.9) | collective-permute-done | bytes 110624 | tf_op jit(solution)/shard_map/ppermute | solution.py:394
  36.7 0.9 %collective-permute-done.10 = f32[4,54,128]{2,1,0:T(8,128)S(1)} collective-permute-done((f32[4,54,128]{2,1,0:T(8,128)S(1)}, f32[4,54,128]{2,1,0:T(8,128)S(1)}, u32[]{:S(2)}, u32[]{:S(2)}) %collective-permute-start.10) | collective-permute-done | bytes 110624 | tf_op jit(solution)/shard_map/ppermute | solution.py:394
  37.6 1.2 %collective-permute-done.11 = f32[4,54,128]{2,1,0:T(8,128)S(1)} collective-permute-done((f32[4,54,128]{2,1,0:T(8,128)S(1)}, f32[4,54,128]{2,1,0:T(8,128)S(1)}, u32[]{:S(2)}, u32[]{:S(2)}) %collective-permute-start.11) | collective-permute-done | bytes 110624 | tf_op jit(solution)/shard_map/ppermute | solution.py:394
  38.9 1.5 %collective-permute-start.12 = (f32[78,128]{1,0:T(8,128)S(1)}, f32[78,128]{1,0:T(8,128)S(1)}, u32[]{:S(2)}, u32[]{:S(2)}) collective-permute-start(f32[78,128]{1,0:T(8,128)S(1)} %pad_maximum_fusion), channel_id=1, source_target_pairs={{0,2},{1,3},{2,0},{3,1},{4,6},{5,7},{6,4},{7,5},{8,10},{9,11},{10,... | collective-permute-start | bytes 119816 | tf_op jit(solution)/shard_map/ppermute | solution.py:394
  40.4 0.3 collective-permute-start.14
  40.8 2.6 %collective-permute-start.13 = (f32[1,54,128]{2,1,0:T(8,128)S(1)}, f32[1,54,128]{2,1,0:T(8,128)S(1)}, u32[]{:S(2)}, u32[]{:S(2)}) collective-permute-start(f32[1,54,128]{2,1,0:T(8,128)S(1)} %get-tuple-element.70), channel_id=1, source_target_pairs={{0,18},{1,19},{2,16},{3,17},{4,22},{5,23},{6,20},{7,21},{8,26},{9,... | collective-permute-start | bytes 82952 | tf_op jit(solution)/shard_map/ppermute | solution.py:394
  43.3 0.0 collective-permute-done.12
  43.3 2.0 %collective-permute-done.14 = f32[1,54,128]{2,1,0:T(8,128)S(1)} collective-permute-done((f32[1,54,128]{2,1,0:T(8,128)S(1)}, f32[1,54,128]{2,1,0:T(8,128)S(1)}, u32[]{:S(2)}, u32[]{:S(2)}) %collective-permute-start.14) | collective-permute-done | bytes 27680 | tf_op jit(solution)/shard_map/ppermute | solution.py:394
  45.3 1.1 %collective-permute-done.13 = f32[1,54,128]{2,1,0:T(8,128)S(1)} collective-permute-done((f32[1,54,128]{2,1,0:T(8,128)S(1)}, f32[1,54,128]{2,1,0:T(8,128)S(1)}, u32[]{:S(2)}, u32[]{:S(2)}) %collective-permute-start.13) | collective-permute-done | bytes 27680 | tf_op jit(solution)/shard_map/ppermute | solution.py:394
  46.4 0.7 %finish.1 = (f32[3]{0:T(128)}, f32[3,1024]{1,0:T(4,128)}, f32[3,18,128]{2,1,0:T(8,128)}) custom-call(f32[3,54,128]{2,1,0:T(8,128)S(1)} %get-tuple-element.58.mix, f32[8,128]{1,0:T(8,128)S(1)} %get-tuple-element.59.capital, f32[24,128]{1,0:T(8,128)S(1)} %get-tuple-element.74.trade_keep, f32[24,128]{1,0:T(8,128)S(1)} %slice.8.trade_more, ...), custom_call_target="tpu_custom_call" | custom-call | flops 1000000 | bytes 65536 | tf_op jit(solution)/shard_map/finish/pallas_call | solution.py:556
  (9 shorter events, 0.1 us)
Async XLA Ops:
  0.6 8.3 %copy-start.4 = (s32[6400]{0:T(1024)S(1)}, s32[6400]{0:T(1024)}, u32[]{:S(2)}) copy-start(s32[6400]{0:T(1024)} %param.9) | copy-start | bytes 76804
  0.6 8.3 %copy-start = (s32[4096]{0:T(1024)S(1)}, s32[4096]{0:T(1024)}, u32[]{:S(2)}) copy-start(s32[4096]{0:T(1024)} %param.8) | copy-start | bytes 49156
  0.7 8.3 %copy-start.1 = (s32[8]{0:T(128)S(1)}, s32[8]{0:T(128)}, u32[]{:S(2)}) copy-start(s32[8]{0:T(128)} %count.3) | copy-start | bytes 100
  0.7 8.3 %copy-start.2 = (f32[18]{0:T(128)S(1)}, f32[18]{0:T(128)}, u32[]{:S(2)}) copy-start(f32[18]{0:T(128)} %weight.3) | copy-start | bytes 220
  5.9 4.6 %collective-permute-start = (f32[1,1600]{1,0:T(1,128)S(1)}, f32[1,1600]{1,0:T(1,128)S(1)}, u32[]{:S(2)}, u32[]{:S(2)}) collective-permute-start(f32[1,1600]{1,0:T(1,128)S(1)} %get-tuple-element.36.own), channel_id=1, source_target_pairs={{0,4},{1,5},{2,6},{3,7},{4,0},{5,1},{6,2},{7,3},{8,12},{9,13},{10,... | collective-permute-start | bytes 19208 | tf_op jit(solution)/shard_map/ppermute | solution.py:394
  10.5 8.0 %collective-permute-start.3 = (f32[1,1600]{1,0:T(1,128)S(1)}, f32[1,1600]{1,0:T(1,128)S(1)}, u32[]{:S(2)}, u32[]{:S(2)}) collective-permute-start(f32[1,1600]{1,0:T(1,128)S(1)} %add.15.own), channel_id=1, source_target_pairs={{0,8},{1,9},{2,10},{3,11},{4,12},{5,13},{6,14},{7,15},{8,0},{9,1},... | collective-permute-start | bytes 19208 | tf_op jit(solution)/shard_map/ppermute | solution.py:394
  12.7 5.8 %collective-permute-start.2 = (f32[1,1600]{1,0:T(1,128)S(1)}, f32[1,1600]{1,0:T(1,128)S(1)}, u32[]{:S(2)}, u32[]{:S(2)}) collective-permute-start(f32[1,1600]{1,0:T(1,128)S(1)} %add.15.own), channel_id=1, source_target_pairs={{0,16},{1,17},{2,18},{3,19},{4,20},{5,21},{6,22},{7,23},{8,24},{9,... | collective-permute-start | bytes 19208 | tf_op jit(solution)/shard_map/ppermute | solution.py:394
  15.3 5.4 %collective-permute-start.1 = (f32[1,1600]{1,0:T(1,128)S(1)}, f32[1,1600]{1,0:T(1,128)S(1)}, u32[]{:S(2)}, u32[]{:S(2)}) collective-permute-start(f32[1,1600]{1,0:T(1,128)S(1)} %add.15.own), channel_id=1, source_target_pairs={{0,24},{1,25},{2,26},{3,27},{4,28},{5,29},{6,30},{7,31},{8,16},{9,... | collective-permute-start | bytes 19208 | tf_op jit(solution)/shard_map/ppermute | solution.py:394
  21.1 5.1 %collective-permute-start.6 = (f32[24,128]{1,0:T(8,128)S(1)}, f32[24,128]{1,0:T(8,128)S(1)}, u32[]{:S(2)}, u32[]{:S(2)}) collective-permute-start(f32[24,128]{1,0:T(8,128)S(1)} %get-tuple-element.47.refs_0_), channel_id=1, source_target_pairs={{0,3},{1,2},{2,1},{3,0},{4,7},{5,6},{6,5},{7,4},{8,11},{9,10},{10,... | collective-permute-start | bytes 36872 | tf_op jit(solution)/shard_map/ppermute | solution.py:394
  21.1 5.1 %collective-permute-start.5 = (f32[24,128]{1,0:T(8,128)S(1)}, f32[24,128]{1,0:T(8,128)S(1)}, u32[]{:S(2)}, u32[]{:S(2)}) collective-permute-start(f32[24,128]{1,0:T(8,128)S(1)} %get-tuple-element.47.refs_0_), channel_id=1, source_target_pairs={{0,2},{1,3},{2,0},{3,1},{4,6},{5,7},{6,4},{7,5},{8,10},{9,11},{10,... | collective-permute-start | bytes 36872 | tf_op jit(solution)/shard_map/ppermute | solution.py:394
  22.7 3.5 %collective-permute-start.4 = (f32[24,128]{1,0:T(8,128)S(1)}, f32[24,128]{1,0:T(8,128)S(1)}, u32[]{:S(2)}, u32[]{:S(2)}) collective-permute-start(f32[24,128]{1,0:T(8,128)S(1)} %get-tuple-element.47.refs_0_), channel_id=1, source_target_pairs={{0,1},{1,0},{2,3},{3,2},{4,5},{5,4},{6,7},{7,6},{8,9},{9,8},{10,11... | collective-permute-start | bytes 36872 | tf_op jit(solution)/shard_map/ppermute | solution.py:394
  26.2 1.6 %copy-start.3 = (f32[18]{0:T(128)S(1)}, f32[18]{0:T(128)}, u32[]{:S(2)}) copy-start(f32[18]{0:T(128)} %load.1) | copy-start | bytes 220
  27.5 1.9 %collective-permute-start.7 = (f32[16,54,128]{2,1,0:T(8,128)S(1)}, f32[16,54,128]{2,1,0:T(8,128)S(1)}, u32[]{:S(2)}, u32[]{:S(2)}) collective-permute-start(f32[16,54,128]{2,1,0:T(8,128)S(1)} %get-tuple-element.63), channel_id=1, source_target_pairs={{0,1},{1,0},{2,3},{3,2},{4,5},{5,4},{6,7},{7,6},{8,9},{9,8},{10,11... | collective-permute-start | bytes 1327112 | tf_op jit(solution)/shard_map/ppermute | solution.py:394
  29.5 3.8 %collective-permute-start.8 = (f32[2,24,128]{2,1,0:T(8,128)S(1)}, f32[2,24,128]{2,1,0:T(8,128)S(1)}, u32[]{:S(2)}, u32[]{:S(2)}) collective-permute-start(f32[2,24,128]{2,1,0:T(8,128)S(1)} %get-tuple-element.64), channel_id=1, source_target_pairs={{0,1},{1,0},{2,3},{3,2},{4,5},{5,4},{6,7},{7,6},{8,9},{9,8},{10,11... | collective-permute-start | bytes 73736 | tf_op jit(solution)/shard_map/ppermute | solution.py:394
  29.8 6.9 %collective-permute-start.9 = (f32[4,54,128]{2,1,0:T(8,128)S(1)}, f32[4,54,128]{2,1,0:T(8,128)S(1)}, u32[]{:S(2)}, u32[]{:S(2)}) collective-permute-start(f32[4,54,128]{2,1,0:T(8,128)S(1)} %get-tuple-element.66), channel_id=1, source_target_pairs={{0,12},{1,13},{2,14},{3,15},{4,8},{5,9},{6,10},{7,11},{8,4},{9,5},... | collective-permute-start | bytes 331784 | tf_op jit(solution)/shard_map/ppermute | solution.py:394
  29.8 7.8 %collective-permute-start.10 = (f32[4,54,128]{2,1,0:T(8,128)S(1)}, f32[4,54,128]{2,1,0:T(8,128)S(1)}, u32[]{:S(2)}, u32[]{:S(2)}) collective-permute-start(f32[4,54,128]{2,1,0:T(8,128)S(1)} %get-tuple-element.67), channel_id=1, source_target_pairs={{0,4},{1,5},{2,6},{3,7},{4,0},{5,1},{6,2},{7,3},{8,12},{9,13},{10,... | collective-permute-start | bytes 331784 | tf_op jit(solution)/shard_map/ppermute | solution.py:394
  31.5 7.3 %collective-permute-start.11 = (f32[4,54,128]{2,1,0:T(8,128)S(1)}, f32[4,54,128]{2,1,0:T(8,128)S(1)}, u32[]{:S(2)}, u32[]{:S(2)}) collective-permute-start(f32[4,54,128]{2,1,0:T(8,128)S(1)} %get-tuple-element.68), channel_id=1, source_target_pairs={{0,8},{1,9},{2,10},{3,11},{4,12},{5,13},{6,14},{7,15},{8,0},{9,1},... | collective-permute-start | bytes 331784 | tf_op jit(solution)/shard_map/ppermute | solution.py:394
  38.9 4.5 %collective-permute-start.12 = (f32[78,128]{1,0:T(8,128)S(1)}, f32[78,128]{1,0:T(8,128)S(1)}, u32[]{:S(2)}, u32[]{:S(2)}) collective-permute-start(f32[78,128]{1,0:T(8,128)S(1)} %pad_maximum_fusion), channel_id=1, source_target_pairs={{0,2},{1,3},{2,0},{3,1},{4,6},{5,7},{6,4},{7,5},{8,10},{9,11},{10,... | collective-permute-start | bytes 119816 | tf_op jit(solution)/shard_map/ppermute | solution.py:394
  40.4 4.9 %collective-permute-start.14 = (f32[1,54,128]{2,1,0:T(8,128)S(1)}, f32[1,54,128]{2,1,0:T(8,128)S(1)}, u32[]{:S(2)}, u32[]{:S(2)}) collective-permute-start(f32[1,54,128]{2,1,0:T(8,128)S(1)} %get-tuple-element.69), channel_id=1, source_target_pairs={{0,16},{1,17},{2,18},{3,19},{4,20},{5,21},{6,22},{7,23},{8,24},{9,... | collective-permute-start | bytes 82952 | tf_op jit(solution)/shard_map/ppermute | solution.py:394
  40.8 5.7 %collective-permute-start.13 = (f32[1,54,128]{2,1,0:T(8,128)S(1)}, f32[1,54,128]{2,1,0:T(8,128)S(1)}, u32[]{:S(2)}, u32[]{:S(2)}) collective-permute-start(f32[1,54,128]{2,1,0:T(8,128)S(1)} %get-tuple-element.70), channel_id=1, source_target_pairs={{0,18},{1,19},{2,16},{3,17},{4,22},{5,23},{6,20},{7,21},{8,26},{9,... | collective-permute-start | bytes 82952 | tf_op jit(solution)/shard_map/ppermute | solution.py:394

commit v4 on v3

--- a/solution.py
+++ b/solution.py
@@ -60,17 +60,114 @@
     return lax.dot_general(a, b, (((1,), (1,)), ((), ())), preferred_element_type=f32)
 
 
-def totals_kernel(count_hbm, sens, held, raw, count, sems, count_sem):
+def three_parts(value):
+    upper = value.astype(bf16).astype(f32)
+    middle = (value - upper).astype(bf16).astype(f32)
+    return upper, middle, value - upper - middle
+
+
+def fill_tables(
+    count, weight, nodes, bucket, low_hot, pair_hot, hot, ones_hot, factor_weight, me, spots
+):
+    bits = len(spots)
+    inner = (NODES >> bits).bit_length() - 1
+    node = nodes[...]
+    other = (node >> inner) ^ me
+    label = node & ((1 << inner) - 1)
+    for i in range(bits):
+        label = label + ((other >> i) & 1) * spots[i]
+    low = label & (LOW - 1)
+    high = label >> (LOW.bit_length() - 1)
+    for i in range(node.shape[1] // BLOCK):
+        part = slice(i * BLOCK, (i + 1) * BLOCK)
+        here = lax.broadcasted_iota(jnp.int32, (LOW, BLOCK), 0) == low[:, part]
+        low_hot[:, part] = jnp.where(here, 1.0, 0.0).astype(bf16)
+        row = lax.broadcasted_iota(jnp.int32, (2 * GROUP, BLOCK), 0)
+        away = high[:, part] - jnp.where(row < GROUP, 0, 1)
+        slot = lax.broadcasted_iota(jnp.int32, (2 * GROUP, BLOCK), 1)
+        away = jnp.where(slot < count[i], away, -1)
+        for p in range(HIGH // 2):
+            pair_hot[p, :, part] = jnp.where(away == 2 * p, 1.0, 0.0).astype(bf16)
+    width = bucket.shape[1]
+    column = lax.rem(lax.broadcasted_iota(jnp.int32, (1, width), 1), TENORS)
+    row = lax.broadcasted_iota(jnp.int32, (GROUP, width), 0)
+    every = row == bucket
+    by_tenor = [jnp.where(every & (column == m), 1.0, 0.0) for m in range(TENORS)]
+    fill = [jnp.zeros((8, width), f32)]
+    hot[...] = jnp.concatenate(by_tenor + fill, 0).astype(bf16)
+    every = [jnp.where(every, 1.0, 0.0)]
+    ones_hot[...] = jnp.concatenate(by_tenor[:-1] + every + fill, 0).astype(bf16)
+    total = jnp.zeros((1, width), f32)
+    for b in range(BUCKETS):
+        total = jnp.where(bucket == b, weight[b], total)
+    factor_weight[...] = total
+
+
+def totals_kernel(
+    count_hbm,
+    weight_hbm,
+    nodes_hbm,
+    buckets_hbm,
+    sens,
+    held,
+    raw,
+    low_hot,
+    pair_hot,
+    hot,
+    ones_hot,
+    factor_weight,
+    count,
+    weight,
+    nodes,
+    buckets,
+    bucket,
+    sems,
+    small_sems,
+    *,
+    spots,
+    factor_size,
+):
     width, trades = sens.shape
     pieces = [(start, min(PIECE, width - start)) for start in range(0, width, PIECE)]
-    counting = pltpu.make_async_copy(count_hbm, count, count_sem)
-    counting.start()
+    small = []
+    for i, (source, target) in enumerate(
+        [(count_hbm, count), (weight_hbm, weight), (nodes_hbm, nodes), (buckets_hbm, buckets)]
+    ):
+        small.append(pltpu.make_async_copy(source, target, small_sems.at[i]))
+        small[-1].start()
     copies = []
     for i, (start, rows) in enumerate(pieces):
         part = pl.ds(start, rows)
         copies.append(pltpu.make_async_copy(sens.at[part], held.at[part], sems.at[i]))
-        copies[-1].start()
-    counting.wait()
+    copies[0].start()
+    for copy in small:
+        copy.wait()
+    for copy in copies[1:]:
+        copy.start()
+    f = lax.axis_index("factor")
+    me = lax.axis_index("trade") * factor_size + f
+    for i in range(factor_size):
+
+        @pl.when(f == i)
+        def _(i=i):
+            first, off = divmod(i * width, LANES)
+            last = -(-(off + width) // LANES) + first
+            row = jnp.concatenate([buckets[r : r + 1] for r in range(first, last)], 1)
+            bucket[...] = row[:, off : off + width]
+
+    fill_tables(
+        count,
+        weight,
+        nodes,
+        bucket[...],
+        low_hot,
+        pair_hot,
+        hot,
+        ones_hot,
+        factor_weight,
+        me,
+        spots,
+    )
     ones = jnp.ones((16, 3 * LANES), bf16)
 
     def run(tiles):
@@ -85,11 +182,7 @@
                 j = i % chains
                 totals[j] = part if totals[j] is None else totals[j] + part
             value = sum(totals[1:], totals[0])
-            upper = value.astype(bf16)
-            value = value - upper.astype(f32)
-            middle = value.astype(bf16)
-            lower = (value - middle.astype(f32)).astype(bf16)
-            parts = jnp.concatenate([upper, middle, lower], 1)
+            parts = jnp.concatenate(three_parts(value), 1).astype(bf16)
             raw[:, start : start + rows] = dot_t(ones, parts)[:1]
 
     full = count[0] == BLOCK
@@ -107,67 +200,6 @@
         run(tiles)
 
 
-def tables_kernel(
-    count,
-    weight,
-    own,
-    nodes,
-    buckets,
-    low_hot,
-    pair_hot,
-    tenor_hot,
-    factor_weight,
-    tenor,
-    passed,
-    mine,
-    *,
-    spots,
-    factor_size,
-):
-    passed[...] = own[...]
-    f = lax.axis_index("factor")
-    me = lax.axis_index("trade") * factor_size + f
-    bits = len(spots)
-    inner = (NODES >> bits).bit_length() - 1
-    node = nodes[...]
-    other = (node >> inner) ^ me
-    label = node & ((1 << inner) - 1)
-    for i in range(bits):
-        label = label + ((other >> i) & 1) * spots[i]
-    low = label & (LOW - 1)
-    high = label >> (LOW.bit_length() - 1)
-    trades = node.shape[1]
-    for start in range(0, trades, 512):
-        part = pl.ds(start, 512)
-        here = lax.broadcasted_iota(jnp.int32, (LOW, 512), 0) == low[:, start : start + 512]
-        low_hot[:, part] = jnp.where(here, 1.0, 0.0).astype(bf16)
-        row = lax.broadcasted_iota(jnp.int32, (2 * GROUP, 512), 0)
-        away = high[:, start : start + 512] - jnp.where(row < GROUP, 0, 1)
-        slot = lax.broadcasted_iota(jnp.int32, (2 * GROUP, 512), 1)
-        away = jnp.where(slot < count[start // BLOCK], away, -1)
-        for p in range(HIGH // 2):
-            pair_hot[p, :, part] = jnp.where(away == 2 * p, 1.0, 0.0).astype(bf16)
-    width = own.shape[1]
-    for i in range(factor_size):
-
-        @pl.when(f == i)
-        def _(i=i):
-            mine[...] = buckets[:, i * width : (i + 1) * width]
-
-    bucket = mine[...]
-    place = lax.broadcasted_iota(jnp.int32, (1, width), 1)
-    column = lax.rem(place, TENORS)
-    tenor[...] = column
-    row = lax.broadcasted_iota(jnp.int32, (GROUP, width), 0)
-    for m in range(TENORS):
-        hot = (row == bucket) & (column == m)
-        tenor_hot[GROUP * m : GROUP * (m + 1), :] = jnp.where(hot, 1.0, 0.0)
-    total = jnp.zeros((1, width), f32)
-    for b in range(BUCKETS):
-        total = jnp.where(bucket == b, weight[b], total)
-    factor_weight[...] = total
-
-
 def multiply(weights, held, product):
     for start in range(0, held.shape[1], BLOCK):
         part = pl.ds(start, BLOCK)
@@ -178,13 +210,9 @@
     return jnp.concatenate([value, value], 0).astype(bf16)
 
 
-def ones_kernel(own, tenor_hot, held, product, rounded, passed):
+def ones_kernel(own, ones_hot, held, product, rounded, passed):
     passed[...] = own[...]
-    hot = tenor_hot[...]
-    every = sum(hot[GROUP * m : GROUP * (m + 1)] for m in range(TENORS))
-    fill = jnp.zeros((8, held.shape[0]), f32)
-    hot = jnp.concatenate([hot[: GROUP * (TENORS - 1)], every, fill], 0).astype(bf16)
-    multiply(hot, held, product)
+    multiply(ones_hot[...], held, product)
     rounded[...] = twice(product[GROUP * (TENORS - 1) : GROUP * TENORS])
 
 
@@ -204,10 +232,10 @@
 
 
 def weights_kernel(*refs):
-    *raws, factor_weight, tenor, tenor_hot, spread, sums = refs
-    width = tenor.shape[1]
+    *raws, factor_weight, hot, ones_hot, spread, sums = refs
+    width = factor_weight.shape[1]
     weighted = factor_weight[...] * sum(r[...] for r in raws)
-    own_tenor = tenor[...]
+    own_tenor = lax.rem(lax.broadcasted_iota(jnp.int32, (1, width), 1), TENORS)
     name = weighted
     for d in range(1, TENORS):
         zeros = jnp.zeros((1, d), f32)
@@ -216,25 +244,21 @@
         name = name + jnp.where(own_tenor < TENORS - d, after, 0.0)
         name = name + jnp.where(own_tenor >= d, before, 0.0)
     near = float(LEVELS[0, 1] - LEVELS[0, 3]) * name + float(SAME_BOTH[0]) * weighted
-    hot = tenor_hot[:GROUP, :]
-    for m in range(1, TENORS):
-        hot = hot + tenor_hot[GROUP * m : GROUP * (m + 1), :]
-    full = jnp.concatenate([hot * weighted, hot * near], 0)
+    every = ones_hot[GROUP * (TENORS - 1) : GROUP * TENORS].astype(f32)
+    full = jnp.concatenate([every * weighted, every * near], 0)
     upper = full.astype(bf16).astype(f32)
     fill = jnp.zeros((32, width), f32)
     spread[...] = jnp.concatenate([upper, full - upper, fill], 0).astype(bf16)
     lane = lax.broadcasted_iota(jnp.int32, (GROUP, LANES), 1)
-    out = jnp.zeros((GROUP, LANES), f32)
-    square = jnp.zeros((GROUP, 1), f32)
+    square = jnp.sum(every * (weighted * weighted), 1, keepdims=True)
+    out = jnp.where(lane == TENORS, square, 0.0)
+    first = jnp.where(own_tenor == 0, name, 0.0)
+    names = jnp.sum(every * (first * first), 1, keepdims=True)
+    out = jnp.where(lane == TENORS + 1, names, out)
+    by_tenor = hot[...].astype(f32) * weighted
     for m in range(TENORS):
-        hot = tenor_hot[GROUP * m : GROUP * (m + 1), :]
-        part = hot * weighted
-        out = jnp.where(lane == m, jnp.sum(part, 1, keepdims=True), out)
-        square = square + jnp.sum(part * weighted, 1, keepdims=True)
-        if m == 0:
-            names = jnp.sum(hot * (name * name), 1, keepdims=True)
-    out = jnp.where(lane == TENORS, square, out)
-    out = jnp.where(lane == TENORS + 1, names, out)
+        part = jnp.sum(by_tenor[GROUP * m : GROUP * (m + 1)], 1, keepdims=True)
+        out = jnp.where(lane == m, part, out)
     sums[...] = out
 
 
@@ -395,7 +419,7 @@
 
     over_factor = list(range(1, factor_bits))
     over_trade = list(range(factor_bits, bits))
-    groups = [over_trade[:2], over_factor[:1] + over_trade[2:3]]
+    groups = [over_factor[:1] + over_trade[:1], over_trade[1:3]]
     groups += [[b] for b in over_factor[1:] + over_trade[3:]]
     order = [0] + sum(groups, [])
     places = [7, 11, 10, 9, 8, 6, 5, 4, 3, 2, 1, 0]
@@ -403,48 +427,47 @@
     for i, bit in enumerate(order):
         spots[bit] = 1 << places[i]
 
-    by_factor = pltpu.with_memory_space_constraint(sensitivity.T, pltpu.HBM)
-    held, raw = call(
-        totals_kernel,
-        (pltpu.VMEM((width, trade_rows), bf16), shape(1, width)),
-        [ANY, ANY],
-        (VMEM, VMEM),
+    def in_hbm(x):
+        return pltpu.with_memory_space_constraint(x, pltpu.HBM)
+
+    rows = pltpu.VMEM((GROUP, trade_rows), f32)
+    multiplied = pltpu.VMEM((128, trade_rows), f32)
+    rounded = pltpu.VMEM((2 * GROUP, trade_rows), bf16)
+    lines = (factor_bucket.shape[0] // LANES, LANES)
+    held, raw, low_hot, pair_hot, hot, ones_hot, factor_weight = call(
+        functools.partial(totals_kernel, spots=spots, factor_size=factor_size),
+        (
+            pltpu.VMEM((width, trade_rows), bf16),
+            shape(1, width),
+            pltpu.VMEM((LOW, trade_rows), bf16),
+            pltpu.VMEM((HIGH // 2, 2 * GROUP, trade_rows), bf16),
+            pltpu.VMEM((128, width), bf16),
+            pltpu.VMEM((128, width), bf16),
+            pltpu.VMEM((1, width), f32),
+        ),
+        [ANY] * 5,
+        (VMEM,) * 7,
         "totals",
         scratch=[
             pltpu.SMEM(block_count.shape, jnp.int32),
+            pltpu.SMEM(risk_weight.shape, f32),
+            pltpu.VMEM((1, trade_rows), jnp.int32),
+            pltpu.VMEM(lines, jnp.int32),
+            pltpu.VMEM((1, width), jnp.int32),
             pltpu.SemaphoreType.DMA((-(-width // PIECE),)),
-            pltpu.SemaphoreType.DMA,
+            pltpu.SemaphoreType.DMA((4,)),
         ],
         flops=10**7,
-    )(pltpu.with_memory_space_constraint(block_count, pltpu.HBM), by_factor)
-
-    rows = pltpu.VMEM((GROUP, trade_rows), f32)
-    multiplied = pltpu.VMEM((128, trade_rows), f32)
-    rounded = pltpu.VMEM((2 * GROUP, trade_rows), bf16)
+    )(
+        in_hbm(block_count),
+        in_hbm(risk_weight),
+        in_hbm(trade_node[None, :]),
+        in_hbm(factor_bucket.reshape(lines)),
+        in_hbm(sensitivity.T),
+    )
+
     trade_mask = [1 << b for b in over_trade]
     other = exchange(raw, trade_mask[0])
-    low_hot, pair_hot, tenor_hot, factor_weight, tenor, raw = call(
-        functools.partial(tables_kernel, spots=spots, factor_size=factor_size),
-        (
-            pltpu.VMEM((LOW, trade_rows), bf16),
-            pltpu.VMEM((HIGH // 2, 2 * GROUP, trade_rows), bf16),
-            pltpu.VMEM((GROUP * TENORS, width), f32),
-            pltpu.VMEM((1, width), f32),
-            pltpu.VMEM((1, width), jnp.int32),
-            shape(1, width),
-        ),
-        [SMEM, SMEM, VMEM, VMEM, VMEM],
-        (VMEM,) * 6,
-        "tables",
-        scratch=[pltpu.VMEM((1, width), jnp.int32)],
-        flops=10**7,
-    )(block_count, risk_weight, raw, trade_node[None, :], factor_bucket[None, :])
-
-    for mask in trade_mask[3:]:
-        raw = raw + other
-        other = exchange(raw, mask)
-    raw = raw + other
-    others = [exchange(raw, mask) for mask in (trade_mask[1] + trade_mask[2], trade_mask[2], trade_mask[1])]
     tenors, ones_rounded, raw = call(
         ones_kernel,
         (multiplied, rounded, shape(1, width)),
@@ -452,7 +475,14 @@
         (VMEM,) * 3,
         "ones",
         flops=2 * 128 * width * trade_rows,
-    )(raw, tenor_hot, held)
+    )(raw, ones_hot, held)
+    raw = raw + other
+    for mask in trade_mask[3:]:
+        raw = raw + exchange(raw, mask)
+    others = [
+        exchange(raw, mask)
+        for mask in (trade_mask[1], trade_mask[2], trade_mask[1] + trade_mask[2])
+    ]
 
     all_nodes = (HIGH, 3 * BUCKETS, LOW // 2)
     nodes_flops = 2 * 512 * trade_rows * LOW
@@ -472,7 +502,7 @@
         (VMEM, VMEM),
         "weights",
         flops=10**6,
-    )(raw, *others, factor_weight, tenor, tenor_hot)
+    )(raw, *others, factor_weight, hot, ones_hot)
 
     others = [exchange(sums, mask) for mask in range(1, factor_size)]
     near, weighted_rounded = call(
@@ -537,7 +567,7 @@
             message = chunks[c]
             if len(part) == 1 and part[0] in over_factor:
                 trade_send, trade_keep = jnp.split(trade_keep + trade_more, 2, 0)[::-1]
-                if message.shape[2] == LANES:
+                if message.shape[2] == LANES and i > 0:
                     cut = trade_send.shape[0] * trade_send.shape[1]
                     message = jnp.concatenate(
                         [trade_send.reshape(cut, LANES), message.reshape(-1, LANES)], 0

time: 47.3 us -> 46.2 us (0.977)
  Pallas kernels: 16.6 us -> 15.7 us
  waiting for transfers between devices: 11.3 us -> 10.5 us
  starting transfers between devices: 18.3 us -> 18.9 us
    pallas_call x2 -> x1, Pallas kernels: 6.66 us -> 5.75 us  [local(): call(functools.partial(totals_kernel, spots=spots, factor_size=factor_siz...]
    ppermute x15 -> x16, waiting for transfers between devices: 11.3 us -> 10.5 us  [exchange(): return lax.ppermute(x, AXES, [(o, o ^ mask) for o in range(devices)])]
    ppermute x15 -> x16, starting transfers between devices: 18.3 us -> 18.9 us  [exchange(): return lax.ppermute(x, AXES, [(o, o ^ mask) for o in range(devices)])]
  transfers between devices with their start and end apart: 15 -> 16, of which waited for: 8 -> 6; matrix products, arithmetic and copies ran while one was open for 0% -> 0% of each run, Pallas kernels for 19% -> 16%
where the time goes in v4:
time: 46.2 us; the launch traced here: 46.1 us
  starting transfers between devices  18.9 us (41%)
  Pallas kernels  15.7 us (34%)
  waiting for transfers between devices  10.5 us (23%)
  between operations  0.95 us (2%)
    ppermute x16, starting transfers between devices, exchange(): return lax.ppermute(x, AXES, [(o, o ^ mask) for o in range(devices)])  18.9 us
    ppermute x16, waiting for transfers between devices, exchange(): return lax.ppermute(x, AXES, [(o, o ^ mask) for o in range(devices)])  10.5 us
    pallas_call x1, Pallas kernels, local(): call(functools.partial(totals_kernel, spots=spots, factor_size=factor_siz...  5.75 us
    pallas_call x1, Pallas kernels, local(): call(ones_kernel, (multiplied, rounded, shape(1, width)), [VMEM] * 3, (VM...  2.11 us
    pallas_call x1, Pallas kernels, local(): call(spread_kernel, (multiplied, rounded), [VMEM] * 2, (VMEM,) * 2, 'spre...  2.08 us
    pallas_call x1, Pallas kernels, local(): call(product_nodes_kernel, (rows, shape(GROUP, LANES), pltpu.VMEM(all_nod...  1.29 us
    pallas_call x1, Pallas kernels, local(): call(functools.partial(capital_kernel, trades_total=trades_total, parts=f...  1.2 us
    pallas_call x1, Pallas kernels, local(): call(ones_nodes_kernel, (pltpu.VMEM(all_nodes, f32), pltpu.VMEM(all_nodes...  1.07 us
  transfers between devices with their start and end apart: 16, of which 6 were waited for; matrix products, arithmetic and copies ran while one was open for 0% of the time, Pallas kernels for 16%

profile of v4, /device:TPU:0, one launch (start us, length us, event | category | flops | bytes accessed | tf_op | source)
XLA Modules:
  0.0 46.1 jit_solution(9917693582532509583)
XLA Ops:
  0.6 5.8 %totals.1 = (bf16[1600,4096]{1,0:T(8,128)(2,1)S(1)}, f32[1,1600]{1,0:T(1,128)S(1)}, bf16[256,4096]{1,0:T(8,128)(2,1)S(1)}, bf16[8,48,4096]{2,1,0:T(8,128)(2,1)S(...) custom-call(s32[8]{0:T(128)} %count.1, f32[18]{0:T(128)} %weight.1, ...), custom_call_target="tpu_custom_call" | custom-call | flops 10000000 | bytes 65536 | tf_op jit(solution)/shard_map/totals/pallas_call | solution.py:437
  6.4 2.8 %collective-permute-start = (f32[1,1600]{1,0:T(1,128)S(1)}, f32[1,1600]{1,0:T(1,128)S(1)}, u32[]{:S(2)}, u32[]{:S(2)}) collective-permute-start(f32[1,1600]{1,0:T(1,128)S(1)} %get-tuple-element.35.own), channel_id=1, source_target_pairs={{0,4},{1,5},{2,6},{3,7},{4,0},{5,1},{6,2},{7,3},{8,12},{9,13},{10,... | collective-permute-start | bytes 19208 | tf_op jit(solution)/shard_map/ppermute | solution.py:418
  9.2 2.1 %ones.1 = (f32[128,4096]{1,0:T(8,128)S(1)}, bf16[48,4096]{1,0:T(8,128)(2,1)S(1)}, f32[1,1600]{1,0:T(1,128)S(1)}) custom-call(f32[1,1600]{1,0:T(1,128)S(1)} %get-tuple-element.35.own, bf16[128,1600]{1,0:T(8,128)(2,1)S(1)} %get-tuple-element.36.ones_hot.refs_6_, bf16[1600,4096]{1,0:T(8,128)(2,1)S(1)} %get-tuple-element.37.held), custom_call_target="tpu_custom_call" | custom-call | flops 1677721600 | bytes 65536 | tf_op jit(solution)/shard_map/ones/pallas_call | solution.py:471
  11.3 0.0 collective-permute-done
  11.4 3.7 %collective-permute-start.3 = (f32[1,1600]{1,0:T(1,128)S(1)}, f32[1,1600]{1,0:T(1,128)S(1)}, u32[]{:S(2)}, u32[]{:S(2)}) collective-permute-start(f32[1,1600]{1,0:T(1,128)S(1)} %add.15.own), channel_id=1, source_target_pairs={{0,24},{1,25},{2,26},{3,27},{4,28},{5,29},{6,30},{7,31},{8,16},{9,... | collective-permute-start | bytes 19208 | tf_op jit(solution)/shard_map/ppermute | solution.py:418
  15.0 0.0 collective-permute-start.2
  15.0 0.8 %collective-permute-start.1 = (f32[1,1600]{1,0:T(1,128)S(1)}, f32[1,1600]{1,0:T(1,128)S(1)}, u32[]{:S(2)}, u32[]{:S(2)}) collective-permute-start(f32[1,1600]{1,0:T(1,128)S(1)} %add.15.own), channel_id=1, source_target_pairs={{0,8},{1,9},{2,10},{3,11},{4,12},{5,13},{6,14},{7,15},{8,0},{9,1},... | collective-permute-start | bytes 19208 | tf_op jit(solution)/shard_map/ppermute | solution.py:418
  15.8 1.1 %ones_nodes.1 = (f32[16,54,128]{2,1,0:T(8,128)S(1)}, f32[16,54,128]{2,1,0:T(8,128)S(1)}, f32[1,1600]{1,0:T(1,128)S(1)}) custom-call(f32[1,1600]{1,0:T(1,128)S(1)} %add.15.own, bf16[48,4096]{1,0:T(8,128)(2,1)S(1)} %get-tuple-element.39.rounded, bf16[256,4096]{1,0:T(8,128)(2,1)S(1)} %get-tuple-element.40.low_hot.refs_6_, ...), custom_call_target="tpu_custom_call" | custom-call | flops 1073741824 | bytes 65536 | tf_op jit(solution)/shard_map/ones_nodes/pallas_call | solution.py:489
  16.9 0.0 collective-permute-done.3.refs_3_
  16.9 2.7 %collective-permute-done.2.refs_2_ = f32[1,1600]{1,0:T(1,128)S(1)} collective-permute-done((f32[1,1600]{1,0:T(1,128)S(1)}, f32[1,1600]{1,0:T(1,128)S(1)}, u32[]{:S(2)}, u32[]{:S(2)}) %collective-permute-start.2) | collective-permute-done | bytes 6432 | tf_op jit(solution)/shard_map/ppermute | solution.py:418
  19.6 0.0 collective-permute-done.1.refs_1_
  19.6 0.4 weights.1
  20.0 0.1 collective-permute-start.6
  20.0 1.6 %collective-permute-start.5 = (f32[24,128]{1,0:T(8,128)S(1)}, f32[24,128]{1,0:T(8,128)S(1)}, u32[]{:S(2)}, u32[]{:S(2)}) collective-permute-start(f32[24,128]{1,0:T(8,128)S(1)} %get-tuple-element.45.refs_0_), channel_id=1, source_target_pairs={{0,2},{1,3},{2,0},{3,1},{4,6},{5,7},{6,4},{7,5},{8,10},{9,11},{10,... | collective-permute-start | bytes 36872 | tf_op jit(solution)/shard_map/ppermute | solution.py:418
  21.6 0.3 collective-permute-start.4
  21.9 2.1 %spread.1 = (f32[128,4096]{1,0:T(8,128)S(1)}, bf16[48,4096]{1,0:T(8,128)(2,1)S(1)}) custom-call(bf16[128,1600]{1,0:T(8,128)(2,1)S(1)} %get-tuple-element.46.spread, bf16[1600,4096]{1,0:T(8,128)(2,1)S(1)} %get-tuple-element.37.held), custom_call_target="tpu_custom_call" | custom-call | flops 1677721600 | bytes 65536 | tf_op jit(solution)/shard_map/spread/pallas_call | solution.py:508
  24.0 1.1 %weighted_nodes.1 = (f32[16,54,128]{2,1,0:T(8,128)S(1)}, f32[16,54,128]{2,1,0:T(8,128)S(1)}) custom-call(bf16[48,4096]{1,0:T(8,128)(2,1)S(1)} %get-tuple-element.49.rounded, bf16[256,4096]{1,0:T(8,128)(2,1)S(1)} %get-tuple-element.40.low_hot.refs_6_, ...), custom_call_target="tpu_custom_call", output_to_operand_aliasing={{0}: (3, {}), {1}: (4, {})} | custom-call | flops 1073741824 | bytes 65536 | tf_op jit(solution)/shard_map/weighted_nodes/pallas_call | solution.py:516
  25.0 0.0 collective-permute-done.6.refs_3_
  25.0 0.0 collective-permute-done.5.refs_2_
  25.0 0.0 collective-permute-done.4.refs_1_
  25.0 0.0 copy-start
  25.1 0.0 copy-start.1
  25.1 0.0 copy-start.2
  25.1 1.3 %product_nodes.1 = (f32[24,4096]{1,0:T(8,128)S(1)}, f32[24,128]{1,0:T(8,128)S(1)}, f32[16,54,128]{2,1,0:T(8,128)S(1)}, f32[16,54,128]{2,1,0:T(8,128)S(1)}) custom-call(f32[24,128]{1,0:T(8,128)S(1)} %get-tuple-element.45.refs_0_, f32[24,128]{1,0:T(8,128)S(1)} %collective-permute-done.4.refs_1_, ...), custom_call_target="tpu_custom_call", output_to_operand_aliasing={{2}: (8, {}), {3}: (9, {})} | custom-call | flops 1073741824 | bytes 65536 | tf_op jit(solution)/shard_map/product_nodes/pallas_call | solution.py:526
  26.4 0.3 collective-permute-start.7
  26.7 0.0 copy-done
  26.7 0.0 copy-done.1
  26.7 0.0 copy-done.2
  26.7 1.2 %capital.1 = (f32[2,24,128]{2,1,0:T(8,128)S(1)}, f32[2,24,128]{2,1,0:T(8,128)S(1)}, f32[3,54,128]{2,1,0:T(8,128)S(1)}, f32[8,128]{1,0:T(8,128)S(1)}) custom-call(s32[8]{0:T(128)S(1)} %copy-done, f32[18]{0:T(128)S(1)} %copy-done.1, f32[18]{0:T(128)S(1)} %copy-done.2, f32[24,128]{1,0:T(8,128)S(1)} %get-tuple-element.54.total, ...), custom_call_target="tpu_custom_call" | custom-call | flops 10000000 | bytes 65536 | tf_op jit(solution)/shard_map/capital/pallas_call | solution.py:539
  27.9 0.4 collective-permute-done.7.more
  28.3 0.1 join.1
  28.3 2.5 %collective-permute-start.10 = (f32[4,54,128]{2,1,0:T(8,128)S(1)}, f32[4,54,128]{2,1,0:T(8,128)S(1)}, u32[]{:S(2)}, u32[]{:S(2)}) collective-permute-start(f32[4,54,128]{2,1,0:T(8,128)S(1)} %get-tuple-element.64), channel_id=1, source_target_pairs={{0,6},{1,7},{2,4},{3,5},{4,2},{5,3},{6,0},{7,1},{8,14},{9,15},{10,... | collective-permute-start | bytes 331784 | tf_op jit(solution)/shard_map/ppermute | solution.py:418
  30.8 0.5 %collective-permute-start.11 = (f32[4,54,128]{2,1,0:T(8,128)S(1)}, f32[4,54,128]{2,1,0:T(8,128)S(1)}, u32[]{:S(2)}, u32[]{:S(2)}) collective-permute-start(f32[4,54,128]{2,1,0:T(8,128)S(1)} %get-tuple-element.65), channel_id=1, source_target_pairs={{0,2},{1,3},{2,0},{3,1},{4,6},{5,7},{6,4},{7,5},{8,10},{9,11},{10,... | collective-permute-start | bytes 331784 | tf_op jit(solution)/shard_map/ppermute | solution.py:418
  31.4 0.5 %collective-permute-start.12 = (f32[4,54,128]{2,1,0:T(8,128)S(1)}, f32[4,54,128]{2,1,0:T(8,128)S(1)}, u32[]{:S(2)}, u32[]{:S(2)}) collective-permute-start(f32[4,54,128]{2,1,0:T(8,128)S(1)} %get-tuple-element.66), channel_id=1, source_target_pairs={{0,4},{1,5},{2,6},{3,7},{4,0},{5,1},{6,2},{7,3},{8,12},{9,13},{10,... | collective-permute-start | bytes 331784 | tf_op jit(solution)/shard_map/ppermute | solution.py:418
  31.9 0.0 collective-permute-start.8
  31.9 1.2 %collective-permute-done.8 = f32[2,24,128]{2,1,0:T(8,128)S(1)} collective-permute-done((f32[2,24,128]{2,1,0:T(8,128)S(1)}, f32[2,24,128]{2,1,0:T(8,128)S(1)}, u32[]{:S(2)}, u32[]{:S(2)}) %collective-permute-start.8) | collective-permute-done | bytes 24608 | tf_op jit(solution)/shard_map/ppermute | solution.py:418
  33.1 2.2 %collective-permute-done.10 = f32[4,54,128]{2,1,0:T(8,128)S(1)} collective-permute-done((f32[4,54,128]{2,1,0:T(8,128)S(1)}, f32[4,54,128]{2,1,0:T(8,128)S(1)}, u32[]{:S(2)}, u32[]{:S(2)}) %collective-permute-start.10) | collective-permute-done | bytes 110624 | tf_op jit(solution)/shard_map/ppermute | solution.py:418
  35.3 1.8 %collective-permute-done.11 = f32[4,54,128]{2,1,0:T(8,128)S(1)} collective-permute-done((f32[4,54,128]{2,1,0:T(8,128)S(1)}, f32[4,54,128]{2,1,0:T(8,128)S(1)}, u32[]{:S(2)}, u32[]{:S(2)}) %collective-permute-start.11) | collective-permute-done | bytes 110624 | tf_op jit(solution)/shard_map/ppermute | solution.py:418
  37.1 0.0 collective-permute-done.12
  37.1 2.1 %collective-permute-start.15 = (f32[1,54,128]{2,1,0:T(8,128)S(1)}, f32[1,54,128]{2,1,0:T(8,128)S(1)}, u32[]{:S(2)}, u32[]{:S(2)}) collective-permute-start(f32[1,54,128]{2,1,0:T(8,128)S(1)} %get-tuple-element.67), channel_id=1, source_target_pairs={{0,16},{1,17},{2,18},{3,19},{4,20},{5,21},{6,22},{7,23},{8,24},{9,... | collective-permute-start | bytes 82952 | tf_op jit(solution)/shard_map/ppermute | solution.py:418
  39.2 0.0 collective-permute-start.14
  39.2 2.4 %collective-permute-start.13 = (f32[1,54,128]{2,1,0:T(8,128)S(1)}, f32[1,54,128]{2,1,0:T(8,128)S(1)}, u32[]{:S(2)}, u32[]{:S(2)}) collective-permute-start(f32[1,54,128]{2,1,0:T(8,128)S(1)} %get-tuple-element.69), channel_id=1, source_target_pairs={{0,24},{1,25},{2,26},{3,27},{4,28},{5,29},{6,30},{7,31},{8,16},{9,... | collective-permute-start | bytes 82952 | tf_op jit(solution)/shard_map/ppermute | solution.py:418
  41.6 1.4 %collective-permute-start.9 = (f32[1,24,128]{2,1,0:T(8,128)S(1)}, f32[1,24,128]{2,1,0:T(8,128)S(1)}, u32[]{:S(2)}, u32[]{:S(2)}) collective-permute-start(f32[1,24,128]{2,1,0:T(8,128)S(1)} %get-tuple-element.71), channel_id=1, source_target_pairs={{0,2},{1,3},{2,0},{3,1},{4,6},{5,7},{6,4},{7,5},{8,10},{9,11},{10,... | collective-permute-start | bytes 36872 | tf_op jit(solution)/shard_map/ppermute | solution.py:418
  43.0 2.3 %collective-permute-done.9 = f32[1,24,128]{2,1,0:T(8,128)S(1)} collective-permute-done((f32[1,24,128]{2,1,0:T(8,128)S(1)}, f32[1,24,128]{2,1,0:T(8,128)S(1)}, u32[]{:S(2)}, u32[]{:S(2)}) %collective-permute-start.9) | collective-permute-done | bytes 12320 | tf_op jit(solution)/shard_map/ppermute | solution.py:418
  45.3 0.0 collective-permute-done.15
  45.3 0.0 collective-permute-done.14
  45.3 0.0 collective-permute-done.13
  45.3 0.7 %finish.1 = (f32[3]{0:T(128)}, f32[3,1024]{1,0:T(4,128)}, f32[3,18,128]{2,1,0:T(8,128)}) custom-call(f32[3,54,128]{2,1,0:T(8,128)S(1)} %get-tuple-element.56.mix, f32[8,128]{1,0:T(8,128)S(1)} %get-tuple-element.57.capital, f32[24,128]{1,0:T(8,128)S(1)} %get-tuple-element.72.trade_keep, f32[24,128]{1,0:T(8,128)S(1)} %bitcast.14, ...), custom_call_target="tpu_custom_call" | custom-call | flops 1000000 | bytes 65536 | tf_op jit(solution)/shard_map/finish/pallas_call | solution.py:586
  (5 shorter events, 0.1 us)
Async XLA Ops:
  6.4 4.9 %collective-permute-start = (f32[1,1600]{1,0:T(1,128)S(1)}, f32[1,1600]{1,0:T(1,128)S(1)}, u32[]{:S(2)}, u32[]{:S(2)}) collective-permute-start(f32[1,1600]{1,0:T(1,128)S(1)} %get-tuple-element.35.own), channel_id=1, source_target_pairs={{0,4},{1,5},{2,6},{3,7},{4,0},{5,1},{6,2},{7,3},{8,12},{9,13},{10,... | collective-permute-start | bytes 19208 | tf_op jit(solution)/shard_map/ppermute | solution.py:418
  11.4 5.5 %collective-permute-start.3 = (f32[1,1600]{1,0:T(1,128)S(1)}, f32[1,1600]{1,0:T(1,128)S(1)}, u32[]{:S(2)}, u32[]{:S(2)}) collective-permute-start(f32[1,1600]{1,0:T(1,128)S(1)} %add.15.own), channel_id=1, source_target_pairs={{0,24},{1,25},{2,26},{3,27},{4,28},{5,29},{6,30},{7,31},{8,16},{9,... | collective-permute-start | bytes 19208 | tf_op jit(solution)/shard_map/ppermute | solution.py:418
  15.0 4.5 %collective-permute-start.2 = (f32[1,1600]{1,0:T(1,128)S(1)}, f32[1,1600]{1,0:T(1,128)S(1)}, u32[]{:S(2)}, u32[]{:S(2)}) collective-permute-start(f32[1,1600]{1,0:T(1,128)S(1)} %add.15.own), channel_id=1, source_target_pairs={{0,16},{1,17},{2,18},{3,19},{4,20},{5,21},{6,22},{7,23},{8,24},{9,... | collective-permute-start | bytes 19208 | tf_op jit(solution)/shard_map/ppermute | solution.py:418
  15.0 4.5 %collective-permute-start.1 = (f32[1,1600]{1,0:T(1,128)S(1)}, f32[1,1600]{1,0:T(1,128)S(1)}, u32[]{:S(2)}, u32[]{:S(2)}) collective-permute-start(f32[1,1600]{1,0:T(1,128)S(1)} %add.15.own), channel_id=1, source_target_pairs={{0,8},{1,9},{2,10},{3,11},{4,12},{5,13},{6,14},{7,15},{8,0},{9,1},... | collective-permute-start | bytes 19208 | tf_op jit(solution)/shard_map/ppermute | solution.py:418
  20.0 5.1 %collective-permute-start.6 = (f32[24,128]{1,0:T(8,128)S(1)}, f32[24,128]{1,0:T(8,128)S(1)}, u32[]{:S(2)}, u32[]{:S(2)}) collective-permute-start(f32[24,128]{1,0:T(8,128)S(1)} %get-tuple-element.45.refs_0_), channel_id=1, source_target_pairs={{0,3},{1,2},{2,1},{3,0},{4,7},{5,6},{6,5},{7,4},{8,11},{9,10},{10,... | collective-permute-start | bytes 36872 | tf_op jit(solution)/shard_map/ppermute | solution.py:418
  20.0 5.0 %collective-permute-start.5 = (f32[24,128]{1,0:T(8,128)S(1)}, f32[24,128]{1,0:T(8,128)S(1)}, u32[]{:S(2)}, u32[]{:S(2)}) collective-permute-start(f32[24,128]{1,0:T(8,128)S(1)} %get-tuple-element.45.refs_0_), channel_id=1, source_target_pairs={{0,2},{1,3},{2,0},{3,1},{4,6},{5,7},{6,4},{7,5},{8,10},{9,11},{10,... | collective-permute-start | bytes 36872 | tf_op jit(solution)/shard_map/ppermute | solution.py:418
  21.6 3.5 %collective-permute-start.4 = (f32[24,128]{1,0:T(8,128)S(1)}, f32[24,128]{1,0:T(8,128)S(1)}, u32[]{:S(2)}, u32[]{:S(2)}) collective-permute-start(f32[24,128]{1,0:T(8,128)S(1)} %get-tuple-element.45.refs_0_), channel_id=1, source_target_pairs={{0,1},{1,0},{2,3},{3,2},{4,5},{5,4},{6,7},{7,6},{8,9},{9,8},{10,11... | collective-permute-start | bytes 36872 | tf_op jit(solution)/shard_map/ppermute | solution.py:418
  25.0 1.6 %copy-start = (s32[8]{0:T(128)S(1)}, s32[8]{0:T(128)}, u32[]{:S(2)}) copy-start(s32[8]{0:T(128)} %count.1) | copy-start | bytes 100
  25.1 1.6 %copy-start.1 = (f32[18]{0:T(128)S(1)}, f32[18]{0:T(128)}, u32[]{:S(2)}) copy-start(f32[18]{0:T(128)} %weight.1) | copy-start | bytes 220
  25.1 1.6 %copy-start.2 = (f32[18]{0:T(128)S(1)}, f32[18]{0:T(128)}, u32[]{:S(2)}) copy-start(f32[18]{0:T(128)} %load.1) | copy-start | bytes 220
  26.4 1.9 %collective-permute-start.7 = (f32[16,54,128]{2,1,0:T(8,128)S(1)}, f32[16,54,128]{2,1,0:T(8,128)S(1)}, u32[]{:S(2)}, u32[]{:S(2)}) collective-permute-start(f32[16,54,128]{2,1,0:T(8,128)S(1)} %get-tuple-element.61), channel_id=1, source_target_pairs={{0,1},{1,0},{2,3},{3,2},{4,5},{5,4},{6,7},{7,6},{8,9},{9,8},{10,11... | collective-permute-start | bytes 1327112 | tf_op jit(solution)/shard_map/ppermute | solution.py:418
  28.3 6.9 %collective-permute-start.10 = (f32[4,54,128]{2,1,0:T(8,128)S(1)}, f32[4,54,128]{2,1,0:T(8,128)S(1)}, u32[]{:S(2)}, u32[]{:S(2)}) collective-permute-start(f32[4,54,128]{2,1,0:T(8,128)S(1)} %get-tuple-element.64), channel_id=1, source_target_pairs={{0,6},{1,7},{2,4},{3,5},{4,2},{5,3},{6,0},{7,1},{8,14},{9,15},{10,... | collective-permute-start | bytes 331784 | tf_op jit(solution)/shard_map/ppermute | solution.py:418
  30.8 6.2 %collective-permute-start.11 = (f32[4,54,128]{2,1,0:T(8,128)S(1)}, f32[4,54,128]{2,1,0:T(8,128)S(1)}, u32[]{:S(2)}, u32[]{:S(2)}) collective-permute-start(f32[4,54,128]{2,1,0:T(8,128)S(1)} %get-tuple-element.65), channel_id=1, source_target_pairs={{0,2},{1,3},{2,0},{3,1},{4,6},{5,7},{6,4},{7,5},{8,10},{9,11},{10,... | collective-permute-start | bytes 331784 | tf_op jit(solution)/shard_map/ppermute | solution.py:418
  31.4 5.7 %collective-permute-start.12 = (f32[4,54,128]{2,1,0:T(8,128)S(1)}, f32[4,54,128]{2,1,0:T(8,128)S(1)}, u32[]{:S(2)}, u32[]{:S(2)}) collective-permute-start(f32[4,54,128]{2,1,0:T(8,128)S(1)} %get-tuple-element.66), channel_id=1, source_target_pairs={{0,4},{1,5},{2,6},{3,7},{4,0},{5,1},{6,2},{7,3},{8,12},{9,13},{10,... | collective-permute-start | bytes 331784 | tf_op jit(solution)/shard_map/ppermute | solution.py:418
  31.9 1.2 %collective-permute-start.8 = (f32[2,24,128]{2,1,0:T(8,128)S(1)}, f32[2,24,128]{2,1,0:T(8,128)S(1)}, u32[]{:S(2)}, u32[]{:S(2)}) collective-permute-start(f32[2,24,128]{2,1,0:T(8,128)S(1)} %get-tuple-element.62), channel_id=1, source_target_pairs={{0,1},{1,0},{2,3},{3,2},{4,5},{5,4},{6,7},{7,6},{8,9},{9,8},{10,11... | collective-permute-start | bytes 73736 | tf_op jit(solution)/shard_map/ppermute | solution.py:418
  37.1 8.2 %collective-permute-start.15 = (f32[1,54,128]{2,1,0:T(8,128)S(1)}, f32[1,54,128]{2,1,0:T(8,128)S(1)}, u32[]{:S(2)}, u32[]{:S(2)}) collective-permute-start(f32[1,54,128]{2,1,0:T(8,128)S(1)} %get-tuple-element.67), channel_id=1, source_target_pairs={{0,16},{1,17},{2,18},{3,19},{4,20},{5,21},{6,22},{7,23},{8,24},{9,... | collective-permute-start | bytes 82952 | tf_op jit(solution)/shard_map/ppermute | solution.py:418
  39.2 6.1 %collective-permute-start.14 = (f32[1,54,128]{2,1,0:T(8,128)S(1)}, f32[1,54,128]{2,1,0:T(8,128)S(1)}, u32[]{:S(2)}, u32[]{:S(2)}) collective-permute-start(f32[1,54,128]{2,1,0:T(8,128)S(1)} %get-tuple-element.68), channel_id=1, source_target_pairs={{0,8},{1,9},{2,10},{3,11},{4,12},{5,13},{6,14},{7,15},{8,0},{9,1},... | collective-permute-start | bytes 82952 | tf_op jit(solution)/shard_map/ppermute | solution.py:418
  39.2 6.1 %collective-permute-start.13 = (f32[1,54,128]{2,1,0:T(8,128)S(1)}, f32[1,54,128]{2,1,0:T(8,128)S(1)}, u32[]{:S(2)}, u32[]{:S(2)}) collective-permute-start(f32[1,54,128]{2,1,0:T(8,128)S(1)} %get-tuple-element.69), channel_id=1, source_target_pairs={{0,24},{1,25},{2,26},{3,27},{4,28},{5,29},{6,30},{7,31},{8,16},{9,... | collective-permute-start | bytes 82952 | tf_op jit(solution)/shard_map/ppermute | solution.py:418
  41.6 3.7 %collective-permute-start.9 = (f32[1,24,128]{2,1,0:T(8,128)S(1)}, f32[1,24,128]{2,1,0:T(8,128)S(1)}, u32[]{:S(2)}, u32[]{:S(2)}) collective-permute-start(f32[1,24,128]{2,1,0:T(8,128)S(1)} %get-tuple-element.71), channel_id=1, source_target_pairs={{0,2},{1,3},{2,0},{3,1},{4,6},{5,7},{6,4},{7,5},{8,10},{9,11},{10,... | collective-permute-start | bytes 36872 | tf_op jit(solution)/shard_map/ppermute | solution.py:418

commit v5 on v4

--- a/solution.py
+++ b/solution.py
@@ -222,8 +222,9 @@
     out = dot_t(masked, low_hot[...])
     for h in range(HIGH):
         rows = out[GROUP * h : GROUP * h + BUCKETS]
-        keep[h, first : first + BUCKETS] = rows[:, : LOW // 2]
-        send[h, first : first + BUCKETS] = rows[:, LOW // 2 :]
+        place = 3 * BUCKETS * h + first
+        keep[place : place + BUCKETS] = rows[:, : LOW // 2]
+        send[place : place + BUCKETS] = rows[:, LOW // 2 :]
 
 
 def ones_nodes_kernel(own, rounded, low_hot, pair_hot, keep, send, passed):
@@ -297,6 +298,15 @@
     for c, chunk in enumerate(chunks):
         part = pl.ds(c * size, size)
         chunk[...] = keep[part] + more[part]
+
+
+def middle_kernel(*refs, count):
+    pieces, chunks = refs[:count], refs[count:]
+    total = sum(p[...] for p in pieces)
+    for c, chunk in enumerate(chunks):
+        for j in range(chunk.shape[0]):
+            place = 3 * BUCKETS * (c * chunk.shape[0] + j)
+            chunk[j] = total[place : place + 3 * BUCKETS]
 
 
 def capital_kernel(
@@ -484,7 +494,7 @@
         for mask in (trade_mask[1], trade_mask[2], trade_mask[1] + trade_mask[2])
     ]
 
-    all_nodes = (HIGH, 3 * BUCKETS, LOW // 2)
+    all_nodes = (HIGH * 3 * BUCKETS, LOW // 2)
     nodes_flops = 2 * 512 * trade_rows * LOW
     keep, send, raw = call(
         ones_nodes_kernel,
@@ -548,7 +558,7 @@
     count = 1 << len(groups[0])
     trade_send, *chunks = call(
         join_kernel,
-        (trade_shape,) + (shape(HIGH // count, 3 * BUCKETS, LOW // 2),) * count,
+        (trade_shape,) + (shape(HIGH // count * 3 * BUCKETS, LOW // 2),) * count,
         [VMEM] * 3,
         (VMEM,) * (1 + count),
         "join",
@@ -557,7 +567,7 @@
     trade_more = exchange(trade_send, 1)
     for i, group in enumerate(groups):
         count = 1 << len(group)
-        if i > 0:
+        if i > 1:
             axis = 0 if keep.shape[0] > 1 else 2
             chunks = jnp.split(keep, count, axis)
         pieces = [chunks[0]]
@@ -567,7 +577,7 @@
             message = chunks[c]
             if len(part) == 1 and part[0] in over_factor:
                 trade_send, trade_keep = jnp.split(trade_keep + trade_more, 2, 0)[::-1]
-                if message.shape[2] == LANES and i > 0:
+                if i > 0 and message.shape[2] == LANES:
                     cut = trade_send.shape[0] * trade_send.shape[1]
                     message = jnp.concatenate(
                         [trade_send.reshape(cut, LANES), message.reshape(-1, LANES)], 0
@@ -581,7 +591,18 @@
             else:
                 message = exchange(message, mask)
             pieces.append(message)
-        if i + 1 < len(groups):
+        if i == 0:
+            next_count = 1 << len(groups[1])
+            chunk = shape(HIGH // count // next_count, 3 * BUCKETS, LANES)
+            chunks = call(
+                functools.partial(middle_kernel, count=count),
+                (chunk,) * next_count,
+                [VMEM] * count,
+                (VMEM,) * next_count,
+                "middle",
+                flops=10**6,
+            )(*pieces)
+        elif i + 1 < len(groups):
             keep = sum(pieces[1:], pieces[0])
     return call(
         functools.partial(finish_kernel, scale=1.0 / trades_total**0.5),

time: 46.2 us -> 46.1 us (level)
  transfers between devices with their start and end apart: 16 -> 16, of which waited for: 6 -> 7; matrix products, arithmetic and copies ran while one was open for 0% -> 0% of each run, Pallas kernels for 16% -> 16%
where the time goes in v5:
time: 46.1 us; the launch traced here: 45.8 us
  starting transfers between devices  18.9 us (41%)
  Pallas kernels  15.6 us (34%)
  waiting for transfers between devices  10.4 us (23%)
  between operations  0.94 us (2%)
    ppermute x16, starting transfers between devices, exchange(): return lax.ppermute(x, AXES, [(o, o ^ mask) for o in range(devices)])  18.9 us
    ppermute x16, waiting for transfers between devices, exchange(): return lax.ppermute(x, AXES, [(o, o ^ mask) for o in range(devices)])  10.4 us
    pallas_call x1, Pallas kernels, local(): call(functools.partial(totals_kernel, spots=spots, factor_size=factor_siz...  5.75 us
    pallas_call x1, Pallas kernels, local(): call(ones_kernel, (multiplied, rounded, shape(1, width)), [VMEM] * 3, (VM...  2.11 us
    pallas_call x1, Pallas kernels, local(): call(spread_kernel, (multiplied, rounded), [VMEM] * 2, (VMEM,) * 2, 'spre...  2.08 us
    pallas_call x1, Pallas kernels, local(): call(product_nodes_kernel, (rows, shape(GROUP, LANES), pltpu.VMEM(all_nod...  1.29 us
    pallas_call x1, Pallas kernels, local(): call(functools.partial(capital_kernel, trades_total=trades_total, parts=f...  1.2 us
    pallas_call x1, Pallas kernels, local(): call(weighted_nodes_kernel, (pltpu.VMEM(all_nodes, f32),) * 2, [VMEM] * 5...  1.01 us
  transfers between devices with their start and end apart: 16, of which 7 were waited for; matrix products, arithmetic and copies ran while one was open for 0% of the time, Pallas kernels for 16%

profile of v5, /device:TPU:0, one launch (start us, length us, event | category | flops | bytes accessed | tf_op | source)
XLA Modules:
  0.0 45.8 jit_solution(2697256543432186111)
XLA Ops:
  0.6 5.8 %totals.1 = (bf16[1600,4096]{1,0:T(8,128)(2,1)S(1)}, f32[1,1600]{1,0:T(1,128)S(1)}, bf16[256,4096]{1,0:T(8,128)(2,1)S(1)}, bf16[8,48,4096]{2,1,0:T(8,128)(2,1)S(...) custom-call(s32[8]{0:T(128)} %count.1, f32[18]{0:T(128)} %weight.1, ...), custom_call_target="tpu_custom_call" | custom-call | flops 10000000 | bytes 65536 | tf_op jit(solution)/shard_map/totals/pallas_call | solution.py:447
  6.4 2.8 %collective-permute-start = (f32[1,1600]{1,0:T(1,128)S(1)}, f32[1,1600]{1,0:T(1,128)S(1)}, u32[]{:S(2)}, u32[]{:S(2)}) collective-permute-start(f32[1,1600]{1,0:T(1,128)S(1)} %get-tuple-element.39.own), channel_id=1, source_target_pairs={{0,4},{1,5},{2,6},{3,7},{4,0},{5,1},{6,2},{7,3},{8,12},{9,13},{10,... | collective-permute-start | bytes 19208 | tf_op jit(solution)/shard_map/ppermute | solution.py:428
  9.2 2.1 %ones.1 = (f32[128,4096]{1,0:T(8,128)S(1)}, bf16[48,4096]{1,0:T(8,128)(2,1)S(1)}, f32[1,1600]{1,0:T(1,128)S(1)}) custom-call(f32[1,1600]{1,0:T(1,128)S(1)} %get-tuple-element.39.own, bf16[128,1600]{1,0:T(8,128)(2,1)S(1)} %get-tuple-element.40.ones_hot.refs_6_, bf16[1600,4096]{1,0:T(8,128)(2,1)S(1)} %get-tuple-element.41.held), custom_call_target="tpu_custom_call" | custom-call | flops 1677721600 | bytes 65536 | tf_op jit(solution)/shard_map/ones/pallas_call | solution.py:481
  11.3 0.0 collective-permute-done
  11.4 3.7 %collective-permute-start.3 = (f32[1,1600]{1,0:T(1,128)S(1)}, f32[1,1600]{1,0:T(1,128)S(1)}, u32[]{:S(2)}, u32[]{:S(2)}) collective-permute-start(f32[1,1600]{1,0:T(1,128)S(1)} %add.6.own), channel_id=1, source_target_pairs={{0,24},{1,25},{2,26},{3,27},{4,28},{5,29},{6,30},{7,31},{8,16},{9,... | collective-permute-start | bytes 19208 | tf_op jit(solution)/shard_map/ppermute | solution.py:428
  15.0 0.0 collective-permute-start.2
  15.0 0.8 %collective-permute-start.1 = (f32[1,1600]{1,0:T(1,128)S(1)}, f32[1,1600]{1,0:T(1,128)S(1)}, u32[]{:S(2)}, u32[]{:S(2)}) collective-permute-start(f32[1,1600]{1,0:T(1,128)S(1)} %add.6.own), channel_id=1, source_target_pairs={{0,8},{1,9},{2,10},{3,11},{4,12},{5,13},{6,14},{7,15},{8,0},{9,1},... | collective-permute-start | bytes 19208 | tf_op jit(solution)/shard_map/ppermute | solution.py:428
  15.8 1.0 %ones_nodes.1 = (f32[864,128]{1,0:T(8,128)S(1)}, f32[864,128]{1,0:T(8,128)S(1)}, f32[1,1600]{1,0:T(1,128)S(1)}) custom-call(f32[1,1600]{1,0:T(1,128)S(1)} %add.6.own, bf16[48,4096]{1,0:T(8,128)(2,1)S(1)} %get-tuple-element.43.rounded, bf16[256,4096]{1,0:T(8,128)(2,1)S(1)} %get-tuple-element.44.low_hot.refs_6_, ...), custom_call_target="tpu_custom_call" | custom-call | flops 1073741824 | bytes 65536 | tf_op jit(solution)/shard_map/ones_nodes/pallas_call | solution.py:499
  16.8 0.1 collective-permute-done.3.refs_3_
  16.9 2.6 %collective-permute-done.2.refs_2_ = f32[1,1600]{1,0:T(1,128)S(1)} collective-permute-done((f32[1,1600]{1,0:T(1,128)S(1)}, f32[1,1600]{1,0:T(1,128)S(1)}, u32[]{:S(2)}, u32[]{:S(2)}) %collective-permute-start.2) | collective-permute-done | bytes 6432 | tf_op jit(solution)/shard_map/ppermute | solution.py:428
  19.6 0.0 collective-permute-done.1.refs_1_
  19.6 0.4 weights.1
  20.0 0.1 collective-permute-start.6
  20.0 1.6 %collective-permute-start.5 = (f32[24,128]{1,0:T(8,128)S(1)}, f32[24,128]{1,0:T(8,128)S(1)}, u32[]{:S(2)}, u32[]{:S(2)}) collective-permute-start(f32[24,128]{1,0:T(8,128)S(1)} %get-tuple-element.49.refs_0_), channel_id=1, source_target_pairs={{0,2},{1,3},{2,0},{3,1},{4,6},{5,7},{6,4},{7,5},{8,10},{9,11},{10,... | collective-permute-start | bytes 36872 | tf_op jit(solution)/shard_map/ppermute | solution.py:428
  21.6 0.3 collective-permute-start.4
  21.9 2.1 %spread.1 = (f32[128,4096]{1,0:T(8,128)S(1)}, bf16[48,4096]{1,0:T(8,128)(2,1)S(1)}) custom-call(bf16[128,1600]{1,0:T(8,128)(2,1)S(1)} %get-tuple-element.50.spread, bf16[1600,4096]{1,0:T(8,128)(2,1)S(1)} %get-tuple-element.41.held), custom_call_target="tpu_custom_call" | custom-call | flops 1677721600 | bytes 65536 | tf_op jit(solution)/shard_map/spread/pallas_call | solution.py:518
  24.0 1.0 %weighted_nodes.1 = (f32[864,128]{1,0:T(8,128)S(1)}, f32[864,128]{1,0:T(8,128)S(1)}) custom-call(bf16[48,4096]{1,0:T(8,128)(2,1)S(1)} %get-tuple-element.53.rounded, bf16[256,4096]{1,0:T(8,128)(2,1)S(1)} %get-tuple-element.44.low_hot.refs_6_, ...), custom_call_target="tpu_custom_call", output_to_operand_aliasing={{0}: (3, {}), {1}: (4, {})} | custom-call | flops 1073741824 | bytes 65536 | tf_op jit(solution)/shard_map/weighted_nodes/pallas_call | solution.py:526
  25.0 0.0 collective-permute-done.6.refs_3_
  25.0 0.0 collective-permute-done.5.refs_2_
  25.0 0.0 collective-permute-done.4.refs_1_
  25.0 0.0 copy-start
  25.0 0.0 copy-start.1
  25.0 0.0 copy-start.2
  25.0 1.3 %product_nodes.1 = (f32[24,4096]{1,0:T(8,128)S(1)}, f32[24,128]{1,0:T(8,128)S(1)}, f32[864,128]{1,0:T(8,128)S(1)}, f32[864,128]{1,0:T(8,128)S(1)}) custom-call(f32[24,128]{1,0:T(8,128)S(1)} %get-tuple-element.49.refs_0_, f32[24,128]{1,0:T(8,128)S(1)} %collective-permute-done.4.refs_1_, ...), custom_call_target="tpu_custom_call", output_to_operand_aliasing={{2}: (8, {}), {3}: (9, {})} | custom-call | flops 1073741824 | bytes 65536 | tf_op jit(solution)/shard_map/product_nodes/pallas_call | solution.py:536
  26.3 0.3 collective-permute-start.7
  26.6 0.0 copy-done
  26.6 0.0 copy-done.1
  26.6 0.0 copy-done.2
  26.6 1.2 %capital.1 = (f32[2,24,128]{2,1,0:T(8,128)S(1)}, f32[2,24,128]{2,1,0:T(8,128)S(1)}, f32[3,54,128]{2,1,0:T(8,128)S(1)}, f32[8,128]{1,0:T(8,128)S(1)}) custom-call(s32[8]{0:T(128)S(1)} %copy-done, f32[18]{0:T(128)S(1)} %copy-done.1, f32[18]{0:T(128)S(1)} %copy-done.2, f32[24,128]{1,0:T(8,128)S(1)} %get-tuple-element.58.total, ...), custom_call_target="tpu_custom_call" | custom-call | flops 10000000 | bytes 65536 | tf_op jit(solution)/shard_map/capital/pallas_call | solution.py:549
  27.8 0.4 collective-permute-done.7.more
  28.3 2.5 %collective-permute-start.10 = (f32[216,128]{1,0:T(8,128)S(1)}, f32[216,128]{1,0:T(8,128)S(1)}, u32[]{:S(2)}, u32[]{:S(2)}) collective-permute-start(f32[216,128]{1,0:T(8,128)S(1)} %get-tuple-element.68), channel_id=1, source_target_pairs={{0,6},{1,7},{2,4},{3,5},{4,2},{5,3},{6,0},{7,1},{8,14},{9,15},{10,... | collective-permute-start | bytes 331784 | tf_op jit(solution)/shard_map/ppermute | solution.py:428
  30.7 0.5 %collective-permute-start.11 = (f32[216,128]{1,0:T(8,128)S(1)}, f32[216,128]{1,0:T(8,128)S(1)}, u32[]{:S(2)}, u32[]{:S(2)}) collective-permute-start(f32[216,128]{1,0:T(8,128)S(1)} %get-tuple-element.69), channel_id=1, source_target_pairs={{0,2},{1,3},{2,0},{3,1},{4,6},{5,7},{6,4},{7,5},{8,10},{9,11},{10,... | collective-permute-start | bytes 331784 | tf_op jit(solution)/shard_map/ppermute | solution.py:428
  31.3 0.5 %collective-permute-start.12 = (f32[216,128]{1,0:T(8,128)S(1)}, f32[216,128]{1,0:T(8,128)S(1)}, u32[]{:S(2)}, u32[]{:S(2)}) collective-permute-start(f32[216,128]{1,0:T(8,128)S(1)} %get-tuple-element.70), channel_id=1, source_target_pairs={{0,4},{1,5},{2,6},{3,7},{4,0},{5,1},{6,2},{7,3},{8,12},{9,13},{10,... | collective-permute-start | bytes 331784 | tf_op jit(solution)/shard_map/ppermute | solution.py:428
  31.8 0.0 collective-permute-start.8
  31.8 1.2 %collective-permute-done.8 = f32[2,24,128]{2,1,0:T(8,128)S(1)} collective-permute-done((f32[2,24,128]{2,1,0:T(8,128)S(1)}, f32[2,24,128]{2,1,0:T(8,128)S(1)}, u32[]{:S(2)}, u32[]{:S(2)}) %collective-permute-start.8) | collective-permute-done | bytes 24608 | tf_op jit(solution)/shard_map/ppermute | solution.py:428
  33.0 2.1 %collective-permute-done.10.refs_1_ = f32[216,128]{1,0:T(8,128)S(1)} collective-permute-done((f32[216,128]{1,0:T(8,128)S(1)}, f32[216,128]{1,0:T(8,128)S(1)}, u32[]{:S(2)}, u32[]{:S(2)}) %collective-permute-start.10) | collective-permute-done | bytes 110624 | tf_op jit(solution)/shard_map/ppermute | solution.py:428
  35.1 1.7 %collective-permute-done.11.refs_2_ = f32[216,128]{1,0:T(8,128)S(1)} collective-permute-done((f32[216,128]{1,0:T(8,128)S(1)}, f32[216,128]{1,0:T(8,128)S(1)}, u32[]{:S(2)}, u32[]{:S(2)}) %collective-permute-start.11) | collective-permute-done | bytes 110624 | tf_op jit(solution)/shard_map/ppermute | solution.py:428
  36.8 0.0 collective-permute-done.12.refs_3_
  36.8 1.5 %collective-permute-start.13 = (f32[1,54,128]{2,1,0:T(8,128)S(1)}, f32[1,54,128]{2,1,0:T(8,128)S(1)}, u32[]{:S(2)}, u32[]{:S(2)}) collective-permute-start(f32[1,54,128]{2,1,0:T(8,128)S(1)} %get-tuple-element.72), channel_id=1, source_target_pairs={{0,24},{1,25},{2,26},{3,27},{4,28},{5,29},{6,30},{7,31},{8,16},{9,... | collective-permute-start | bytes 82952 | tf_op jit(solution)/shard_map/ppermute | solution.py:428
  38.4 1.1 %collective-permute-start.14 = (f32[1,54,128]{2,1,0:T(8,128)S(1)}, f32[1,54,128]{2,1,0:T(8,128)S(1)}, u32[]{:S(2)}, u32[]{:S(2)}) collective-permute-start(f32[1,54,128]{2,1,0:T(8,128)S(1)} %get-tuple-element.73), channel_id=1, source_target_pairs={{0,8},{1,9},{2,10},{3,11},{4,12},{5,13},{6,14},{7,15},{8,0},{9,1},... | collective-permute-start | bytes 82952 | tf_op jit(solution)/shard_map/ppermute | solution.py:428
  39.5 1.8 %collective-permute-start.15 = (f32[1,54,128]{2,1,0:T(8,128)S(1)}, f32[1,54,128]{2,1,0:T(8,128)S(1)}, u32[]{:S(2)}, u32[]{:S(2)}) collective-permute-start(f32[1,54,128]{2,1,0:T(8,128)S(1)} %get-tuple-element.74), channel_id=1, source_target_pairs={{0,16},{1,17},{2,18},{3,19},{4,20},{5,21},{6,22},{7,23},{8,24},{9,... | collective-permute-start | bytes 82952 | tf_op jit(solution)/shard_map/ppermute | solution.py:428
  41.3 1.4 %collective-permute-start.9 = (f32[1,24,128]{2,1,0:T(8,128)S(1)}, f32[1,24,128]{2,1,0:T(8,128)S(1)}, u32[]{:S(2)}, u32[]{:S(2)}) collective-permute-start(f32[1,24,128]{2,1,0:T(8,128)S(1)} %get-tuple-element.75), channel_id=1, source_target_pairs={{0,2},{1,3},{2,0},{3,1},{4,6},{5,7},{6,4},{7,5},{8,10},{9,11},{10,... | collective-permute-start | bytes 36872 | tf_op jit(solution)/shard_map/ppermute | solution.py:428
  42.7 2.3 %collective-permute-done.9 = f32[1,24,128]{2,1,0:T(8,128)S(1)} collective-permute-done((f32[1,24,128]{2,1,0:T(8,128)S(1)}, f32[1,24,128]{2,1,0:T(8,128)S(1)}, u32[]{:S(2)}, u32[]{:S(2)}) %collective-permute-start.9) | collective-permute-done | bytes 12320 | tf_op jit(solution)/shard_map/ppermute | solution.py:428
  45.0 0.0 collective-permute-done.13
  45.0 0.0 collective-permute-done.14
  45.0 0.0 collective-permute-done.15
  45.0 0.7 %finish.1 = (f32[3]{0:T(128)}, f32[3,1024]{1,0:T(4,128)}, f32[3,18,128]{2,1,0:T(8,128)}) custom-call(f32[3,54,128]{2,1,0:T(8,128)S(1)} %get-tuple-element.60.mix, f32[8,128]{1,0:T(8,128)S(1)} %get-tuple-element.61.capital, f32[24,128]{1,0:T(8,128)S(1)} %get-tuple-element.76.trade_keep, f32[24,128]{1,0:T(8,128)S(1)} %bitcast.14, f32[54,128]{1,0:T(8,128)S(1)} %bitcast.10, ...), custom_call_target="tpu_custom_call" | custom-call | flops 1000000 | bytes 65536 | tf_op jit(solution)/shard_map/finish/pallas_call | solution.py:607
  (5 shorter events, 0.1 us)
Async XLA Ops:
  6.4 4.9 %collective-permute-start = (f32[1,1600]{1,0:T(1,128)S(1)}, f32[1,1600]{1,0:T(1,128)S(1)}, u32[]{:S(2)}, u32[]{:S(2)}) collective-permute-start(f32[1,1600]{1,0:T(1,128)S(1)} %get-tuple-element.39.own), channel_id=1, source_target_pairs={{0,4},{1,5},{2,6},{3,7},{4,0},{5,1},{6,2},{7,3},{8,12},{9,13},{10,... | collective-permute-start | bytes 19208 | tf_op jit(solution)/shard_map/ppermute | solution.py:428
  11.4 5.6 %collective-permute-start.3 = (f32[1,1600]{1,0:T(1,128)S(1)}, f32[1,1600]{1,0:T(1,128)S(1)}, u32[]{:S(2)}, u32[]{:S(2)}) collective-permute-start(f32[1,1600]{1,0:T(1,128)S(1)} %add.6.own), channel_id=1, source_target_pairs={{0,24},{1,25},{2,26},{3,27},{4,28},{5,29},{6,30},{7,31},{8,16},{9,... | collective-permute-start | bytes 19208 | tf_op jit(solution)/shard_map/ppermute | solution.py:428
  15.0 4.5 %collective-permute-start.2 = (f32[1,1600]{1,0:T(1,128)S(1)}, f32[1,1600]{1,0:T(1,128)S(1)}, u32[]{:S(2)}, u32[]{:S(2)}) collective-permute-start(f32[1,1600]{1,0:T(1,128)S(1)} %add.6.own), channel_id=1, source_target_pairs={{0,16},{1,17},{2,18},{3,19},{4,20},{5,21},{6,22},{7,23},{8,24},{9,... | collective-permute-start | bytes 19208 | tf_op jit(solution)/shard_map/ppermute | solution.py:428
  15.0 4.5 %collective-permute-start.1 = (f32[1,1600]{1,0:T(1,128)S(1)}, f32[1,1600]{1,0:T(1,128)S(1)}, u32[]{:S(2)}, u32[]{:S(2)}) collective-permute-start(f32[1,1600]{1,0:T(1,128)S(1)} %add.6.own), channel_id=1, source_target_pairs={{0,8},{1,9},{2,10},{3,11},{4,12},{5,13},{6,14},{7,15},{8,0},{9,1},... | collective-permute-start | bytes 19208 | tf_op jit(solution)/shard_map/ppermute | solution.py:428
  20.0 5.0 %collective-permute-start.6 = (f32[24,128]{1,0:T(8,128)S(1)}, f32[24,128]{1,0:T(8,128)S(1)}, u32[]{:S(2)}, u32[]{:S(2)}) collective-permute-start(f32[24,128]{1,0:T(8,128)S(1)} %get-tuple-element.49.refs_0_), channel_id=1, source_target_pairs={{0,3},{1,2},{2,1},{3,0},{4,7},{5,6},{6,5},{7,4},{8,11},{9,10},{10,... | collective-permute-start | bytes 36872 | tf_op jit(solution)/shard_map/ppermute | solution.py:428
  20.0 5.0 %collective-permute-start.5 = (f32[24,128]{1,0:T(8,128)S(1)}, f32[24,128]{1,0:T(8,128)S(1)}, u32[]{:S(2)}, u32[]{:S(2)}) collective-permute-start(f32[24,128]{1,0:T(8,128)S(1)} %get-tuple-element.49.refs_0_), channel_id=1, source_target_pairs={{0,2},{1,3},{2,0},{3,1},{4,6},{5,7},{6,4},{7,5},{8,10},{9,11},{10,... | collective-permute-start | bytes 36872 | tf_op jit(solution)/shard_map/ppermute | solution.py:428
  21.6 3.4 %collective-permute-start.4 = (f32[24,128]{1,0:T(8,128)S(1)}, f32[24,128]{1,0:T(8,128)S(1)}, u32[]{:S(2)}, u32[]{:S(2)}) collective-permute-start(f32[24,128]{1,0:T(8,128)S(1)} %get-tuple-element.49.refs_0_), channel_id=1, source_target_pairs={{0,1},{1,0},{2,3},{3,2},{4,5},{5,4},{6,7},{7,6},{8,9},{9,8},{10,11... | collective-permute-start | bytes 36872 | tf_op jit(solution)/shard_map/ppermute | solution.py:428
  25.0 1.6 %copy-start = (s32[8]{0:T(128)S(1)}, s32[8]{0:T(128)}, u32[]{:S(2)}) copy-start(s32[8]{0:T(128)} %count.1) | copy-start | bytes 100
  25.0 1.6 %copy-start.1 = (f32[18]{0:T(128)S(1)}, f32[18]{0:T(128)}, u32[]{:S(2)}) copy-start(f32[18]{0:T(128)} %weight.1) | copy-start | bytes 220
  25.0 1.6 %copy-start.2 = (f32[18]{0:T(128)S(1)}, f32[18]{0:T(128)}, u32[]{:S(2)}) copy-start(f32[18]{0:T(128)} %load.1) | copy-start | bytes 220
  26.3 1.9 %collective-permute-start.7 = (f32[864,128]{1,0:T(8,128)S(1)}, f32[864,128]{1,0:T(8,128)S(1)}, u32[]{:S(2)}, u32[]{:S(2)}) collective-permute-start(f32[864,128]{1,0:T(8,128)S(1)} %get-tuple-element.65), channel_id=1, source_target_pairs={{0,1},{1,0},{2,3},{3,2},{4,5},{5,4},{6,7},{7,6},{8,9},{9,8},{10,11... | collective-permute-start | bytes 1327112 | tf_op jit(solution)/shard_map/ppermute | solution.py:428
  28.3 6.9 %collective-permute-start.10 = (f32[216,128]{1,0:T(8,128)S(1)}, f32[216,128]{1,0:T(8,128)S(1)}, u32[]{:S(2)}, u32[]{:S(2)}) collective-permute-start(f32[216,128]{1,0:T(8,128)S(1)} %get-tuple-element.68), channel_id=1, source_target_pairs={{0,6},{1,7},{2,4},{3,5},{4,2},{5,3},{6,0},{7,1},{8,14},{9,15},{10,... | collective-permute-start | bytes 331784 | tf_op jit(solution)/shard_map/ppermute | solution.py:428
  30.7 6.1 %collective-permute-start.11 = (f32[216,128]{1,0:T(8,128)S(1)}, f32[216,128]{1,0:T(8,128)S(1)}, u32[]{:S(2)}, u32[]{:S(2)}) collective-permute-start(f32[216,128]{1,0:T(8,128)S(1)} %get-tuple-element.69), channel_id=1, source_target_pairs={{0,2},{1,3},{2,0},{3,1},{4,6},{5,7},{6,4},{7,5},{8,10},{9,11},{10,... | collective-permute-start | bytes 331784 | tf_op jit(solution)/shard_map/ppermute | solution.py:428
  31.3 5.5 %collective-permute-start.12 = (f32[216,128]{1,0:T(8,128)S(1)}, f32[216,128]{1,0:T(8,128)S(1)}, u32[]{:S(2)}, u32[]{:S(2)}) collective-permute-start(f32[216,128]{1,0:T(8,128)S(1)} %get-tuple-element.70), channel_id=1, source_target_pairs={{0,4},{1,5},{2,6},{3,7},{4,0},{5,1},{6,2},{7,3},{8,12},{9,13},{10,... | collective-permute-start | bytes 331784 | tf_op jit(solution)/shard_map/ppermute | solution.py:428
  31.8 1.2 %collective-permute-start.8 = (f32[2,24,128]{2,1,0:T(8,128)S(1)}, f32[2,24,128]{2,1,0:T(8,128)S(1)}, u32[]{:S(2)}, u32[]{:S(2)}) collective-permute-start(f32[2,24,128]{2,1,0:T(8,128)S(1)} %get-tuple-element.66), channel_id=1, source_target_pairs={{0,1},{1,0},{2,3},{3,2},{4,5},{5,4},{6,7},{7,6},{8,9},{9,8},{10,11... | collective-permute-start | bytes 73736 | tf_op jit(solution)/shard_map/ppermute | solution.py:428
  36.8 8.2 %collective-permute-start.13 = (f32[1,54,128]{2,1,0:T(8,128)S(1)}, f32[1,54,128]{2,1,0:T(8,128)S(1)}, u32[]{:S(2)}, u32[]{:S(2)}) collective-permute-start(f32[1,54,128]{2,1,0:T(8,128)S(1)} %get-tuple-element.72), channel_id=1, source_target_pairs={{0,24},{1,25},{2,26},{3,27},{4,28},{5,29},{6,30},{7,31},{8,16},{9,... | collective-permute-start | bytes 82952 | tf_op jit(solution)/shard_map/ppermute | solution.py:428
  38.4 6.6 %collective-permute-start.14 = (f32[1,54,128]{2,1,0:T(8,128)S(1)}, f32[1,54,128]{2,1,0:T(8,128)S(1)}, u32[]{:S(2)}, u32[]{:S(2)}) collective-permute-start(f32[1,54,128]{2,1,0:T(8,128)S(1)} %get-tuple-element.73), channel_id=1, source_target_pairs={{0,8},{1,9},{2,10},{3,11},{4,12},{5,13},{6,14},{7,15},{8,0},{9,1},... | collective-permute-start | bytes 82952 | tf_op jit(solution)/shard_map/ppermute | solution.py:428
  39.5 5.5 %collective-permute-start.15 = (f32[1,54,128]{2,1,0:T(8,128)S(1)}, f32[1,54,128]{2,1,0:T(8,128)S(1)}, u32[]{:S(2)}, u32[]{:S(2)}) collective-permute-start(f32[1,54,128]{2,1,0:T(8,128)S(1)} %get-tuple-element.74), channel_id=1, source_target_pairs={{0,16},{1,17},{2,18},{3,19},{4,20},{5,21},{6,22},{7,23},{8,24},{9,... | collective-permute-start | bytes 82952 | tf_op jit(solution)/shard_map/ppermute | solution.py:428
  41.3 3.7 %collective-permute-start.9 = (f32[1,24,128]{2,1,0:T(8,128)S(1)}, f32[1,24,128]{2,1,0:T(8,128)S(1)}, u32[]{:S(2)}, u32[]{:S(2)}) collective-permute-start(f32[1,24,128]{2,1,0:T(8,128)S(1)} %get-tuple-element.75), channel_id=1, source_target_pairs={{0,2},{1,3},{2,0},{3,1},{4,6},{5,7},{6,4},{7,5},{8,10},{9,11},{10,... | collective-permute-start | bytes 36872 | tf_op jit(solution)/shard_map/ppermute | solution.py:428

commit v6 on v5

--- a/solution.py
+++ b/solution.py
@@ -66,9 +66,7 @@
     return upper, middle, value - upper - middle
 
 
-def fill_tables(
-    count, weight, nodes, bucket, low_hot, pair_hot, hot, ones_hot, factor_weight, me, spots
-):
+def fill_labels(count, nodes, low_hot, pair_hot, me, spots):
     bits = len(spots)
     inner = (NODES >> bits).bit_length() - 1
     node = nodes[...]
@@ -88,6 +86,9 @@
         away = jnp.where(slot < count[i], away, -1)
         for p in range(HIGH // 2):
             pair_hot[p, :, part] = jnp.where(away == 2 * p, 1.0, 0.0).astype(bf16)
+
+
+def fill_buckets(weight, bucket, hot, ones_hot, factor_weight):
     width = bucket.shape[1]
     column = lax.rem(lax.broadcasted_iota(jnp.int32, (1, width), 1), TENORS)
     row = lax.broadcasted_iota(jnp.int32, (GROUP, width), 0)
@@ -106,32 +107,27 @@
 def totals_kernel(
     count_hbm,
     weight_hbm,
-    nodes_hbm,
     buckets_hbm,
     sens,
     held,
     raw,
-    low_hot,
-    pair_hot,
     hot,
     ones_hot,
     factor_weight,
     count,
     weight,
-    nodes,
     buckets,
     bucket,
     sems,
     small_sems,
     *,
-    spots,
     factor_size,
 ):
     width, trades = sens.shape
     pieces = [(start, min(PIECE, width - start)) for start in range(0, width, PIECE)]
     small = []
     for i, (source, target) in enumerate(
-        [(count_hbm, count), (weight_hbm, weight), (nodes_hbm, nodes), (buckets_hbm, buckets)]
+        [(count_hbm, count), (weight_hbm, weight), (buckets_hbm, buckets)]
     ):
         small.append(pltpu.make_async_copy(source, target, small_sems.at[i]))
         small[-1].start()
@@ -145,7 +141,6 @@
     for copy in copies[1:]:
         copy.start()
     f = lax.axis_index("factor")
-    me = lax.axis_index("trade") * factor_size + f
     for i in range(factor_size):
 
         @pl.when(f == i)
@@ -155,19 +150,7 @@
             row = jnp.concatenate([buckets[r : r + 1] for r in range(first, last)], 1)
             bucket[...] = row[:, off : off + width]
 
-    fill_tables(
-        count,
-        weight,
-        nodes,
-        bucket[...],
-        low_hot,
-        pair_hot,
-        hot,
-        ones_hot,
-        factor_weight,
-        me,
-        spots,
-    )
+    fill_buckets(weight, bucket[...], hot, ones_hot, factor_weight)
     ones = jnp.ones((16, 3 * LANES), bf16)
 
     def run(tiles):
@@ -227,8 +210,12 @@
         send[place : place + BUCKETS] = rows[:, LOW // 2 :]
 
 
-def ones_nodes_kernel(own, rounded, low_hot, pair_hot, keep, send, passed):
+def ones_nodes_kernel(
+    count, own, nodes, rounded, low_hot, pair_hot, keep, send, passed, *, spots, factor_size
+):
     passed[...] = own[...]
+    me = lax.axis_index("trade") * factor_size + lax.axis_index("factor")
+    fill_labels(count, nodes, low_hot, pair_hot, me, spots)
     sums_by_node(rounded, low_hot, pair_hot, BUCKETS, keep, send)
 
 
@@ -444,34 +431,30 @@
     multiplied = pltpu.VMEM((128, trade_rows), f32)
     rounded = pltpu.VMEM((2 * GROUP, trade_rows), bf16)
     lines = (factor_bucket.shape[0] // LANES, LANES)
-    held, raw, low_hot, pair_hot, hot, ones_hot, factor_weight = call(
-        functools.partial(totals_kernel, spots=spots, factor_size=factor_size),
+    held, raw, hot, ones_hot, factor_weight = call(
+        functools.partial(totals_kernel, factor_size=factor_size),
         (
             pltpu.VMEM((width, trade_rows), bf16),
             shape(1, width),
-            pltpu.VMEM((LOW, trade_rows), bf16),
-            pltpu.VMEM((HIGH // 2, 2 * GROUP, trade_rows), bf16),
             pltpu.VMEM((128, width), bf16),
             pltpu.VMEM((128, width), bf16),
             pltpu.VMEM((1, width), f32),
         ),
-        [ANY] * 5,
-        (VMEM,) * 7,
+        [ANY] * 4,
+        (VMEM,) * 5,
         "totals",
         scratch=[
             pltpu.SMEM(block_count.shape, jnp.int32),
             pltpu.SMEM(risk_weight.shape, f32),
-            pltpu.VMEM((1, trade_rows), jnp.int32),
             pltpu.VMEM(lines, jnp.int32),
             pltpu.VMEM((1, width), jnp.int32),
             pltpu.SemaphoreType.DMA((-(-width // PIECE),)),
-            pltpu.SemaphoreType.DMA((4,)),
+            pltpu.SemaphoreType.DMA((3,)),
         ],
         flops=10**7,
     )(
         in_hbm(block_count),
         in_hbm(risk_weight),
-        in_hbm(trade_node[None, :]),
         in_hbm(factor_bucket.reshape(lines)),
         in_hbm(sensitivity.T),
     )
@@ -496,14 +479,20 @@
 
     all_nodes = (HIGH * 3 * BUCKETS, LOW // 2)
     nodes_flops = 2 * 512 * trade_rows * LOW
-    keep, send, raw = call(
-        ones_nodes_kernel,
-        (pltpu.VMEM(all_nodes, f32), pltpu.VMEM(all_nodes, f32), shape(1, width)),
-        [VMEM] * 4,
-        (VMEM,) * 3,
+    low_hot, pair_hot, keep, send, raw = call(
+        functools.partial(ones_nodes_kernel, spots=spots, factor_size=factor_size),
+        (
+            pltpu.VMEM((LOW, trade_rows), bf16),
+            pltpu.VMEM((HIGH // 2, 2 * GROUP, trade_rows), bf16),
+            pltpu.VMEM(all_nodes, f32),
+            pltpu.VMEM(all_nodes, f32),
+            shape(1, width),
+        ),
+        [SMEM] + [VMEM] * 3,
+        (VMEM,) * 5,
         "ones_nodes",
         flops=nodes_flops,
-    )(raw, ones_rounded, low_hot, pair_hot)
+    )(block_count, raw, trade_node[None, :], ones_rounded)
 
     spread, sums = call(
         weights_kernel,

time: 46.1 us -> 46.1 us (level)
  waiting for transfers between devices: 10.4 us -> 9.78 us
  Pallas kernels: 15.6 us -> 16.2 us
    ppermute x16, waiting for transfers between devices: 10.4 us -> 9.78 us  [exchange(): return lax.ppermute(x, AXES, [(o, o ^ mask) for o in range(devices)])]
    pallas_call x2, Pallas kernels: 6.76 us -> 7.24 us  [the longest x1 5.51 us: local(): call(functools.partial(totals_kernel, factor_size=factor_size), (pltpu.VM...]
  transfers between devices with their start and end apart: 16 -> 16, of which waited for: 7 -> 6; matrix products, arithmetic and copies ran while one was open for 0% -> 0% of each run, Pallas kernels for 16% -> 18%
where the time goes in v6:
time: 46.1 us
  starting transfers between devices  19.2 us (42%)
  Pallas kernels  16.2 us (35%)
  waiting for transfers between devices  9.78 us (21%)
  between operations  0.94 us (2%)
    ppermute x16, starting transfers between devices, exchange(): return lax.ppermute(x, AXES, [(o, o ^ mask) for o in range(devices)])  19.2 us
    ppermute x16, waiting for transfers between devices, exchange(): return lax.ppermute(x, AXES, [(o, o ^ mask) for o in range(devices)])  9.78 us
    pallas_call x1, Pallas kernels, local(): call(functools.partial(totals_kernel, factor_size=factor_size), (pltpu.VM...  5.51 us
    pallas_call x1, Pallas kernels, local(): call(ones_kernel, (multiplied, rounded, shape(1, width)), [VMEM] * 3, (VM...  2.11 us
    pallas_call x1, Pallas kernels, local(): call(spread_kernel, (multiplied, rounded), [VMEM] * 2, (VMEM,) * 2, 'spre...  2.11 us
    pallas_call x1, Pallas kernels, local(): call(functools.partial(ones_nodes_kernel, spots=spots, factor_size=factor...  1.73 us
    pallas_call x1, Pallas kernels, local(): call(product_nodes_kernel, (rows, shape(GROUP, LANES), pltpu.VMEM(all_nod...  1.29 us
    pallas_call x1, Pallas kernels, local(): call(functools.partial(capital_kernel, trades_total=trades_total, parts=f...  1.2 us
  transfers between devices with their start and end apart: 16, of which 6 were waited for; matrix products, arithmetic and copies ran while one was open for 0% of the time, Pallas kernels for 18%

profile of v6, /device:TPU:0, one launch (start us, length us, event | category | flops | bytes accessed | tf_op | source)
XLA Modules:
  0.0 46.1 jit_solution(7176985391027409794)
XLA Ops:
  0.6 5.5 %totals.1 = (bf16[1600,4096]{1,0:T(8,128)(2,1)S(1)}, f32[1,1600]{1,0:T(1,128)S(1)}, bf16[128,1600]{1,0:T(8,128)(2,1)S(1)}, bf16[128,1600]{1,0:T(8,128)(2,1)S(1)}, f32[1,1600]{1,0:T(1,128)S(1)}) custom-call(s32[8]{0:T(128)} %count.3, f32[18]{0:T(128)} %weight.1, s32[50,128]{1,0:T(8,128)} %bitcast.17, bf16[1600,4096]{1,0:T(8,128)(2,1)} %bitcast.16), custom_call_target="tpu_custom_call" | custom-call | flops 10000000 | bytes 65536 | tf_op jit(solution)/shard_map/totals/pallas_call | solution.py:434
  6.1 3.0 %collective-permute-start = (f32[1,1600]{1,0:T(1,128)S(1)}, f32[1,1600]{1,0:T(1,128)S(1)}, u32[]{:S(2)}, u32[]{:S(2)}) collective-permute-start(f32[1,1600]{1,0:T(1,128)S(1)} %get-tuple-element.39.own), channel_id=1, source_target_pairs={{0,4},{1,5},{2,6},{3,7},{4,0},{5,1},{6,2},{7,3},{8,12},{9,13},{10,... | collective-permute-start | bytes 19208 | tf_op jit(solution)/shard_map/ppermute | solution.py:415
  9.2 0.0 copy-start
  9.2 0.0 copy-start.3
  9.2 2.1 %ones.1 = (f32[128,4096]{1,0:T(8,128)S(1)}, bf16[48,4096]{1,0:T(8,128)(2,1)S(1)}, f32[1,1600]{1,0:T(1,128)S(1)}) custom-call(f32[1,1600]{1,0:T(1,128)S(1)} %get-tuple-element.39.own, bf16[128,1600]{1,0:T(8,128)(2,1)S(1)} %get-tuple-element.40.ones_hot.refs_6_, bf16[1600,4096]{1,0:T(8,128)(2,1)S(1)} %get-tuple-element.41.held), custom_call_target="tpu_custom_call" | custom-call | flops 1677721600 | bytes 65536 | tf_op jit(solution)/shard_map/ones/pallas_call | solution.py:464
  11.3 0.0 collective-permute-done
  11.3 3.9 %collective-permute-start.3 = (f32[1,1600]{1,0:T(1,128)S(1)}, f32[1,1600]{1,0:T(1,128)S(1)}, u32[]{:S(2)}, u32[]{:S(2)}) collective-permute-start(f32[1,1600]{1,0:T(1,128)S(1)} %add.6.own), channel_id=1, source_target_pairs={{0,24},{1,25},{2,26},{3,27},{4,28},{5,29},{6,30},{7,31},{8,16},{9,... | collective-permute-start | bytes 19208 | tf_op jit(solution)/shard_map/ppermute | solution.py:415
  15.2 0.0 collective-permute-start.2
  15.2 0.6 %collective-permute-start.1 = (f32[1,1600]{1,0:T(1,128)S(1)}, f32[1,1600]{1,0:T(1,128)S(1)}, u32[]{:S(2)}, u32[]{:S(2)}) collective-permute-start(f32[1,1600]{1,0:T(1,128)S(1)} %add.6.own), channel_id=1, source_target_pairs={{0,8},{1,9},{2,10},{3,11},{4,12},{5,13},{6,14},{7,15},{8,0},{9,1},... | collective-permute-start | bytes 19208 | tf_op jit(solution)/shard_map/ppermute | solution.py:415
  15.9 0.0 copy-done
  15.9 0.0 copy-done.3
  15.9 1.7 %ones_nodes.1 = (bf16[256,4096]{1,0:T(8,128)(2,1)S(1)}, bf16[8,48,4096]{2,1,0:T(8,128)(2,1)S(1)}, f32[864,128]{1,0:T(8,128)S(1)}, f32[864,128]{1,0:T(8,128)S(1)}, f32[1,1600]{1,0:T(1,128)S(1)}) custom-call(s32[8]{0:T(128)S(1)} %copy-done, f32[1,1600]{1,0:T(1,128)S(1)} %add.6.own, s32[1,4096]{1,0:T(1,128)S(1)} %bitcast.15, ...), custom_call_target="tpu_custom_call" | custom-call | flops 1073741824 | bytes 65536 | tf_op jit(solution)/shard_map/ones_nodes/pallas_call | solution.py:482
  17.6 0.0 collective-permute-done.3.refs_3_
  17.6 2.1 %collective-permute-done.2.refs_2_ = f32[1,1600]{1,0:T(1,128)S(1)} collective-permute-done((f32[1,1600]{1,0:T(1,128)S(1)}, f32[1,1600]{1,0:T(1,128)S(1)}, u32[]{:S(2)}, u32[]{:S(2)}) %collective-permute-start.2) | collective-permute-done | bytes 6432 | tf_op jit(solution)/shard_map/ppermute | solution.py:415
  19.7 0.0 collective-permute-done.1.refs_1_
  19.8 0.4 weights.1
  20.2 0.1 collective-permute-start.6
  20.2 1.6 %collective-permute-start.5 = (f32[24,128]{1,0:T(8,128)S(1)}, f32[24,128]{1,0:T(8,128)S(1)}, u32[]{:S(2)}, u32[]{:S(2)}) collective-permute-start(f32[24,128]{1,0:T(8,128)S(1)} %get-tuple-element.47.refs_0_), channel_id=1, source_target_pairs={{0,2},{1,3},{2,0},{3,1},{4,6},{5,7},{6,4},{7,5},{8,10},{9,11},{10,... | collective-permute-start | bytes 36872 | tf_op jit(solution)/shard_map/ppermute | solution.py:415
  21.8 0.3 collective-permute-start.4
  22.1 2.1 %spread.1 = (f32[128,4096]{1,0:T(8,128)S(1)}, bf16[48,4096]{1,0:T(8,128)(2,1)S(1)}) custom-call(bf16[128,1600]{1,0:T(8,128)(2,1)S(1)} %get-tuple-element.48.spread, bf16[1600,4096]{1,0:T(8,128)(2,1)S(1)} %get-tuple-element.41.held), custom_call_target="tpu_custom_call" | custom-call | flops 1677721600 | bytes 65536 | tf_op jit(solution)/shard_map/spread/pallas_call | solution.py:507
  24.2 1.1 %weighted_nodes.1 = (f32[864,128]{1,0:T(8,128)S(1)}, f32[864,128]{1,0:T(8,128)S(1)}) custom-call(bf16[48,4096]{1,0:T(8,128)(2,1)S(1)} %get-tuple-element.53.rounded, bf16[256,4096]{1,0:T(8,128)(2,1)S(1)} %get-tuple-element.51.low_hot.refs_6_, ...), custom_call_target="tpu_custom_call", output_to_operand_aliasing={{0}: (3, {}), {1}: (4, {})} | custom-call | flops 1073741824 | bytes 65536 | tf_op jit(solution)/shard_map/weighted_nodes/pallas_call | solution.py:515
  25.3 0.0 collective-permute-done.6.refs_3_
  25.3 0.0 collective-permute-done.5.refs_2_
  25.3 0.0 collective-permute-done.4.refs_1_
  25.3 0.0 copy-start.1
  25.3 0.0 copy-start.2
  25.3 1.3 %product_nodes.1 = (f32[24,4096]{1,0:T(8,128)S(1)}, f32[24,128]{1,0:T(8,128)S(1)}, f32[864,128]{1,0:T(8,128)S(1)}, f32[864,128]{1,0:T(8,128)S(1)}) custom-call(f32[24,128]{1,0:T(8,128)S(1)} %get-tuple-element.47.refs_0_, f32[24,128]{1,0:T(8,128)S(1)} %collective-permute-done.4.refs_1_, ...), custom_call_target="tpu_custom_call", output_to_operand_aliasing={{2}: (8, {}), {3}: (9, {})} | custom-call | flops 1073741824 | bytes 65536 | tf_op jit(solution)/shard_map/product_nodes/pallas_call | solution.py:525
  26.6 0.3 collective-permute-start.7
  26.9 0.0 copy-done.1
  26.9 0.0 copy-done.2
  26.9 1.2 %capital.1 = (f32[2,24,128]{2,1,0:T(8,128)S(1)}, f32[2,24,128]{2,1,0:T(8,128)S(1)}, f32[3,54,128]{2,1,0:T(8,128)S(1)}, f32[8,128]{1,0:T(8,128)S(1)}) custom-call(s32[8]{0:T(128)S(1)} %copy-done, f32[18]{0:T(128)S(1)} %copy-done.1, f32[18]{0:T(128)S(1)} %copy-done.2, f32[24,128]{1,0:T(8,128)S(1)} %get-tuple-element.58.total, ...), custom_call_target="tpu_custom_call" | custom-call | flops 10000000 | bytes 65536 | tf_op jit(solution)/shard_map/capital/pallas_call | solution.py:538
  28.1 0.3 collective-permute-done.7.more
  28.5 2.5 %collective-permute-start.10 = (f32[216,128]{1,0:T(8,128)S(1)}, f32[216,128]{1,0:T(8,128)S(1)}, u32[]{:S(2)}, u32[]{:S(2)}) collective-permute-start(f32[216,128]{1,0:T(8,128)S(1)} %get-tuple-element.68), channel_id=1, source_target_pairs={{0,6},{1,7},{2,4},{3,5},{4,2},{5,3},{6,0},{7,1},{8,14},{9,15},{10,... | collective-permute-start | bytes 331784 | tf_op jit(solution)/shard_map/ppermute | solution.py:415
  31.0 0.5 %collective-permute-start.11 = (f32[216,128]{1,0:T(8,128)S(1)}, f32[216,128]{1,0:T(8,128)S(1)}, u32[]{:S(2)}, u32[]{:S(2)}) collective-permute-start(f32[216,128]{1,0:T(8,128)S(1)} %get-tuple-element.69), channel_id=1, source_target_pairs={{0,2},{1,3},{2,0},{3,1},{4,6},{5,7},{6,4},{7,5},{8,10},{9,11},{10,... | collective-permute-start | bytes 331784 | tf_op jit(solution)/shard_map/ppermute | solution.py:415
  31.6 0.5 %collective-permute-start.12 = (f32[216,128]{1,0:T(8,128)S(1)}, f32[216,128]{1,0:T(8,128)S(1)}, u32[]{:S(2)}, u32[]{:S(2)}) collective-permute-start(f32[216,128]{1,0:T(8,128)S(1)} %get-tuple-element.70), channel_id=1, source_target_pairs={{0,4},{1,5},{2,6},{3,7},{4,0},{5,1},{6,2},{7,3},{8,12},{9,13},{10,... | collective-permute-start | bytes 331784 | tf_op jit(solution)/shard_map/ppermute | solution.py:415
  32.1 0.0 collective-permute-start.8
  32.1 1.2 %collective-permute-done.8 = f32[2,24,128]{2,1,0:T(8,128)S(1)} collective-permute-done((f32[2,24,128]{2,1,0:T(8,128)S(1)}, f32[2,24,128]{2,1,0:T(8,128)S(1)}, u32[]{:S(2)}, u32[]{:S(2)}) %collective-permute-start.8) | collective-permute-done | bytes 24608 | tf_op jit(solution)/shard_map/ppermute | solution.py:415
  33.3 2.1 %collective-permute-done.10.refs_1_ = f32[216,128]{1,0:T(8,128)S(1)} collective-permute-done((f32[216,128]{1,0:T(8,128)S(1)}, f32[216,128]{1,0:T(8,128)S(1)}, u32[]{:S(2)}, u32[]{:S(2)}) %collective-permute-start.10) | collective-permute-done | bytes 110624 | tf_op jit(solution)/shard_map/ppermute | solution.py:415
  35.4 1.7 %collective-permute-done.11.refs_2_ = f32[216,128]{1,0:T(8,128)S(1)} collective-permute-done((f32[216,128]{1,0:T(8,128)S(1)}, f32[216,128]{1,0:T(8,128)S(1)}, u32[]{:S(2)}, u32[]{:S(2)}) %collective-permute-start.11) | collective-permute-done | bytes 110624 | tf_op jit(solution)/shard_map/ppermute | solution.py:415
  37.1 0.0 collective-permute-done.12.refs_3_
  37.1 1.7 %collective-permute-start.13 = (f32[1,54,128]{2,1,0:T(8,128)S(1)}, f32[1,54,128]{2,1,0:T(8,128)S(1)}, u32[]{:S(2)}, u32[]{:S(2)}) collective-permute-start(f32[1,54,128]{2,1,0:T(8,128)S(1)} %get-tuple-element.72), channel_id=1, source_target_pairs={{0,24},{1,25},{2,26},{3,27},{4,28},{5,29},{6,30},{7,31},{8,16},{9,... | collective-permute-start | bytes 82952 | tf_op jit(solution)/shard_map/ppermute | solution.py:415
  38.8 1.0 %collective-permute-start.14 = (f32[1,54,128]{2,1,0:T(8,128)S(1)}, f32[1,54,128]{2,1,0:T(8,128)S(1)}, u32[]{:S(2)}, u32[]{:S(2)}) collective-permute-start(f32[1,54,128]{2,1,0:T(8,128)S(1)} %get-tuple-element.73), channel_id=1, source_target_pairs={{0,8},{1,9},{2,10},{3,11},{4,12},{5,13},{6,14},{7,15},{8,0},{9,1},... | collective-permute-start | bytes 82952 | tf_op jit(solution)/shard_map/ppermute | solution.py:415
  39.8 1.8 %collective-permute-start.15 = (f32[1,54,128]{2,1,0:T(8,128)S(1)}, f32[1,54,128]{2,1,0:T(8,128)S(1)}, u32[]{:S(2)}, u32[]{:S(2)}) collective-permute-start(f32[1,54,128]{2,1,0:T(8,128)S(1)} %get-tuple-element.74), channel_id=1, source_target_pairs={{0,16},{1,17},{2,18},{3,19},{4,20},{5,21},{6,22},{7,23},{8,24},{9,... | collective-permute-start | bytes 82952 | tf_op jit(solution)/shard_map/ppermute | solution.py:415
  41.6 1.4 %collective-permute-start.9 = (f32[1,24,128]{2,1,0:T(8,128)S(1)}, f32[1,24,128]{2,1,0:T(8,128)S(1)}, u32[]{:S(2)}, u32[]{:S(2)}) collective-permute-start(f32[1,24,128]{2,1,0:T(8,128)S(1)} %get-tuple-element.75), channel_id=1, source_target_pairs={{0,2},{1,3},{2,0},{3,1},{4,6},{5,7},{6,4},{7,5},{8,10},{9,11},{10,... | collective-permute-start | bytes 36872 | tf_op jit(solution)/shard_map/ppermute | solution.py:415
  43.0 2.3 %collective-permute-done.9 = f32[1,24,128]{2,1,0:T(8,128)S(1)} collective-permute-done((f32[1,24,128]{2,1,0:T(8,128)S(1)}, f32[1,24,128]{2,1,0:T(8,128)S(1)}, u32[]{:S(2)}, u32[]{:S(2)}) %collective-permute-start.9) | collective-permute-done | bytes 12320 | tf_op jit(solution)/shard_map/ppermute | solution.py:415
  45.3 0.0 collective-permute-done.13
  45.3 0.0 collective-permute-done.14
  45.3 0.0 collective-permute-done.15
  45.3 0.7 %finish.1 = (f32[3]{0:T(128)}, f32[3,1024]{1,0:T(4,128)}, f32[3,18,128]{2,1,0:T(8,128)}) custom-call(f32[3,54,128]{2,1,0:T(8,128)S(1)} %get-tuple-element.60.mix, f32[8,128]{1,0:T(8,128)S(1)} %get-tuple-element.61.capital, f32[24,128]{1,0:T(8,128)S(1)} %get-tuple-element.76.trade_keep, f32[24,128]{1,0:T(8,128)S(1)} %bitcast.14, f32[54,128]{1,0:T(8,128)S(1)} %bitcast.10, ...), custom_call_target="tpu_custom_call" | custom-call | flops 1000000 | bytes 65536 | tf_op jit(solution)/shard_map/finish/pallas_call | solution.py:596
  (5 shorter events, 0.1 us)
Async XLA Ops:
  6.1 5.2 %collective-permute-start = (f32[1,1600]{1,0:T(1,128)S(1)}, f32[1,1600]{1,0:T(1,128)S(1)}, u32[]{:S(2)}, u32[]{:S(2)}) collective-permute-start(f32[1,1600]{1,0:T(1,128)S(1)} %get-tuple-element.39.own), channel_id=1, source_target_pairs={{0,4},{1,5},{2,6},{3,7},{4,0},{5,1},{6,2},{7,3},{8,12},{9,13},{10,... | collective-permute-start | bytes 19208 | tf_op jit(solution)/shard_map/ppermute | solution.py:415
  9.2 6.7 %copy-start = (s32[8]{0:T(128)S(1)}, s32[8]{0:T(128)}, u32[]{:S(2)}) copy-start(s32[8]{0:T(128)} %count.3) | copy-start | bytes 100
  9.2 6.7 %copy-start.3 = (s32[4096]{0:T(1024)S(1)}, s32[4096]{0:T(1024)}, u32[]{:S(2)}) copy-start(s32[4096]{0:T(1024)} %param.8) | copy-start | bytes 49156
  11.3 6.3 %collective-permute-start.3 = (f32[1,1600]{1,0:T(1,128)S(1)}, f32[1,1600]{1,0:T(1,128)S(1)}, u32[]{:S(2)}, u32[]{:S(2)}) collective-permute-start(f32[1,1600]{1,0:T(1,128)S(1)} %add.6.own), channel_id=1, source_target_pairs={{0,24},{1,25},{2,26},{3,27},{4,28},{5,29},{6,30},{7,31},{8,16},{9,... | collective-permute-start | bytes 19208 | tf_op jit(solution)/shard_map/ppermute | solution.py:415
  15.2 4.5 %collective-permute-start.2 = (f32[1,1600]{1,0:T(1,128)S(1)}, f32[1,1600]{1,0:T(1,128)S(1)}, u32[]{:S(2)}, u32[]{:S(2)}) collective-permute-start(f32[1,1600]{1,0:T(1,128)S(1)} %add.6.own), channel_id=1, source_target_pairs={{0,16},{1,17},{2,18},{3,19},{4,20},{5,21},{6,22},{7,23},{8,24},{9,... | collective-permute-start | bytes 19208 | tf_op jit(solution)/shard_map/ppermute | solution.py:415
  15.2 4.5 %collective-permute-start.1 = (f32[1,1600]{1,0:T(1,128)S(1)}, f32[1,1600]{1,0:T(1,128)S(1)}, u32[]{:S(2)}, u32[]{:S(2)}) collective-permute-start(f32[1,1600]{1,0:T(1,128)S(1)} %add.6.own), channel_id=1, source_target_pairs={{0,8},{1,9},{2,10},{3,11},{4,12},{5,13},{6,14},{7,15},{8,0},{9,1},... | collective-permute-start | bytes 19208 | tf_op jit(solution)/shard_map/ppermute | solution.py:415
  20.2 5.1 %collective-permute-start.6 = (f32[24,128]{1,0:T(8,128)S(1)}, f32[24,128]{1,0:T(8,128)S(1)}, u32[]{:S(2)}, u32[]{:S(2)}) collective-permute-start(f32[24,128]{1,0:T(8,128)S(1)} %get-tuple-element.47.refs_0_), channel_id=1, source_target_pairs={{0,3},{1,2},{2,1},{3,0},{4,7},{5,6},{6,5},{7,4},{8,11},{9,10},{10,... | collective-permute-start | bytes 36872 | tf_op jit(solution)/shard_map/ppermute | solution.py:415
  20.2 5.0 %collective-permute-start.5 = (f32[24,128]{1,0:T(8,128)S(1)}, f32[24,128]{1,0:T(8,128)S(1)}, u32[]{:S(2)}, u32[]{:S(2)}) collective-permute-start(f32[24,128]{1,0:T(8,128)S(1)} %get-tuple-element.47.refs_0_), channel_id=1, source_target_pairs={{0,2},{1,3},{2,0},{3,1},{4,6},{5,7},{6,4},{7,5},{8,10},{9,11},{10,... | collective-permute-start | bytes 36872 | tf_op jit(solution)/shard_map/ppermute | solution.py:415
  21.8 3.5 %collective-permute-start.4 = (f32[24,128]{1,0:T(8,128)S(1)}, f32[24,128]{1,0:T(8,128)S(1)}, u32[]{:S(2)}, u32[]{:S(2)}) collective-permute-start(f32[24,128]{1,0:T(8,128)S(1)} %get-tuple-element.47.refs_0_), channel_id=1, source_target_pairs={{0,1},{1,0},{2,3},{3,2},{4,5},{5,4},{6,7},{7,6},{8,9},{9,8},{10,11... | collective-permute-start | bytes 36872 | tf_op jit(solution)/shard_map/ppermute | solution.py:415
  25.3 1.6 %copy-start.1 = (f32[18]{0:T(128)S(1)}, f32[18]{0:T(128)}, u32[]{:S(2)}) copy-start(f32[18]{0:T(128)} %weight.1) | copy-start | bytes 220
  25.3 1.6 %copy-start.2 = (f32[18]{0:T(128)S(1)}, f32[18]{0:T(128)}, u32[]{:S(2)}) copy-start(f32[18]{0:T(128)} %load.1) | copy-start | bytes 220
  26.6 1.9 %collective-permute-start.7 = (f32[864,128]{1,0:T(8,128)S(1)}, f32[864,128]{1,0:T(8,128)S(1)}, u32[]{:S(2)}, u32[]{:S(2)}) collective-permute-start(f32[864,128]{1,0:T(8,128)S(1)} %get-tuple-element.65), channel_id=1, source_target_pairs={{0,1},{1,0},{2,3},{3,2},{4,5},{5,4},{6,7},{7,6},{8,9},{9,8},{10,11... | collective-permute-start | bytes 1327112 | tf_op jit(solution)/shard_map/ppermute | solution.py:415
  28.5 6.9 %collective-permute-start.10 = (f32[216,128]{1,0:T(8,128)S(1)}, f32[216,128]{1,0:T(8,128)S(1)}, u32[]{:S(2)}, u32[]{:S(2)}) collective-permute-start(f32[216,128]{1,0:T(8,128)S(1)} %get-tuple-element.68), channel_id=1, source_target_pairs={{0,6},{1,7},{2,4},{3,5},{4,2},{5,3},{6,0},{7,1},{8,14},{9,15},{10,... | collective-permute-start | bytes 331784 | tf_op jit(solution)/shard_map/ppermute | solution.py:415
  31.0 6.1 %collective-permute-start.11 = (f32[216,128]{1,0:T(8,128)S(1)}, f32[216,128]{1,0:T(8,128)S(1)}, u32[]{:S(2)}, u32[]{:S(2)}) collective-permute-start(f32[216,128]{1,0:T(8,128)S(1)} %get-tuple-element.69), channel_id=1, source_target_pairs={{0,2},{1,3},{2,0},{3,1},{4,6},{5,7},{6,4},{7,5},{8,10},{9,11},{10,... | collective-permute-start | bytes 331784 | tf_op jit(solution)/shard_map/ppermute | solution.py:415
  31.6 5.5 %collective-permute-start.12 = (f32[216,128]{1,0:T(8,128)S(1)}, f32[216,128]{1,0:T(8,128)S(1)}, u32[]{:S(2)}, u32[]{:S(2)}) collective-permute-start(f32[216,128]{1,0:T(8,128)S(1)} %get-tuple-element.70), channel_id=1, source_target_pairs={{0,4},{1,5},{2,6},{3,7},{4,0},{5,1},{6,2},{7,3},{8,12},{9,13},{10,... | collective-permute-start | bytes 331784 | tf_op jit(solution)/shard_map/ppermute | solution.py:415
  32.1 1.2 %collective-permute-start.8 = (f32[2,24,128]{2,1,0:T(8,128)S(1)}, f32[2,24,128]{2,1,0:T(8,128)S(1)}, u32[]{:S(2)}, u32[]{:S(2)}) collective-permute-start(f32[2,24,128]{2,1,0:T(8,128)S(1)} %get-tuple-element.66), channel_id=1, source_target_pairs={{0,1},{1,0},{2,3},{3,2},{4,5},{5,4},{6,7},{7,6},{8,9},{9,8},{10,11... | collective-permute-start | bytes 73736 | tf_op jit(solution)/shard_map/ppermute | solution.py:415
  37.1 8.2 %collective-permute-start.13 = (f32[1,54,128]{2,1,0:T(8,128)S(1)}, f32[1,54,128]{2,1,0:T(8,128)S(1)}, u32[]{:S(2)}, u32[]{:S(2)}) collective-permute-start(f32[1,54,128]{2,1,0:T(8,128)S(1)} %get-tuple-element.72), channel_id=1, source_target_pairs={{0,24},{1,25},{2,26},{3,27},{4,28},{5,29},{6,30},{7,31},{8,16},{9,... | collective-permute-start | bytes 82952 | tf_op jit(solution)/shard_map/ppermute | solution.py:415
  38.8 6.5 %collective-permute-start.14 = (f32[1,54,128]{2,1,0:T(8,128)S(1)}, f32[1,54,128]{2,1,0:T(8,128)S(1)}, u32[]{:S(2)}, u32[]{:S(2)}) collective-permute-start(f32[1,54,128]{2,1,0:T(8,128)S(1)} %get-tuple-element.73), channel_id=1, source_target_pairs={{0,8},{1,9},{2,10},{3,11},{4,12},{5,13},{6,14},{7,15},{8,0},{9,1},... | collective-permute-start | bytes 82952 | tf_op jit(solution)/shard_map/ppermute | solution.py:415
  39.8 5.5 %collective-permute-start.15 = (f32[1,54,128]{2,1,0:T(8,128)S(1)}, f32[1,54,128]{2,1,0:T(8,128)S(1)}, u32[]{:S(2)}, u32[]{:S(2)}) collective-permute-start(f32[1,54,128]{2,1,0:T(8,128)S(1)} %get-tuple-element.74), channel_id=1, source_target_pairs={{0,16},{1,17},{2,18},{3,19},{4,20},{5,21},{6,22},{7,23},{8,24},{9,... | collective-permute-start | bytes 82952 | tf_op jit(solution)/shard_map/ppermute | solution.py:415
  41.6 3.7 %collective-permute-start.9 = (f32[1,24,128]{2,1,0:T(8,128)S(1)}, f32[1,24,128]{2,1,0:T(8,128)S(1)}, u32[]{:S(2)}, u32[]{:S(2)}) collective-permute-start(f32[1,24,128]{2,1,0:T(8,128)S(1)} %get-tuple-element.75), channel_id=1, source_target_pairs={{0,2},{1,3},{2,0},{3,1},{4,6},{5,7},{6,4},{7,5},{8,10},{9,11},{10,... | collective-permute-start | bytes 36872 | tf_op jit(solution)/shard_map/ppermute | solution.py:415
